TPU v7x, 32 devices: a whole 2x2x4 slice. The times are simulated.
32 devices in a mesh: groups: 2 (over x), inp: 16 (over z, y, core).
Axes of the slice: x: 2, y: 2, z: 4, core: 2. Of those that a mesh axis runs over, the one named last changes fastest.
Arguments:
- tokens: bfloat16 [512, 6144], P(('groups', 'inp')), parts along dimension 0, may hold values from -6 to 6
- dropout_masks: int32 [8, 512, 48], P(None, 'groups'), parts along dimension 1, may hold values 0 or 1
- input_gain: float32 [6144], replicated, may hold values from 0.5 to 1.5
- w_qkv: bfloat16 [128, 3, 48, 6144], P('inp'), may hold values from -0.078125 to 0.078125
- w_up: bfloat16 [24576, 6144], P('inp'), may hold values from -0.078125 to 0.078125
- query_gain: float32 [128], replicated, may hold values from 0.1 to 1.9
- key_gain: float32 [128], replicated, may hold values from 0.1 to 1.9
- w_proj: bfloat16 [128, 48, 6144], P('inp'), may hold values from -0.109375 to 0.109375
- w_down: bfloat16 [24576, 6144], P('inp'), may hold values from -0.0546875 to 0.0546875
- final_gain: float32 [6144], replicated, may hold values from 0.5 to 1.5
- w_head: bfloat16 [6144, 1000], P('inp'), may hold values from -0.625 to 0.625
Outputs:
- embedding: float32 [2, 8, 6144], P('groups', None, 'inp'), parts along dimension 0
- bald: float32 [2], P('groups'), parts along dimension 0
There are 2 independent parts, one for each index of `groups`. A program takes and returns all parts, laid end to end along the dimension named above; an argument that names none is the same for every part. Nothing has to cross between parts.
All inputs are finite; a program needn't handle non-finite values.
Results may differ from a plain program's by a relative error of at most 0.0093.
Values may be sent and summed in bfloat16 or wider, within the bound.
No kernel may reach another device: no remote copies, remote signals or barrier semaphores. Data moves between devices by JAX's collectives and lax.ppermute only.
A program may use at most 256 MiB of HBM per device.

v0:
```python
import functools
import math

import jax
import jax.numpy as jnp
from jax import lax
from jax.experimental import pallas as pl
from jax.experimental.pallas import tpu as pltpu
from jax.sharding import PartitionSpec as P

PATCHES = 256


soft_cap = 20.0
PIPELINED_PARTS = 16
UNITS = 256
F32 = jnp.float32
BF16 = jnp.bfloat16
MIB = 1024 * 1024


def norm_last(values, gain):
    average = jnp.mean(values, axis=-1, keepdims=True)
    centered = values - average
    spread_sq = jnp.mean(centered * centered, axis=-1, keepdims=True)
    return centered * lax.rsqrt(spread_sq + 1e-06) * gain


def norm_second(values, gain):
    average = jnp.mean(values, axis=1, keepdims=True)
    centered = values - average
    spread_sq = jnp.mean(centered * centered, axis=1, keepdims=True)
    return centered * lax.rsqrt(spread_sq + 1e-06) * gain[None, :, None, None]


def bald_score(logits):
    exp_logits = jnp.exp(logits)
    totals = jnp.sum(exp_logits, axis=-1, keepdims=True)
    sample_probs = exp_logits / totals
    entropy = jnp.log(totals[..., 0]) - jnp.sum(sample_probs * logits, axis=-1)
    mean_probs = jnp.mean(sample_probs, axis=1)
    joint = -jnp.sum(mean_probs * jnp.log(mean_probs), axis=-1)
    return joint - jnp.mean(entropy, axis=1)


def permuted(array, bits):
    count = lax.axis_size("inp")
    return lax.ppermute(array, "inp", [(i, i ^ bits) for i in range(count)])


def own_norm_kernel(x_ref, gain_ref, first_ref, second_ref):
    y = norm_last(x_ref[...].astype(F32), gain_ref[...]).astype(BF16)
    cut = first_ref.shape[1]
    first_ref[...] = y[:, :cut]
    second_ref[...] = y[:, cut:]


def own_norm(tokens, gain):
    rows, width = tokens.shape
    cut = width // 3 * 2
    return pl.pallas_call(
        own_norm_kernel,
        out_shape=(
            jax.ShapeDtypeStruct((rows, cut), BF16),
            jax.ShapeDtypeStruct((rows, width - cut), BF16),
        ),
        compiler_params=pltpu.CompilerParams(vmem_limit_bytes=8 * MIB),
        name="own_norm",
    )(tokens, gain.reshape(1, width))


def gathered_pieces(first, second, beside):
    along_z = jnp.stack([first] + [permuted(first, 4 * k) for k in range(1, 4)])
    pair = jnp.stack([second, permuted(second, 2)])
    along_z, pair, beside = lax.optimization_barrier((along_z, pair, beside))
    across_y = permuted(along_z, 2)
    moved = [permuted(pair, 4 * k) for k in range(1, 4)]
    across_y, *moved = lax.optimization_barrier((across_y, *moved))
    pieces = [
        (0, [4 * k for k in range(4)], along_z),
        (0, [4 * k + 2 for k in range(4)], across_y),
    ]
    for k, array in enumerate([pair, *moved]):
        pieces.append((first.shape[1], [4 * k, 4 * k + 2], array))
    pieces = pieces + [
        (side, [b ^ 1 for b in bits], permuted(array, 1)) for side, bits, array in pieces
    ]
    return pieces, beside


def place_kernel(layout, me_ref, *refs):
    sources, out_ref = refs[:-1], refs[-1]
    me = me_ref[0]
    for (side, bits), source in zip(layout, sources, strict=True):
        _, rows, columns = source.shape
        for at, bit in enumerate(bits):
            start = pl.multiple_of((me ^ bit) * rows, rows)
            out_ref[pl.ds(start, rows), side : side + columns] = source[at]


def placed(pieces, me):
    rows = pieces[0][2].shape[1]
    total = rows * sum(len(bits) for side, bits, _ in pieces if side == 0)
    width = sum(array.size for _, _, array in pieces) // total
    layout = [(side, bits) for side, bits, _ in pieces]
    return pl.pallas_call(
        functools.partial(place_kernel, layout),
        out_shape=jax.ShapeDtypeStruct((total, width), BF16),
        in_specs=[pl.BlockSpec(memory_space=pltpu.SMEM)]
        + [pl.BlockSpec(memory_space=pltpu.VMEM)] * len(pieces),
        out_specs=pl.BlockSpec(memory_space=pltpu.VMEM),
        compiler_params=pltpu.CompilerParams(vmem_limit_bytes=16 * MIB),
        name="place_rows",
    )(me.reshape(1), *[array for _, _, array in pieces])


ACROSS = (((1,), (1,)), ((), ()))
TILE = 16
BLOCK = 128


def choosers(dropout_masks):
    samples, rows, blocks = dropout_masks.shape
    tiles = rows // TILE
    kept = dropout_masks.astype(BF16).reshape(samples, tiles, TILE, blocks)
    kept = jnp.transpose(kept, (1, 0, 2, 3)).reshape(tiles, samples * TILE, blocks)
    column = jnp.arange(blocks * TILE)
    spread = (column[None] // TILE == jnp.arange(blocks)[:, None]).astype(BF16)
    own = jnp.arange(samples * TILE)[:, None] % TILE == column[None] % TILE
    wide = jnp.einsum("trb,bc->trc", kept, spread, preferred_element_type=F32)
    return jnp.where(own[None], 2.0 * wide, 0.0).astype(BF16)


def block_products(norm_ref, weight, products, first):
    for j in range(weight.shape[1] // BLOCK):
        at = slice(j * BLOCK, (j + 1) * BLOCK)
        products[first + j] = lax.dot_general(
            norm_ref[:, at], weight[:, at], ACROSS, preferred_element_type=F32
        ).astype(BF16)


def summed(choose_ref, products, tile):
    blocks, _, columns = products.shape
    part = products[:, tile * TILE : (tile + 1) * TILE, :].reshape(blocks * TILE, columns)
    return jnp.dot(choose_ref[tile], part, preferred_element_type=F32)


def query_key_kernel(norm_ref, choose_ref, w_ref, out_ref, products, sums, turned):
    step = pl.program_id(0)
    rows, depth = norm_ref.shape
    comps, kinds, heads, _ = w_ref.shape
    columns = comps * kinds * heads
    block_products(
        norm_ref, w_ref[...].reshape(columns, depth), products, step * (depth // BLOCK)
    )

    @pl.when(step == pl.num_programs(0) - 1)
    def _():
        samples = sums.shape[0]
        for tile in range(rows // TILE):
            sums[:, tile * TILE : (tile + 1) * TILE, :] = summed(
                choose_ref, products, tile
            ).reshape(samples, TILE, columns)
        for m in range(samples):
            for part in range(rows // 128):
                at = slice(part * 128, (part + 1) * 128)
                turned[m * (rows // 128) + part] = sums[m, at, :].T
            for part in range(rows // 128):
                at = slice(part * 128, (part + 1) * 128)
                held = turned.at[m * (rows // 128) + part]
                for h in range(heads):
                    both = [
                        held[pl.ds(t * heads + h, comps, stride=kinds * heads), :]
                        for t in range(kinds)
                    ]
                    out_ref[h, m, :, at] = jnp.concatenate(both, axis=0).astype(BF16)


def query_key(norm, choose, w_qkv, chunk, heads):
    rows, width = norm.shape
    samples = choose.shape[1] // TILE
    comps = w_qkv.shape[0]
    depth = width // 2
    columns = 2 * comps * heads
    shape = (heads, samples, 2 * comps, rows)
    return pl.pallas_call(
        query_key_kernel,
        grid=(width // depth,),
        out_shape=jax.ShapeDtypeStruct(shape, BF16),
        in_specs=[
            pl.BlockSpec((rows, depth), lambda k: (0, k)),
            pl.BlockSpec(choose.shape, lambda k: (0, 0, 0)),
            pl.BlockSpec((comps, 2, heads, depth), lambda k: (0, 0, chunk, k)),
        ],
        out_specs=pl.BlockSpec(shape, lambda k: (0, 0, 0, 0)),
        scratch_shapes=[
            pltpu.VMEM((width // BLOCK, rows, columns), BF16),
            pltpu.VMEM((samples, rows, columns), F32),
            pltpu.VMEM((samples * rows // 128, columns, 128), F32),
        ],
        compiler_params=pltpu.CompilerParams(vmem_limit_bytes=54 * MIB),
        cost_estimate=pl.CostEstimate(
            flops=8 * rows * width * columns,
            bytes_accessed=2 * (norm.size + choose.size + columns * width),
            transcendentals=0,
        ),
        name="query_key",
    )(norm, choose, w_qkv)


def value_kernel(norm_ref, choose_ref, w_ref, out_ref, products):
    step = pl.program_id(0)
    rows, depth = norm_ref.shape
    comps, _, heads, _ = w_ref.shape
    block_products(
        norm_ref, w_ref[:, 0].reshape(comps * heads, depth), products, step * (depth // BLOCK)
    )

    @pl.when(step == pl.num_programs(0) - 1)
    def _():
        samples = out_ref.shape[0]
        for tile in range(rows // TILE):
            out_ref[:, tile * TILE : (tile + 1) * TILE, :] = (
                summed(choose_ref, products, tile)
                .reshape(samples, TILE, comps * heads)
                .astype(BF16)
            )


def values_of(norm, choose, w_qkv):
    rows, width = norm.shape
    samples = choose.shape[1] // TILE
    comps, _, heads, _ = w_qkv.shape
    depth = width // 2
    columns = comps * heads
    return pl.pallas_call(
        value_kernel,
        grid=(width // depth,),
        out_shape=jax.ShapeDtypeStruct((samples, rows, columns), BF16),
        in_specs=[
            pl.BlockSpec((rows, depth), lambda k: (0, k)),
            pl.BlockSpec(choose.shape, lambda k: (0, 0, 0)),
            pl.BlockSpec((comps, 1, heads, depth), lambda k: (0, 2, 0, k)),
        ],
        out_specs=pl.BlockSpec((samples, rows, columns), lambda k: (0, 0, 0)),
        scratch_shapes=[pltpu.VMEM((width // BLOCK, rows, columns), BF16)],
        compiler_params=pltpu.CompilerParams(vmem_limit_bytes=54 * MIB),
        cost_estimate=pl.CostEstimate(
            flops=8 * rows * width * columns,
            bytes_accessed=2 * (norm.size + choose.size + columns * width),
            transcendentals=0,
        ),
        name="value_rows",
    )(norm, choose, w_qkv)


def erf(x):
    x = jnp.clip(x, -4.0, 4.0)
    s = x * x
    top = s * -2.72614225801306e-10 + 2.77068142495902e-08
    for c in (
        -2.10102402082508e-06,
        -5.69250639462346e-05,
        -7.34990630326855e-04,
        -2.95459980854025e-03,
        -1.60960333262415e-02,
    ):
        top = top * s + c
    low = s * -1.45660718464996e-05 + -2.13374055278905e-04
    for c in (-1.68282697438203e-03, -7.37332916720468e-03, -1.42647390514189e-02):
        low = low * s + c
    return x * top / low


def hidden_kernel(norm_ref, choose_ref, up_ref, out_ref, products):
    step = pl.program_id(1)
    rows, depth = norm_ref.shape
    samples, units = out_ref.shape
    block_products(norm_ref, up_ref, products, step * (depth // BLOCK))

    @pl.when(step == pl.num_programs(1) - 1)
    def _():
        total = jnp.zeros((samples, units), F32)
        for tile in range(rows // TILE):
            v = summed(choose_ref, products, tile)
            active = (0.5 * v) * (1.0 + erf(v * math.sqrt(0.5)))
            total = total + jnp.sum(active.reshape(samples, TILE, units), axis=1)
        out_ref[...] = total * (1.0 / rows)


def hidden_part(norm, choose, w_up, first, tiles):
    rows, width = norm.shape
    samples = choose.shape[1] // TILE
    depth = width // 2
    return pl.pallas_call(
        hidden_kernel,
        grid=(tiles, width // depth),
        out_shape=jax.ShapeDtypeStruct((samples, tiles * UNITS), F32),
        in_specs=[
            pl.BlockSpec((rows, depth), lambda i, k: (0, k)),
            pl.BlockSpec(choose.shape, lambda i, k: (0, 0, 0)),
            pl.BlockSpec((UNITS, depth), lambda i, k: (first + i, k)),
        ],
        out_specs=pl.BlockSpec((samples, UNITS), lambda i, k: (0, i)),
        scratch_shapes=[pltpu.VMEM((width // BLOCK, rows, UNITS), BF16)],
        compiler_params=pltpu.CompilerParams(vmem_limit_bytes=54 * MIB),
        cost_estimate=pl.CostEstimate(
            flops=8 * rows * width * UNITS * tiles,
            bytes_accessed=2 * (norm.size + choose.size + UNITS * tiles * width),
            transcendentals=samples * rows * UNITS * tiles,
        ),
        name="hidden_part",
    )(norm, choose, w_up)


def down_kernel(pooled_ref, down_ref, out_ref):
    samples = pooled_ref.shape[0]
    mean = pooled_ref[...]
    mean = jnp.concatenate([mean, jnp.zeros_like(mean)], axis=0).astype(BF16)
    part = jnp.dot(mean, down_ref[...], preferred_element_type=F32)[:samples]

    @pl.when(pl.program_id(0) == 0)
    def _():
        out_ref[...] = part

    @pl.when(pl.program_id(0) > 0)
    def _():
        out_ref[...] += part


def down_part(pooled, w_down):
    samples, units = pooled.shape
    width = w_down.shape[1]
    return pl.pallas_call(
        down_kernel,
        grid=(units // UNITS,),
        out_shape=jax.ShapeDtypeStruct((samples, width), F32),
        in_specs=[
            pl.BlockSpec((samples, UNITS), lambda i: (0, i)),
            pl.BlockSpec((UNITS, width), lambda i: (i, 0)),
        ],
        out_specs=pl.BlockSpec((samples, width), lambda i: (0, 0)),
        compiler_params=pltpu.CompilerParams(vmem_limit_bytes=54 * MIB),
        cost_estimate=pl.CostEstimate(
            flops=32 * units * width, bytes_accessed=2 * units * width, transcendentals=0
        ),
        name="down_part",
    )(pooled, w_down)


def attention_kernel(items, x_ref, query_gain_ref, key_gain_ref, out_ref):
    parts, _, both, rows = x_ref.shape
    comps = both // 2
    head_dim = parts * comps

    def normed(values, gain_ref):
        values = values.reshape(head_dim, rows)
        average = jnp.mean(values, axis=0, keepdims=True)
        centered = values - average
        spread_sq = jnp.mean(centered * centered, axis=0, keepdims=True)
        return (centered * lax.rsqrt(spread_sq + 1e-06) * gain_ref[...]).astype(BF16)

    for j in range(items):
        x = x_ref[:, j].astype(F32)
        query = normed(x[:, :comps], query_gain_ref)
        key = normed(x[:, comps:], key_gain_ref)
        scores = lax.dot_general(
            query, key, (((0,), (0,)), ((), ())), preferred_element_type=F32
        )
        e = jnp.exp2(scores * (math.log2(math.e) / math.sqrt(head_dim)))
        weights = (e * (1.0 / jnp.sum(e, axis=1, keepdims=True))).astype(BF16)
        out_ref[j : j + 1, :] = jnp.sum(weights.astype(F32), axis=0, keepdims=True) * (1.0 / rows)


def key_weights(exchanged, query_gain, key_gain):
    parts, items, both, rows = exchanged.shape
    head_dim = parts * both // 2
    return pl.pallas_call(
        functools.partial(attention_kernel, items),
        out_shape=jax.ShapeDtypeStruct((items, rows), F32),
        compiler_params=pltpu.CompilerParams(vmem_limit_bytes=16 * MIB),
        cost_estimate=pl.CostEstimate(
            flops=2 * items * rows * rows * head_dim,
            bytes_accessed=2 * exchanged.size,
            transcendentals=items * rows * rows,
        ),
        name="key_weights",
    )(exchanged, query_gain.reshape(head_dim, 1), key_gain.reshape(head_dim, 1))


def feature_kernel(key_ref, value_ref, proj_ref, hidden_ref, token_ref, out_ref, attended):
    step = pl.program_id(0)
    parts, pieces, _ = key_ref.shape
    samples, rows, columns = value_ref.shape
    chunks = pieces // samples
    heads = parts * chunks

    @pl.when(step == 0)
    def _():
        row = lax.broadcasted_iota(jnp.int32, (heads, columns), 0)
        column = lax.broadcasted_iota(jnp.int32, (heads, columns), 1)
        own = lax.rem(column, heads) == row
        results = []
        for m in range(samples):
            key = jnp.concatenate(
                [
                    key_ref[:, c * samples + m, :].astype(F32)
                    for c in range(chunks)
                ], axis=0
            )
            product = jnp.dot(key.astype(BF16), value_ref[m], preferred_element_type=F32)
            results.append(jnp.sum(jnp.where(own, product, 0.0), axis=0, keepdims=True))
        results.append(jnp.zeros((16 - samples, columns), F32))
        attended[...] = jnp.concatenate(results, axis=0).astype(BF16)

    part = jnp.dot(attended[...], proj_ref[...], preferred_element_type=F32)[:samples]
    part = part + hidden_ref[...]
    part = part + jnp.sum(token_ref[...].astype(F32), axis=0, keepdims=True) * (1.0 / rows)
    width = out_ref.shape[2]
    for j in range(out_ref.shape[0]):
        out_ref[j] = part[:, j * width : (j + 1) * width]


def feature_part(key_mean, value, w_proj, hidden, tokens, steps):
    parts = key_mean.shape[0]
    samples, rows, columns = value.shape
    own_rows, width = tokens.shape
    cut = width // steps
    return pl.pallas_call(
        feature_kernel,
        grid=(steps,),
        out_shape=jax.ShapeDtypeStruct((parts, samples, width // parts), F32),
        in_specs=[
            pl.BlockSpec(key_mean.shape, lambda i: (0, 0, 0)),
            pl.BlockSpec(value.shape, lambda i: (0, 0, 0)),
            pl.BlockSpec((columns, cut), lambda i: (0, i)),
            pl.BlockSpec((samples, cut), lambda i: (0, i)),
            pl.BlockSpec((own_rows, cut), lambda i: (0, i)),
        ],
        out_specs=pl.BlockSpec((parts // steps, samples, width // parts), lambda i: (i, 0, 0)),
        scratch_shapes=[pltpu.VMEM((16, columns), BF16)],
        compiler_params=pltpu.CompilerParams(vmem_limit_bytes=54 * MIB),
        cost_estimate=pl.CostEstimate(
            flops=2 * samples * rows * columns * 2 + 32 * columns * width,
            bytes_accessed=2 * columns * width + 2 * value.size,
            transcendentals=0,
        ),
        name="feature_part",
    )(key_mean, value, w_proj, hidden, tokens)


def pooled_logits(feature, final_gain, w_head):
    highest = lax.Precision.HIGHEST
    gain_head = jnp.dot(final_gain[None], w_head.astype(F32), precision=highest)
    mean = jnp.mean(feature, axis=-1, keepdims=True)
    centered = feature - mean
    spread = jnp.sum(centered * centered, axis=-1, keepdims=True)
    logits = jnp.dot(centered * final_gain, w_head.astype(F32), precision=highest)
    columns = feature.shape[1]
    samples, classes = logits.shape
    bits = 1
    while bits < lax.axis_size("inp"):
        sent = jnp.concatenate(
            [
                jnp.concatenate([logits, mean, spread], axis=1),
                jnp.pad(gain_head, ((0, 0), (0, 2))),
            ],
            axis=0,
        )
        other = permuted(sent, bits)
        other_mean = other[:samples, classes : classes + 1]
        joint = 0.5 * (mean + other_mean)
        logits = (
            logits
            + other[:samples, :classes]
            + (mean - joint) * gain_head
            + (other_mean - joint) * other[samples:, :classes]
        )
        gap = mean - other_mean
        spread = spread + other[:samples, classes + 1 :] + gap * gap * (0.5 * columns)
        gain_head = gain_head + other[samples:, :classes]
        mean = joint
        columns = 2 * columns
        bits = 2 * bits
    scale = lax.rsqrt(spread / columns + 1e-06)
    return mean, scale, logits * scale


def pipelined(
    tokens,
    dropout_masks,
    input_gain,
    w_qkv,
    w_up,
    query_gain,
    key_gain,
    w_proj,
    w_down,
    final_gain,
    w_head,
):
    n_parts = lax.axis_size("inp")
    me = lax.axis_index("inp")
    model_width = tokens.shape[1]
    n_comps, _, n_heads, _ = w_qkv.shape
    choose = choosers(dropout_masks)
    pieces, choose = gathered_pieces(*own_norm(tokens, input_gain), choose)
    norm = placed(pieces, me)
    together = lax.optimization_barrier

    def exchange(array):
        return lax.all_to_all(array, "inp", split_axis=0, concat_axis=0, tiled=True)

    both = [query_key(norm, choose, w_qkv, c, n_parts) for c in range(n_heads // n_parts)]
    value = values_of(norm, choose, w_qkv)
    exchanged = [exchange(both[0])]
    *both, value = together((*both[1:], value))
    tiles = w_up.shape[0] // UNITS // len(both)
    key_mean, pooled = [], []
    for at, sent in enumerate(both):
        last = exchanged[-1]
        if at > 0:
            pooled[-1], key_mean[-1], sent = together((pooled[-1], key_mean[-1], sent))
        exchanged.append(exchange(sent))
        norm_here, last = together((norm, last))
        pooled.append(hidden_part(norm_here, choose, w_up, at * tiles, tiles))
        key_mean.append(key_weights(last, query_gain, key_gain))
    key_mean.append(key_weights(exchanged[-1], query_gain, key_gain))
    pooled[-1], key_mean[-1] = together((pooled[-1], key_mean[-1]))
    key_mean = jnp.concatenate(key_mean, axis=0).astype(BF16)
    hidden = down_part(jnp.concatenate(pooled, axis=1), w_down)
    key_mean = lax.all_to_all(
        jnp.broadcast_to(key_mean[None], (n_parts,) + key_mean.shape),
        "inp",
        split_axis=0,
        concat_axis=0,
        tiled=True,
    )
    partial_feature = feature_part(
        key_mean, value, w_proj.reshape(n_comps * n_heads, model_width), hidden, tokens, 4
    )
    slice_width = model_width // n_parts
    feature = jnp.sum(
        lax.all_to_all(partial_feature, "inp", split_axis=0, concat_axis=0, tiled=True), axis=0
    )
    gain = lax.dynamic_slice_in_dim(final_gain, me * slice_width, slice_width, 0)
    mean, scale, raw_logits = pooled_logits(feature, gain, w_head)
    embedding = (feature - mean) * scale * gain
    logits = soft_cap * jnp.tanh(raw_logits / soft_cap)
    return (embedding[None], bald_score(logits[None]))


def local(
    tokens,
    dropout_masks,
    input_gain,
    w_qkv,
    w_up,
    query_gain,
    key_gain,
    w_proj,
    w_down,
    final_gain,
    w_head,
):
    n_parts = lax.axis_size("inp")
    local_rows, model_width = tokens.shape
    n_masks, all_rows, n_blocks = dropout_masks.shape
    block_width = model_width // n_blocks
    n_comps, three_kinds, n_heads, ignored_width = w_qkv.shape
    n_units = w_up.shape[0]
    head_dim = n_comps * n_parts
    images = all_rows // PATCHES
    qkv_cols = three_kinds * n_heads * n_comps
    items_dev = n_masks * n_heads // n_parts
    highest = lax.Precision.HIGHEST
    joined_weight = jnp.concatenate(
        [jnp.transpose(w_qkv, (1, 2, 0, 3)).reshape(qkv_cols, model_width), w_up], axis=0
    )
    row_piece = lax.all_gather(tokens, "inp", axis=0, tiled=True)
    row_count = row_piece.shape[0]
    normed = norm_last(row_piece.astype(jnp.float32), input_gain).astype(jnp.bfloat16)
    masked = (
        normed.reshape(1, row_count, n_blocks, block_width)
        * dropout_masks.astype(jnp.bfloat16)[..., None]
    )
    masked = masked.reshape(n_masks, row_count, model_width)
    result = jnp.einsum("mkd,cd->mck", masked, joined_weight, preferred_element_type=jnp.float32)
    projected = 2.0 * result
    qkv_half = (
        projected[:, :qkv_cols]
        .astype(jnp.bfloat16)
        .reshape(n_masks, three_kinds, n_heads * n_comps, all_rows)
    )
    item_shape = (n_parts, items_dev, n_comps, all_rows)
    query_send = qkv_half[:, 0].reshape(item_shape)
    key_send = qkv_half[:, 1].reshape(item_shape)
    value_send = qkv_half[:, 2].reshape(item_shape)
    activated = jax.nn.gelu(projected[:, qkv_cols:], approximate=False)
    pooled_hidden = jnp.mean(activated.reshape(n_masks, n_units, images, PATCHES), axis=-1).astype(
        jnp.bfloat16
    )
    query_in = lax.all_to_all(query_send, "inp", split_axis=0, concat_axis=2, tiled=True)
    key_in = lax.all_to_all(key_send, "inp", split_axis=0, concat_axis=2, tiled=True)
    value_in = lax.all_to_all(value_send, "inp", split_axis=0, concat_axis=2, tiled=True)
    n_items = query_in.shape[1]
    shape_four = (n_items, head_dim, images, PATCHES)
    query_norm = norm_second(query_in.reshape(shape_four).astype(jnp.float32), query_gain).astype(
        jnp.bfloat16
    )
    key_norm = norm_second(key_in.reshape(shape_four).astype(jnp.float32), key_gain).astype(
        jnp.bfloat16
    )
    scores = jnp.einsum(
        "jcip,jciq->jipq", query_norm, key_norm, preferred_element_type=jnp.float32
    ) / math.sqrt(head_dim)
    exp_scores = jnp.exp(scores)
    weights = (exp_scores / jnp.sum(exp_scores, axis=-1, keepdims=True)).astype(jnp.bfloat16)
    query_mean = jnp.sum(weights, axis=2, dtype=jnp.float32) / PATCHES
    pooled = jnp.einsum(
        "jiq,jciq->jic",
        query_mean,
        value_in.reshape(shape_four).astype(jnp.float32),
        precision=highest,
    )
    attended = pooled.astype(jnp.bfloat16)[None]
    returned = lax.all_to_all(attended, "inp", split_axis=3, concat_axis=0, tiled=True)
    returned = returned.reshape(n_masks, n_heads, images, n_comps)
    mixed_sum = jnp.einsum("mhic,chd->imd", returned, w_proj, preferred_element_type=jnp.float32)
    mixed_sum = mixed_sum + jnp.einsum(
        "mfi,fd->imd", pooled_hidden, w_down, preferred_element_type=jnp.float32
    )
    row_ids = lax.axis_index("inp") * local_rows + jnp.arange(local_rows, dtype=jnp.int32)
    row_owner = (row_ids // PATCHES)[None, :] == jnp.arange(images, dtype=jnp.int32)[:, None]
    input_sum = (
        jnp.dot(row_owner.astype(jnp.bfloat16), tokens, preferred_element_type=jnp.float32)
        / PATCHES
    )
    partial_feature = mixed_sum + input_sum[:, None, :]
    feature = lax.psum(partial_feature, "inp")
    normalized = norm_last(feature, final_gain)
    slice_width = model_width // n_parts
    embedding = lax.dynamic_slice_in_dim(
        normalized, lax.axis_index("inp") * slice_width, slice_width, 2
    )
    logit_part = jnp.einsum(
        "imd,dc->imc", embedding.astype(jnp.bfloat16), w_head, preferred_element_type=jnp.float32
    )
    raw_logits = lax.psum(logit_part, "inp")
    logits = soft_cap * jnp.tanh(raw_logits / soft_cap)
    return (embedding, bald_score(logits))


def solution(mesh):
    fits = mesh.shape["inp"] == PIPELINED_PARTS
    return jax.shard_map(
        pipelined if fits else local,
        mesh=mesh,
        in_specs=(
            P(("groups", "inp"), None),
            P(None, "groups", None),
            P(),
            P("inp", None, None, None),
            P("inp", None),
            P(),
            P(),
            P("inp", None, None),
            P("inp", None),
            P(),
            P("inp", None),
        ),
        out_specs=(P("groups", None, "inp"), P("groups")),
        check_vma=False,
    )
```

profile of v0, /device:TPU:0, one launch (start us, length us, event | category | flops | bytes accessed | tf_op | source)
XLA Modules:
  0.0 201.4 jit_solution(16947141730076743943)
XLA Ops:
  0.7 1.0 copy-done.2
  1.6 0.7 copy-done.3
  2.4 0.3 own_norm.1
  2.7 3.1 %collective-permute-start = (bf16[16,4096]{1,0:T(8,128)(2,1)S(1)}, bf16[16,4096]{1,0:T(8,128)(2,1)S(1)}, u32[]{:S(2)}, u32[]{:S(2)}) collective-permute-start(bf16[16,4096]{1,0:T(8,128)(2,1)S(1)} %get-tuple-element.23), channel_id=1, source_target_pairs={{0,4},{1,5},{2,6},{3,7},{4,0},{5,1},{6,2},{7,3},{8,12},{9,13},{10,... | collective-permute-start | bytes 393224 | tf_op jit(solution)/shard_map/ppermute | solution.py:48
  5.8 2.6 %collective-permute-start.1 = (bf16[16,4096]{1,0:T(8,128)(2,1)S(1)}, bf16[16,4096]{1,0:T(8,128)(2,1)S(1)}, u32[]{:S(2)}, u32[]{:S(2)}) collective-permute-start(bf16[16,4096]{1,0:T(8,128)(2,1)S(1)} %get-tuple-element.23), channel_id=1, source_target_pairs={{0,8},{1,9},{2,10},{3,11},{4,12},{5,13},{6,14},{7,15},{8,0},{9,1},... | collective-permute-start | bytes 393224 | tf_op jit(solution)/shard_map/ppermute | solution.py:48
  8.4 1.7 collective-permute-start.3
  10.1 1.3 copy.27
  11.7 2.7 %fusion.choose_ref = bf16[16,128,768]{2,1,0:T(8,128)(2,1)} fusion(pred[128,768]{1,0:T(8,128)(4,1)S(1)} %broadcast_compare_fusion, bf16[16,128,48]{2,1,0:T(8,128)(2,1)S(1)} %bitcast.49, s32[768]{0:T(1024)S(1)} %add_select_fusion), kind=kOutput, calls=%fused_computation.1 | convolution fusion | flops 155750400 | bytes 3443712 | tf_op jit(solution)/shard_map/trb,bc->trc/dot_general | solution.py:130
  14.4 4.3 %collective-permute-done.1 = bf16[16,4096]{1,0:T(8,128)(2,1)S(1)} collective-permute-done((bf16[16,4096]{1,0:T(8,128)(2,1)S(1)}, bf16[16,4096]{1,0:T(8,128)(2,1)S(1)}, u32[]{:S(2)}, u32[]{:S(2)}) %collective-permute-start.1) | collective-permute-done | bytes 131104 | tf_op jit(solution)/shard_map/ppermute | solution.py:48
  18.8 1.6 collective-permute-start.4
  20.4 2.0 collective-permute-start.5
  22.3 1.0 collective-permute-start.6
  23.3 1.5 collective-permute-start.7
  24.8 1.7 collective-permute-done.5.refs_3_
  26.5 7.3 %collective-permute-done.6.refs_4_ = bf16[2,16,2048]{2,1,0:T(8,128)(2,1)S(1)} collective-permute-done((bf16[2,16,2048]{2,1,0:T(8,128)(2,1)S(1)}, bf16[2,16,2048]{2,1,0:T(8,128)(2,1)S(1)}, u32[]{:S(2)}, u32[]{:S(2)}) %collective-permute-start.6) | collective-permute-done | bytes 131104 | tf_op jit(solution)/shard_map/ppermute | solution.py:48
  33.8 0.5 collective-permute-start.10
  34.4 0.4 collective-permute-start.12
  34.8 1.3 collective-permute-done.10.refs_8_
  36.2 0.2 collective-permute-done.12.refs_10_
  36.4 1.2 collective-permute-done.13.refs_11_
  37.6 1.2 place_rows.1.norm_ref
  38.8 1.7 copy-done.1
  40.5 8.1 %query_key.3 = bf16[16,8,16,256]{3,2,1,0:T(8,128)(2,1)} custom-call(bf16[256,6144]{1,0:T(8,128)(2,1)} %copy-done.1, bf16[16,128,768]{2,1,0:T(8,128)(2,1)} %fusion.choose_ref, bf16[8,3,48,6144]{3,2,1,0:T(8,128)(2,1)} %w_ref.7), custom_call_target="tpu_custom_call" | custom-call | flops 3221225472 | bytes 9437184 | tf_op jit(solution)/shard_map/query_key/pallas_call | solution.py:186
  48.6 4.3 %all-to-all-start = ((bf16[16,8,16,256]{3,2,1,0:T(8,128)(2,1)}), bf16[16,8,16,256]{3,2,1,0:T(8,128)(2,1)S(1)}, u32[]{:S(2)}, u32[]{:S(2)}) async-start(bf16[16,8,16,256]{3,2,1,0:T(8,128)(2,1)} %query_key.3), calls=%async_computation | async-start | bytes 2097152 | tf_op jit(solution)/shard_map/all_to_all | solution.py:512
  52.9 8.2 %query_key.5 = bf16[16,8,16,256]{3,2,1,0:T(8,128)(2,1)} custom-call(bf16[256,6144]{1,0:T(8,128)(2,1)} %copy-done.1, bf16[16,128,768]{2,1,0:T(8,128)(2,1)} %fusion.choose_ref, bf16[8,3,48,6144]{3,2,1,0:T(8,128)(2,1)} %w_ref.7), custom_call_target="tpu_custom_call" | custom-call | flops 3221225472 | bytes 9437184 | tf_op jit(solution)/shard_map/query_key/pallas_call | solution.py:186
  61.1 8.1 %query_key.4 = bf16[16,8,16,256]{3,2,1,0:T(8,128)(2,1)} custom-call(bf16[256,6144]{1,0:T(8,128)(2,1)} %copy-done.1, bf16[16,128,768]{2,1,0:T(8,128)(2,1)} %fusion.choose_ref, bf16[8,3,48,6144]{3,2,1,0:T(8,128)(2,1)} %w_ref.7), custom_call_target="tpu_custom_call" | custom-call | flops 3221225472 | bytes 9437184 | tf_op jit(solution)/shard_map/query_key/pallas_call | solution.py:186
  69.3 8.9 %value_rows.1.value_ref = bf16[8,256,384]{2,1,0:T(8,128)(2,1)} custom-call(bf16[256,6144]{1,0:T(8,128)(2,1)} %copy-done.1, bf16[16,128,768]{2,1,0:T(8,128)(2,1)} %fusion.choose_ref, bf16[8,3,48,6144]{3,2,1,0:T(8,128)(2,1)} %w_ref.7), custom_call_target="tpu_custom_call" | custom-call | flops 4831838208 | bytes 11010048 | tf_op jit(solution)/shard_map/value_rows/pallas_call | solution.py:236
  78.1 6.0 %all-to-all-start.1 = ((bf16[16,8,16,256]{3,2,1,0:T(8,128)(2,1)}), bf16[16,8,16,256]{3,2,1,0:T(8,128)(2,1)S(1)}, u32[]{:S(2)}, u32[]{:S(2)}) async-start(bf16[16,8,16,256]{3,2,1,0:T(8,128)(2,1)} %query_key.4), calls=%async_computation.1 | async-start | bytes 2097152 | tf_op jit(solution)/shard_map/all_to_all | solution.py:512
  84.4 2.1 %key_weights.3 = f32[8,256]{1,0:T(8,128)S(1)} custom-call(bf16[16,8,16,256]{3,2,1,0:T(8,128)(2,1)S(1)} %all-to-all-done.x_ref, f32[128,1]{1,0:T(8,128)S(1)} %copy.31.query_gain_ref, f32[128,1]{1,0:T(8,128)S(1)} %copy.32.key_gain_ref), custom_call_target="tpu_custom_call" | custom-call | flops 134217728 | bytes 1048576 | tf_op jit(solution)/shard_map/key_weights/pallas_call | solution.py:378
  86.5 19.2 %hidden_part.2 = f32[8,768]{1,0:T(8,128)} custom-call(bf16[256,6144]{1,0:T(8,128)(2,1)} %copy-done.1, bf16[16,128,768]{2,1,0:T(8,128)(2,1)} %fusion.choose_ref, bf16[1536,6144]{1,0:T(8,128)(2,1)} %up_ref.3), custom_call_target="tpu_custom_call" | custom-call | flops 9663676416 | bytes 15728640 | tf_op jit(solution)/shard_map/hidden_part/pallas_call | solution.py:295
  105.7 1.4 all-to-all-done.1.x_ref
  107.1 6.9 %all-to-all-start.2 = ((bf16[16,8,16,256]{3,2,1,0:T(8,128)(2,1)}), bf16[16,8,16,256]{3,2,1,0:T(8,128)(2,1)S(1)}, u32[]{:S(2)}, u32[]{:S(2)}) async-start(bf16[16,8,16,256]{3,2,1,0:T(8,128)(2,1)} %query_key.5), calls=%async_computation.2 | async-start | bytes 2097152 | tf_op jit(solution)/shard_map/all_to_all | solution.py:512
  114.0 2.1 %key_weights.4 = f32[8,256]{1,0:T(8,128)S(1)} custom-call(bf16[16,8,16,256]{3,2,1,0:T(8,128)(2,1)S(1)} %all-to-all-done.1.x_ref, f32[128,1]{1,0:T(8,128)S(1)} %copy.31.query_gain_ref, f32[128,1]{1,0:T(8,128)S(1)} %copy.32.key_gain_ref), custom_call_target="tpu_custom_call" | custom-call | flops 134217728 | bytes 1048576 | tf_op jit(solution)/shard_map/key_weights/pallas_call | solution.py:378
  116.1 19.2 %hidden_part.3 = f32[8,768]{1,0:T(8,128)} custom-call(bf16[256,6144]{1,0:T(8,128)(2,1)} %copy-done.1, bf16[16,128,768]{2,1,0:T(8,128)(2,1)} %fusion.choose_ref, bf16[1536,6144]{1,0:T(8,128)(2,1)} %up_ref.3), custom_call_target="tpu_custom_call" | custom-call | flops 9663676416 | bytes 15728640 | tf_op jit(solution)/shard_map/hidden_part/pallas_call | solution.py:295
  135.3 1.6 all-to-all-done.2.x_ref
  136.9 2.1 %key_weights.5 = f32[8,256]{1,0:T(8,128)S(1)} custom-call(bf16[16,8,16,256]{3,2,1,0:T(8,128)(2,1)S(1)} %all-to-all-done.2.x_ref, f32[128,1]{1,0:T(8,128)S(1)} %copy.31.query_gain_ref, f32[128,1]{1,0:T(8,128)S(1)} %copy.32.key_gain_ref), custom_call_target="tpu_custom_call" | custom-call | flops 134217728 | bytes 1048576 | tf_op jit(solution)/shard_map/key_weights/pallas_call | solution.py:378
  139.0 0.7 broadcast_in_dim.18
  139.7 6.9 %all-to-all-start.3 = ((bf16[16,24,256]{2,1,0:T(8,128)(2,1)}), bf16[16,24,256]{2,1,0:T(8,128)(2,1)S(1)}, u32[]{:S(2)}, u32[]{:S(2)}) async-start(bf16[16,24,256]{2,1,0:T(8,128)(2,1)} %broadcast_in_dim.18), calls=%async_computation.3 | async-start | bytes 393216 | tf_op jit(solution)/shard_map/all_to_all | solution.py:532
  146.6 1.4 pad_maximum_fusion.2.pooled_ref
  147.9 9.4 %down_part.1.hidden_ref = f32[8,6144]{1,0:T(8,128)} custom-call(f32[8,1536]{1,0:T(8,128)} %pad_maximum_fusion.2.pooled_ref, bf16[1536,6144]{1,0:T(8,128)(2,1)} %down_ref.1), custom_call_target="tpu_custom_call" | custom-call | flops 301989888 | bytes 18874368 | tf_op jit(solution)/shard_map/down_part/pallas_call | solution.py:334
  157.4 0.7 copy-done.4
  158.1 5.5 %feature_part.1 = f32[16,8,384]{2,1,0:T(8,128)} custom-call(bf16[16,24,256]{2,1,0:T(8,128)(2,1)} %copy-done.4, bf16[8,256,384]{2,1,0:T(8,128)(2,1)} %value_rows.1.value_ref, bf16[384,6144]{1,0:T(8,128)(2,1)} %bitcast.47, f32[8,6144]{1,0:T(8,128)} %down_part.1.hidden_ref, bf16[16,6144]{1,0:T(8,128)(2,1)} %token_ref.1), custom_call_target="tpu_custom_call" | custom-call | flops 78643200 | bytes 6291456 | tf_op jit(solution)/shard_map/feature_part/pallas_call | solution.py:429
  163.6 6.0 %all-to-all-start.4 = ((f32[16,8,384]{2,1,0:T(8,128)}), f32[16,8,384]{2,1,0:T(8,128)S(1)}, u32[]{:S(2)}, u32[]{:S(2)}) async-start(f32[16,8,384]{2,1,0:T(8,128)} %feature_part.1), calls=%async_computation.4 | async-start | bytes 393216 | tf_op jit(solution)/shard_map/all_to_all | solution.py:544
  169.6 0.8 dynamic_slice.3
  170.4 0.7 fusion.45
  171.2 7.5 %all-to-all-done.4 = f32[16,8,384]{2,1,0:T(8,128)S(1)} async-done(((f32[16,8,384]{2,1,0:T(8,128)}), f32[16,8,384]{2,1,0:T(8,128)S(1)}, u32[]{:S(2)}, u32[]{:S(2)}) %all-to-all-start.4) | async-done | bytes 196640 | tf_op jit(solution)/shard_map/all_to_all | solution.py:544
  178.6 0.2 fusion.40
  178.8 0.8 fusion.19
  179.5 0.2 multiply_reduce_fusion.1
  180.0 1.2 collective-permute-done.14
  181.3 0.2 subtract_reduce_fusion.7
  181.6 4.3 %collective-permute-done.15 = f32[9,1002]{1,0:T(8,128)S(1)} collective-permute-done((f32[9,1002]{1,0:T(8,128)S(1)}, f32[9,1002]{1,0:T(8,128)S(1)}, u32[]{:S(2)}, u32[]{:S(2)}) %collective-permute-start.15) | collective-permute-done | bytes 36104 | tf_op jit(solution)/shard_map/ppermute | solution.py:48
  185.9 0.2 subtract_reduce_fusion.5
  186.2 0.1 collective-permute-start.16
  186.4 4.1 %collective-permute-done.16 = f32[9,1002]{1,0:T(8,128)S(1)} collective-permute-done((f32[9,1002]{1,0:T(8,128)S(1)}, f32[9,1002]{1,0:T(8,128)S(1)}, u32[]{:S(2)}, u32[]{:S(2)}) %collective-permute-start.16) | collective-permute-done | bytes 36104 | tf_op jit(solution)/shard_map/ppermute | solution.py:48
  190.5 0.2 subtract_reduce_fusion.3
  190.8 0.7 collective-permute-start.17
  191.6 4.7 %collective-permute-done.17 = f32[9,1002]{1,0:T(8,128)S(1)} collective-permute-done((f32[9,1002]{1,0:T(8,128)S(1)}, f32[9,1002]{1,0:T(8,128)S(1)}, u32[]{:S(2)}, u32[]{:S(2)}) %collective-permute-start.17) | collective-permute-done | bytes 36104 | tf_op jit(solution)/shard_map/ppermute | solution.py:48
  196.3 0.2 subtract_reduce_fusion.1
  196.5 0.2 exponential_reduce_fusion
  196.7 0.2 multiply_reduce_fusion
  196.9 0.7 subtract_reduce_fusion.8
  197.6 0.6 fusion.25
  198.9 0.7 fusion.18
  (58 shorter events, 1.6 us)
Async XLA Ops:
  0.6 169.8 %copy-start = (bf16[384,1000]{0,1:T(8,128)(2,1)S(1)}, bf16[384,1000]{0,1:T(8,128)(2,1)}, u32[]{:S(2)}) copy-start(bf16[384,1000]{0,1:T(8,128)(2,1)} %param.21) | copy-start | bytes 2304004
  0.6 1.0 copy-start.2
  1.6 0.7 copy-start.3
  2.7 11.7 %collective-permute-start = (bf16[16,4096]{1,0:T(8,128)(2,1)S(1)}, bf16[16,4096]{1,0:T(8,128)(2,1)S(1)}, u32[]{:S(2)}, u32[]{:S(2)}) collective-permute-start(bf16[16,4096]{1,0:T(8,128)(2,1)S(1)} %get-tuple-element.23), channel_id=1, source_target_pairs={{0,4},{1,5},{2,6},{3,7},{4,0},{5,1},{6,2},{7,3},{8,12},{9,13},{10,... | collective-permute-start | bytes 393224 | tf_op jit(solution)/shard_map/ppermute | solution.py:48
  5.8 12.9 %collective-permute-start.1 = (bf16[16,4096]{1,0:T(8,128)(2,1)S(1)}, bf16[16,4096]{1,0:T(8,128)(2,1)S(1)}, u32[]{:S(2)}, u32[]{:S(2)}) collective-permute-start(bf16[16,4096]{1,0:T(8,128)(2,1)S(1)} %get-tuple-element.23), channel_id=1, source_target_pairs={{0,8},{1,9},{2,10},{3,11},{4,12},{5,13},{6,14},{7,15},{8,0},{9,1},... | collective-permute-start | bytes 393224 | tf_op jit(solution)/shard_map/ppermute | solution.py:48
  8.4 10.3 %collective-permute-start.2 = (bf16[16,4096]{1,0:T(8,128)(2,1)S(1)}, bf16[16,4096]{1,0:T(8,128)(2,1)S(1)}, u32[]{:S(2)}, u32[]{:S(2)}) collective-permute-start(bf16[16,4096]{1,0:T(8,128)(2,1)S(1)} %get-tuple-element.23), channel_id=1, source_target_pairs={{0,12},{1,13},{2,14},{3,15},{4,8},{5,9},{6,10},{7,11},{8,4},{9,5},... | collective-permute-start | bytes 393224 | tf_op jit(solution)/shard_map/ppermute | solution.py:48
  8.4 6.0 %collective-permute-start.3 = (bf16[16,2048]{1,0:T(8,128)(2,1)S(1)}, bf16[16,2048]{1,0:T(8,128)(2,1)S(1)}, u32[]{:S(2)}, u32[]{:S(2)}) collective-permute-start(bf16[16,2048]{1,0:T(8,128)(2,1)S(1)} %get-tuple-element.24), channel_id=1, source_target_pairs={{0,2},{1,3},{2,0},{3,1},{4,6},{5,7},{6,4},{7,5},{8,10},{9,11},{10,... | collective-permute-start | bytes 196616 | tf_op jit(solution)/shard_map/ppermute | solution.py:48
  18.8 15.0 %collective-permute-start.4 = (bf16[4,16,4096]{2,1,0:T(8,128)(2,1)S(1)}, bf16[4,16,4096]{2,1,0:T(8,128)(2,1)S(1)}, u32[]{:S(2)}, u32[]{:S(2)}) collective-permute-start(bf16[4,16,4096]{2,1,0:T(8,128)(2,1)S(1)} %pad_maximum_fusion.refs_0_), channel_id=1, source_target_pairs={{0,2},{1,3},{2,0},{3,1},{4,6},{5,7},{6,4},{7,5},{8,10},{9,11},{10,... | collective-permute-start | bytes 1572872 | tf_op jit(solution)/shard_map/ppermute | solution.py:48
  20.4 6.1 %collective-permute-start.5 = (bf16[2,16,2048]{2,1,0:T(8,128)(2,1)S(1)}, bf16[2,16,2048]{2,1,0:T(8,128)(2,1)S(1)}, u32[]{:S(2)}, u32[]{:S(2)}) collective-permute-start(bf16[2,16,2048]{2,1,0:T(8,128)(2,1)S(1)} %pad_maximum_fusion.1.refs_2_), channel_id=1, source_target_pairs={{0,4},{1,5},{2,6},{3,7},{4,0},{5,1},{6,2},{7,3},{8,12},{9,13},{10,... | collective-permute-start | bytes 393224 | tf_op jit(solution)/shard_map/ppermute | solution.py:48
  22.3 11.5 %collective-permute-start.6 = (bf16[2,16,2048]{2,1,0:T(8,128)(2,1)S(1)}, bf16[2,16,2048]{2,1,0:T(8,128)(2,1)S(1)}, u32[]{:S(2)}, u32[]{:S(2)}) collective-permute-start(bf16[2,16,2048]{2,1,0:T(8,128)(2,1)S(1)} %pad_maximum_fusion.1.refs_2_), channel_id=1, source_target_pairs={{0,8},{1,9},{2,10},{3,11},{4,12},{5,13},{6,14},{7,15},{8,0},{9,1},... | collective-permute-start | bytes 393224 | tf_op jit(solution)/shard_map/ppermute | solution.py:48
  23.3 10.5 %collective-permute-start.7 = (bf16[2,16,2048]{2,1,0:T(8,128)(2,1)S(1)}, bf16[2,16,2048]{2,1,0:T(8,128)(2,1)S(1)}, u32[]{:S(2)}, u32[]{:S(2)}) collective-permute-start(bf16[2,16,2048]{2,1,0:T(8,128)(2,1)S(1)} %pad_maximum_fusion.1.refs_2_), channel_id=1, source_target_pairs={{0,12},{1,13},{2,14},{3,15},{4,8},{5,9},{6,10},{7,11},{8,4},{9,5},... | collective-permute-start | bytes 393224 | tf_op jit(solution)/shard_map/ppermute | solution.py:48
  24.8 11.4 %collective-permute-start.8 = (bf16[4,16,4096]{2,1,0:T(8,128)(2,1)S(1)}, bf16[4,16,4096]{2,1,0:T(8,128)(2,1)S(1)}, u32[]{:S(2)}, u32[]{:S(2)}) collective-permute-start(bf16[4,16,4096]{2,1,0:T(8,128)(2,1)S(1)} %pad_maximum_fusion.refs_0_), channel_id=1, source_target_pairs={{0,1},{1,0},{2,3},{3,2},{4,5},{5,4},{6,7},{7,6},{8,9},{9,8},{10,11... | collective-permute-start | bytes 1572872 | tf_op jit(solution)/shard_map/ppermute | solution.py:48
  33.8 3.8 %collective-permute-start.9 = (bf16[4,16,4096]{2,1,0:T(8,128)(2,1)S(1)}, bf16[4,16,4096]{2,1,0:T(8,128)(2,1)S(1)}, u32[]{:S(2)}, u32[]{:S(2)}) collective-permute-start(bf16[4,16,4096]{2,1,0:T(8,128)(2,1)S(1)} %collective-permute-done.4.refs_1_), channel_id=1, source_target_pairs={{0,1},{1,0},{2,3},{3,2},{4,5},{5,4},{6,7},{7,6},{8,9},{9,8},{10,11... | collective-permute-start | bytes 1572872 | tf_op jit(solution)/shard_map/ppermute | solution.py:48
  33.8 2.3 %collective-permute-start.10 = (bf16[2,16,2048]{2,1,0:T(8,128)(2,1)S(1)}, bf16[2,16,2048]{2,1,0:T(8,128)(2,1)S(1)}, u32[]{:S(2)}, u32[]{:S(2)}) collective-permute-start(bf16[2,16,2048]{2,1,0:T(8,128)(2,1)S(1)} %pad_maximum_fusion.1.refs_2_), channel_id=1, source_target_pairs={{0,1},{1,0},{2,3},{3,2},{4,5},{5,4},{6,7},{7,6},{8,9},{9,8},{10,11... | collective-permute-start | bytes 393224 | tf_op jit(solution)/shard_map/ppermute | solution.py:48
  34.3 1.9 collective-permute-start.11
  34.4 2.0 %collective-permute-start.12 = (bf16[2,16,2048]{2,1,0:T(8,128)(2,1)S(1)}, bf16[2,16,2048]{2,1,0:T(8,128)(2,1)}, u32[]{:S(2)}, u32[]{:S(2)}) collective-permute-start(bf16[2,16,2048]{2,1,0:T(8,128)(2,1)S(1)} %collective-permute-done.6.refs_4_), channel_id=1, source_target_pairs={{0,1},{1,0},{2,3},{3,2},{4,5},{5,4},{6,7},{7,6},{8,9},{9,8},{10,11... | collective-permute-start | bytes 393224 | tf_op jit(solution)/shard_map/ppermute | solution.py:48
  36.1 1.5 collective-permute-start.13
  38.8 1.7 copy-start.1
  48.6 29.5 %all-to-all-start = ((bf16[16,8,16,256]{3,2,1,0:T(8,128)(2,1)}), bf16[16,8,16,256]{3,2,1,0:T(8,128)(2,1)S(1)}, u32[]{:S(2)}, u32[]{:S(2)}) async-start(bf16[16,8,16,256]{3,2,1,0:T(8,128)(2,1)} %query_key.3), calls=%async_computation | async-start | bytes 2097152 | tf_op jit(solution)/shard_map/all_to_all | solution.py:512
  69.3 14.9 %copy-start.6 = (f32[128]{0:T(128)S(1)}, f32[128]{0:T(128)}, u32[]{:S(2)}) copy-start(f32[128]{0:T(128)} %param.16) | copy-start | bytes 1540
  69.3 15.0 %copy-start.7 = (f32[128]{0:T(128)S(1)}, f32[128]{0:T(128)}, u32[]{:S(2)}) copy-start(f32[128]{0:T(128)} %param.17) | copy-start | bytes 1540
  78.1 29.0 %all-to-all-start.1 = ((bf16[16,8,16,256]{3,2,1,0:T(8,128)(2,1)}), bf16[16,8,16,256]{3,2,1,0:T(8,128)(2,1)S(1)}, u32[]{:S(2)}, u32[]{:S(2)}) async-start(bf16[16,8,16,256]{3,2,1,0:T(8,128)(2,1)} %query_key.4), calls=%async_computation.1 | async-start | bytes 2097152 | tf_op jit(solution)/shard_map/all_to_all | solution.py:512
  107.1 29.8 %all-to-all-start.2 = ((bf16[16,8,16,256]{3,2,1,0:T(8,128)(2,1)}), bf16[16,8,16,256]{3,2,1,0:T(8,128)(2,1)S(1)}, u32[]{:S(2)}, u32[]{:S(2)}) async-start(bf16[16,8,16,256]{3,2,1,0:T(8,128)(2,1)} %query_key.5), calls=%async_computation.2 | async-start | bytes 2097152 | tf_op jit(solution)/shard_map/all_to_all | solution.py:512
  116.1 30.5 %copy-start.5 = (f32[8,768]{1,0:T(8,128)S(1)}, f32[8,768]{1,0:T(8,128)}, u32[]{:S(2)}) copy-start(f32[8,768]{1,0:T(8,128)} %hidden_part.2) | copy-start | bytes 73732
  139.7 17.7 %all-to-all-start.3 = ((bf16[16,24,256]{2,1,0:T(8,128)(2,1)}), bf16[16,24,256]{2,1,0:T(8,128)(2,1)S(1)}, u32[]{:S(2)}, u32[]{:S(2)}) async-start(bf16[16,24,256]{2,1,0:T(8,128)(2,1)} %broadcast_in_dim.18), calls=%async_computation.3 | async-start | bytes 393216 | tf_op jit(solution)/shard_map/all_to_all | solution.py:532
  157.4 0.7 copy-start.4
  163.6 15.0 %all-to-all-start.4 = ((f32[16,8,384]{2,1,0:T(8,128)}), f32[16,8,384]{2,1,0:T(8,128)S(1)}, u32[]{:S(2)}, u32[]{:S(2)}) async-start(f32[16,8,384]{2,1,0:T(8,128)} %feature_part.1), calls=%async_computation.4 | async-start | bytes 393216 | tf_op jit(solution)/shard_map/all_to_all | solution.py:544
  180.0 1.3 collective-permute-start.14
  181.6 4.3 %collective-permute-start.15 = (f32[9,1002]{1,0:T(8,128)S(1)}, f32[9,1002]{1,0:T(8,128)S(1)}, u32[]{:S(2)}, u32[]{:S(2)}) collective-permute-start(f32[9,1002]{1,0:T(8,128)S(1)} %select_maximum_fusion.2), channel_id=1, source_target_pairs={{0,2},{1,3},{2,0},{3,1},{4,6},{5,7},{6,4},{7,5},{8,10},{9,11},{10,... | collective-permute-start | bytes 108224 | tf_op jit(solution)/shard_map/ppermute | solution.py:48
  186.2 4.3 %collective-permute-start.16 = (f32[9,1002]{1,0:T(8,128)S(1)}, f32[9,1002]{1,0:T(8,128)S(1)}, u32[]{:S(2)}, u32[]{:S(2)}) collective-permute-start(f32[9,1002]{1,0:T(8,128)S(1)} %select_maximum_fusion.1), channel_id=1, source_target_pairs={{0,4},{1,5},{2,6},{3,7},{4,0},{5,1},{6,2},{7,3},{8,12},{9,13},{10,... | collective-permute-start | bytes 108224 | tf_op jit(solution)/shard_map/ppermute | solution.py:48
  190.8 5.4 %collective-permute-start.17 = (f32[9,1002]{1,0:T(8,128)S(1)}, f32[9,1002]{1,0:T(8,128)S(1)}, u32[]{:S(2)}, u32[]{:S(2)}) collective-permute-start(f32[9,1002]{1,0:T(8,128)S(1)} %select_maximum_fusion), channel_id=1, source_target_pairs={{0,8},{1,9},{2,10},{3,11},{4,12},{5,13},{6,14},{7,15},{8,0},{9,1},... | collective-permute-start | bytes 108224 | tf_op jit(solution)/shard_map/ppermute | solution.py:48
where the time goes:
time: 202 us; the launch traced here: 201 us
  Pallas kernels  94.5 us (47%)
  starting transfers between devices  45.5 us (23%)
  waiting for transfers between devices  40.7 us (20%)
  local copies, waits for them, and re-layouts  7.34 us (4%)
  other arithmetic  5.75 us (3%)
  matrix products  4.17 us (2%)
  between operations  3.39 us (2%)
    pallas_call x2, Pallas kernels, hidden_part(): pl.pallas_call(hidden_kernel, grid=(tiles, width // depth), out_shape=jax...  38.4 us
    ppermute x18, waiting for transfers between devices, permuted(): return lax.ppermute(array, 'inp', [(i, i ^ bits) for i in range(count)])  30.2 us
    pallas_call x3, Pallas kernels, query_key(): pl.pallas_call(query_key_kernel, grid=(width // depth,), out_shape=jax.Sh...  24.5 us
    all_to_all x3, starting transfers between devices, exchange(): return lax.all_to_all(array, 'inp', split_axis=0, concat_axis=0, tiled=True)  17.1 us
    ppermute x18, starting transfers between devices, permuted(): return lax.ppermute(array, 'inp', [(i, i ^ bits) for i in range(count)])  15.5 us
    pallas_call x1, Pallas kernels, down_part(): pl.pallas_call(down_kernel, grid=(units // UNITS,), out_shape=jax.ShapeDt...  9.44 us
    pallas_call x1, Pallas kernels, values_of(): pl.pallas_call(value_kernel, grid=(width // depth,), out_shape=jax.ShapeD...  8.87 us
    all_to_all x1, waiting for transfers between devices, pipelined(): lax.all_to_all(partial_feature, 'inp', split_axis=0, concat_axis=0, tiled...  7.46 us
  transfers between devices with their start and end apart: 23, of which 13 were waited for; matrix products, arithmetic and copies ran while one was open for 4% of the time, Pallas kernels for 38%

commit v1 on v0

--- a/solution.py
+++ b/solution.py
@@ -328,7 +328,7 @@
         out_ref[...] += part
 
 
-def down_part(pooled, w_down):
+def down_part(pooled, w_down, first):
     samples, units = pooled.shape
     width = w_down.shape[1]
     return pl.pallas_call(
@@ -337,7 +337,7 @@
         out_shape=jax.ShapeDtypeStruct((samples, width), F32),
         in_specs=[
             pl.BlockSpec((samples, UNITS), lambda i: (0, i)),
-            pl.BlockSpec((UNITS, width), lambda i: (i, 0)),
+            pl.BlockSpec((UNITS, width), lambda i: (first + i, 0)),
         ],
         out_specs=pl.BlockSpec((samples, width), lambda i: (0, 0)),
         compiler_params=pltpu.CompilerParams(vmem_limit_bytes=54 * MIB),
@@ -399,7 +399,11 @@
     def _():
         row = lax.broadcasted_iota(jnp.int32, (heads, columns), 0)
         column = lax.broadcasted_iota(jnp.int32, (heads, columns), 1)
-        own = lax.rem(column, heads) == row
+        source, piece = lax.rem(row, parts), row // parts
+        head = jnp.where(
+            piece == 0, heads - parts + source, source * (chunks - 1) + piece - 1
+        )
+        own = lax.rem(column, heads) == head
         results = []
         for m in range(samples):
             key = jnp.concatenate(
@@ -439,7 +443,7 @@
         ],
         out_specs=pl.BlockSpec((parts // steps, samples, width // parts), lambda i: (i, 0, 0)),
         scratch_shapes=[pltpu.VMEM((16, columns), BF16)],
-        compiler_params=pltpu.CompilerParams(vmem_limit_bytes=54 * MIB),
+        compiler_params=pltpu.CompilerParams(vmem_limit_bytes=16 * MIB),
         cost_estimate=pl.CostEstimate(
             flops=2 * samples * rows * columns * 2 + 32 * columns * width,
             bytes_accessed=2 * columns * width + 2 * value.size,
@@ -509,26 +513,28 @@
     together = lax.optimization_barrier
 
     def exchange(array):
+        heads, samples, both, rows = array.shape
+        array = array.reshape(n_parts, heads // n_parts * samples, both, rows)
         return lax.all_to_all(array, "inp", split_axis=0, concat_axis=0, tiled=True)
 
-    both = [query_key(norm, choose, w_qkv, c, n_parts) for c in range(n_heads // n_parts)]
+    ahead = n_parts
+    behind = n_heads - ahead
+    first = query_key(norm, choose, w_qkv, behind // ahead, ahead)
+    second = query_key(norm, choose, w_qkv, 0, behind)
     value = values_of(norm, choose, w_qkv)
-    exchanged = [exchange(both[0])]
-    *both, value = together((*both[1:], value))
-    tiles = w_up.shape[0] // UNITS // len(both)
-    key_mean, pooled = [], []
-    for at, sent in enumerate(both):
-        last = exchanged[-1]
-        if at > 0:
-            pooled[-1], key_mean[-1], sent = together((pooled[-1], key_mean[-1], sent))
-        exchanged.append(exchange(sent))
-        norm_here, last = together((norm, last))
-        pooled.append(hidden_part(norm_here, choose, w_up, at * tiles, tiles))
-        key_mean.append(key_weights(last, query_gain, key_gain))
-    key_mean.append(key_weights(exchanged[-1], query_gain, key_gain))
-    pooled[-1], key_mean[-1] = together((pooled[-1], key_mean[-1]))
-    key_mean = jnp.concatenate(key_mean, axis=0).astype(BF16)
-    hidden = down_part(jnp.concatenate(pooled, axis=1), w_down)
+    first = exchange(first)
+    second, value = together((second, value))
+    second = exchange(second)
+    norm, first = together((norm, first))
+    tiles = w_up.shape[0] // UNITS // 2
+    pooled = hidden_part(norm, choose, w_up, 0, tiles)
+    more_pooled = hidden_part(norm, choose, w_up, tiles, tiles)
+    hidden = down_part(pooled, w_down, 0)
+    key_mean = key_weights(first, query_gain, key_gain)
+    more = key_weights(second, query_gain, key_gain)
+    hidden, more_pooled, key_mean, more = together((hidden, more_pooled, key_mean, more))
+    key_mean = jnp.concatenate([key_mean, more], axis=0).astype(BF16)
+    hidden = hidden + down_part(more_pooled, w_down, tiles)
     key_mean = lax.all_to_all(
         jnp.broadcast_to(key_mean[None], (n_parts,) + key_mean.shape),
         "inp",

time: 202 us -> 193 us (0.955)
  starting transfers between devices: 45.5 us -> 36.3 us
  local copies, waits for them, and re-layouts: 7.34 us -> 11.2 us
  Pallas kernels: 94.5 us -> 91.4 us
    all_to_all x3 -> x2, starting transfers between devices: 17.1 us -> 11.1 us  [exchange(): return lax.all_to_all(array, 'inp', split_axis=0, concat_axis=0, tiled=True)]
    unnamed x17 -> x25, local copies, waits for them, and re-layouts: 5.44 us -> 9.35 us
    pallas_call x3 -> x2, Pallas kernels: 24.5 us -> 21 us  [query_key(): pl.pallas_call(query_key_kernel, grid=(width // depth,), out_shape=jax.Sh...]
    pallas_call x1, Pallas kernels: 5.55 us -> 2.82 us  [feature_part(): pl.pallas_call(feature_kernel, grid=(steps,), out_shape=jax.ShapeDtypeStr...]
    all_to_all x1, waiting for transfers between devices: 0.01 us -> 2.2 us  [pipelined(): lax.all_to_all(jnp.broadcast_to(key_mean[None], (n_parts,) + key_mean.sha...]
    all_to_all x1, starting transfers between devices: 6 us -> 3.84 us  [pipelined(): lax.all_to_all(partial_feature, 'inp', split_axis=0, concat_axis=0, tiled...]
    pallas_call x1 -> x2, Pallas kernels: 9.44 us -> 11.5 us  [down_part(): pl.pallas_call(down_kernel, grid=(units // UNITS,), out_shape=jax.ShapeDt...]
    pallas_call x3 -> x2, Pallas kernels: 6.27 us -> 7.2 us  [key_weights(): pl.pallas_call(functools.partial(attention_kernel, items), out_shape=jax....]
  transfers between devices with their start and end apart: 23 -> 22, of which waited for: 13 -> 13; matrix products, arithmetic and copies ran while one was open for 4% -> 4% of each run, Pallas kernels for 38% -> 38%
where the time goes in v1:
time: 193 us; the launch traced here: 192 us
  Pallas kernels  91.4 us (47%)
  waiting for transfers between devices  40 us (21%)
  starting transfers between devices  36.3 us (19%)
  local copies, waits for them, and re-layouts  11.2 us (6%)
  other arithmetic  5.27 us (3%)
  matrix products  4.16 us (2%)
  between operations  3.36 us (2%)
    pallas_call x2, Pallas kernels, hidden_part(): pl.pallas_call(hidden_kernel, grid=(tiles, width // depth), out_shape=jax...  38.4 us
    ppermute x18, waiting for transfers between devices, permuted(): return lax.ppermute(array, 'inp', [(i, i ^ bits) for i in range(count)])  29.3 us
    pallas_call x2, Pallas kernels, query_key(): pl.pallas_call(query_key_kernel, grid=(width // depth,), out_shape=jax.Sh...  21 us
    ppermute x18, starting transfers between devices, permuted(): return lax.ppermute(array, 'inp', [(i, i ^ bits) for i in range(count)])  15.4 us
    pallas_call x2, Pallas kernels, down_part(): pl.pallas_call(down_kernel, grid=(units // UNITS,), out_shape=jax.ShapeDt...  11.5 us
    all_to_all x2, starting transfers between devices, exchange(): return lax.all_to_all(array, 'inp', split_axis=0, concat_axis=0, tiled=True)  11.1 us
    unnamed x25, local copies, waits for them, and re-layouts  9.35 us
    pallas_call x1, Pallas kernels, values_of(): pl.pallas_call(value_kernel, grid=(width // depth,), out_shape=jax.ShapeD...  8.96 us
  transfers between devices with their start and end apart: 22, of which 13 were waited for; matrix products, arithmetic and copies ran while one was open for 4% of the time, Pallas kernels for 38%

profile of v1, /device:TPU:0, one launch (start us, length us, event | category | flops | bytes accessed | tf_op | source)
XLA Modules:
  0.0 191.8 jit_solution(18244674480657286094)
XLA Ops:
  0.7 1.0 copy-done.6
  1.6 0.7 copy-done.8
  2.4 0.3 own_norm.1
  2.7 5.1 %collective-permute-start.2 = (bf16[16,4096]{1,0:T(8,128)(2,1)S(1)}, bf16[16,4096]{1,0:T(8,128)(2,1)S(1)}, u32[]{:S(2)}, u32[]{:S(2)}) collective-permute-start(bf16[16,4096]{1,0:T(8,128)(2,1)S(1)} %get-tuple-element.19), channel_id=1, source_target_pairs={{0,12},{1,13},{2,14},{3,15},{4,8},{5,9},{6,10},{7,11},{8,4},{9,5},... | collective-permute-start | bytes 393224 | tf_op jit(solution)/shard_map/ppermute | solution.py:48
  7.8 0.6 collective-permute-start
  8.5 1.7 collective-permute-start.3
  10.1 1.3 copy.25
  11.7 2.7 %fusion.choose_ref = bf16[16,128,768]{2,1,0:T(8,128)(2,1)} fusion(pred[128,768]{1,0:T(8,128)(4,1)S(1)} %broadcast_compare_fusion, bf16[16,128,48]{2,1,0:T(8,128)(2,1)S(1)} %bitcast.51, s32[768]{0:T(1024)S(1)} %add_select_fusion), kind=kOutput, calls=%fused_computation.1 | convolution fusion | flops 155750400 | bytes 3443712 | tf_op jit(solution)/shard_map/trb,bc->trc/dot_general | solution.py:130
  14.4 4.5 %collective-permute-done.1 = bf16[16,4096]{1,0:T(8,128)(2,1)S(1)} collective-permute-done((bf16[16,4096]{1,0:T(8,128)(2,1)S(1)}, bf16[16,4096]{1,0:T(8,128)(2,1)S(1)}, u32[]{:S(2)}, u32[]{:S(2)}) %collective-permute-start.1) | collective-permute-done | bytes 131104 | tf_op jit(solution)/shard_map/ppermute | solution.py:48
  19.0 1.6 collective-permute-start.4
  20.6 3.0 %collective-permute-start.6 = (bf16[2,16,2048]{2,1,0:T(8,128)(2,1)S(1)}, bf16[2,16,2048]{2,1,0:T(8,128)(2,1)S(1)}, u32[]{:S(2)}, u32[]{:S(2)}) collective-permute-start(bf16[2,16,2048]{2,1,0:T(8,128)(2,1)S(1)} %pad_maximum_fusion.1.refs_2_), channel_id=1, source_target_pairs={{0,8},{1,9},{2,10},{3,11},{4,12},{5,13},{6,14},{7,15},{8,0},{9,1},... | collective-permute-start | bytes 393224 | tf_op jit(solution)/shard_map/ppermute | solution.py:48
  23.6 1.3 collective-permute-start.7
  24.9 1.7 collective-permute-done.5.refs_3_
  26.6 6.2 %collective-permute-done.6.refs_4_ = bf16[2,16,2048]{2,1,0:T(8,128)(2,1)S(1)} collective-permute-done((bf16[2,16,2048]{2,1,0:T(8,128)(2,1)S(1)}, bf16[2,16,2048]{2,1,0:T(8,128)(2,1)S(1)}, u32[]{:S(2)}, u32[]{:S(2)}) %collective-permute-start.6) | collective-permute-done | bytes 131104 | tf_op jit(solution)/shard_map/ppermute | solution.py:48
  32.8 0.5 collective-permute-start.10
  33.4 0.4 collective-permute-start.12
  33.8 1.3 collective-permute-done.10.refs_8_
  35.1 0.1 collective-permute-start.13
  35.2 0.2 collective-permute-done.12.refs_10_
  35.4 1.2 collective-permute-done.13.refs_11_
  36.6 1.2 place_rows.1.norm_ref
  37.8 1.7 copy-done.1
  39.5 8.1 %query_key.2 = bf16[16,8,16,256]{3,2,1,0:T(8,128)(2,1)} custom-call(bf16[256,6144]{1,0:T(8,128)(2,1)} %copy-done.1, bf16[16,128,768]{2,1,0:T(8,128)(2,1)} %fusion.choose_ref, bf16[8,3,48,6144]{3,2,1,0:T(8,128)(2,1)} %w_ref.5), custom_call_target="tpu_custom_call" | custom-call | flops 3221225472 | bytes 9437184 | tf_op jit(solution)/shard_map/query_key/pallas_call | solution.py:186
  47.6 4.2 %all-to-all-start = ((bf16[16,8,16,256]{3,2,1,0:T(8,128)(2,1)}), bf16[16,8,16,256]{3,2,1,0:T(8,128)(2,1)S(1)}, u32[]{:S(2)}, u32[]{:S(2)}) async-start(bf16[16,8,16,256]{3,2,1,0:T(8,128)(2,1)} %query_key.2), calls=%async_computation | async-start | bytes 2097152 | tf_op jit(solution)/shard_map/all_to_all | solution.py:518
  51.8 9.0 %value_rows.1.value_ref = bf16[8,256,384]{2,1,0:T(8,128)(2,1)} custom-call(bf16[256,6144]{1,0:T(8,128)(2,1)} %copy-done.1, bf16[16,128,768]{2,1,0:T(8,128)(2,1)} %fusion.choose_ref, bf16[8,3,48,6144]{3,2,1,0:T(8,128)(2,1)} %w_ref.5), custom_call_target="tpu_custom_call" | custom-call | flops 4831838208 | bytes 11010048 | tf_op jit(solution)/shard_map/value_rows/pallas_call | solution.py:236
  60.8 12.9 %query_key.3 = bf16[32,8,16,256]{3,2,1,0:T(8,128)(2,1)} custom-call(bf16[256,6144]{1,0:T(8,128)(2,1)} %copy-done.1, bf16[16,128,768]{2,1,0:T(8,128)(2,1)} %fusion.choose_ref, bf16[8,3,48,6144]{3,2,1,0:T(8,128)(2,1)} %w_ref.5), custom_call_target="tpu_custom_call" | custom-call | flops 6442450944 | bytes 12582912 | tf_op jit(solution)/shard_map/query_key/pallas_call | solution.py:186
  73.7 1.1 all-to-all-done.x_ref
  74.8 1.0 copy-done.4
  75.8 6.9 %all-to-all-start.1 = ((bf16[16,16,16,256]{3,2,1,0:T(8,128)(2,1)}), bf16[16,16,16,256]{3,2,1,0:T(8,128)(2,1)S(1)}, u32[]{:S(2)}, u32[]{:S(2)}) async-start(bf16[16,16,16,256]{3,2,1,0:T(8,128)(2,1)} %bitcast.50), calls=%async_computation.1 | async-start | bytes 4194304 | tf_op jit(solution)/shard_map/all_to_all | solution.py:518
  82.9 1.2 copy-done.5
  84.1 2.1 %key_weights.2 = f32[8,256]{1,0:T(8,128)S(1)} custom-call(bf16[16,8,16,256]{3,2,1,0:T(8,128)(2,1)S(1)} %copy-done.5, f32[128,1]{1,0:T(8,128)S(1)} %copy.29.query_gain_ref, f32[128,1]{1,0:T(8,128)S(1)} %copy.30.key_gain_ref), custom_call_target="tpu_custom_call" | custom-call | flops 134217728 | bytes 1048576 | tf_op jit(solution)/shard_map/key_weights/pallas_call | solution.py:378
  86.2 19.2 %hidden_part.2.pooled_ref = f32[8,768]{1,0:T(8,128)} custom-call(bf16[256,6144]{1,0:T(8,128)(2,1)} %copy-done.1, bf16[16,128,768]{2,1,0:T(8,128)(2,1)} %fusion.choose_ref, bf16[1536,6144]{1,0:T(8,128)(2,1)} %up_ref.3), custom_call_target="tpu_custom_call" | custom-call | flops 9663676416 | bytes 15728640 | tf_op jit(solution)/shard_map/hidden_part/pallas_call | solution.py:295
  105.4 5.7 %down_part.2 = f32[8,6144]{1,0:T(8,128)} custom-call(f32[8,768]{1,0:T(8,128)} %hidden_part.2.pooled_ref, bf16[1536,6144]{1,0:T(8,128)(2,1)} %down_ref.3), custom_call_target="tpu_custom_call" | custom-call | flops 150994944 | bytes 9437184 | tf_op jit(solution)/shard_map/down_part/pallas_call | solution.py:334
  111.1 19.2 %hidden_part.3.pooled_ref = f32[8,768]{1,0:T(8,128)} custom-call(bf16[256,6144]{1,0:T(8,128)(2,1)} %copy-done.1, bf16[16,128,768]{2,1,0:T(8,128)(2,1)} %fusion.choose_ref, bf16[1536,6144]{1,0:T(8,128)(2,1)} %up_ref.3), custom_call_target="tpu_custom_call" | custom-call | flops 9663676416 | bytes 15728640 | tf_op jit(solution)/shard_map/hidden_part/pallas_call | solution.py:295
  130.3 5.1 %key_weights.3 = f32[16,256]{1,0:T(8,128)S(1)} custom-call(bf16[16,16,16,256]{3,2,1,0:T(8,128)(2,1)S(1)} %all-to-all-done.1.x_ref, f32[128,1]{1,0:T(8,128)S(1)} %copy.29.query_gain_ref, f32[128,1]{1,0:T(8,128)S(1)} %copy.30.key_gain_ref), custom_call_target="tpu_custom_call" | custom-call | flops 268435456 | bytes 2097152 | tf_op jit(solution)/shard_map/key_weights/pallas_call | solution.py:378
  135.4 0.7 broadcast_in_dim.18
  136.1 6.0 %all-to-all-start.2 = ((bf16[16,24,256]{2,1,0:T(8,128)(2,1)}), bf16[16,24,256]{2,1,0:T(8,128)(2,1)S(1)}, u32[]{:S(2)}, u32[]{:S(2)}) async-start(bf16[16,24,256]{2,1,0:T(8,128)(2,1)} %broadcast_in_dim.18), calls=%async_computation.2 | async-start | bytes 393216 | tf_op jit(solution)/shard_map/all_to_all | solution.py:538
  142.1 5.8 %down_part.3 = f32[8,6144]{1,0:T(8,128)} custom-call(f32[8,768]{1,0:T(8,128)} %hidden_part.3.pooled_ref, bf16[1536,6144]{1,0:T(8,128)(2,1)} %down_ref.3), custom_call_target="tpu_custom_call" | custom-call | flops 150994944 | bytes 9437184 | tf_op jit(solution)/shard_map/down_part/pallas_call | solution.py:334
  147.9 0.9 add.128.hidden_ref
  148.9 2.2 %all-to-all-done.2.key_ref = bf16[16,24,256]{2,1,0:T(8,128)(2,1)S(1)} async-done(((bf16[16,24,256]{2,1,0:T(8,128)(2,1)}), bf16[16,24,256]{2,1,0:T(8,128)(2,1)S(1)}, u32[]{:S(2)}, u32[]{:S(2)}) %all-to-all-start.2) | async-done | bytes 196640 | tf_op jit(solution)/shard_map/all_to_all | solution.py:538
  151.1 2.3 %copy-done.3 = bf16[8,48,6144]{2,1,0:T(8,128)(2,1)S(1)} copy-done((bf16[8,48,6144]{2,1,0:T(8,128)(2,1)S(1)}, bf16[8,48,6144]{2,1,0:T(8,128)(2,1)}, u32[]{:S(2)}) %copy-start.3) | copy-done | bytes 4718616
  153.4 2.8 %feature_part.1 = f32[16,8,384]{2,1,0:T(8,128)} custom-call(bf16[16,24,256]{2,1,0:T(8,128)(2,1)S(1)} %all-to-all-done.2.key_ref, bf16[8,256,384]{2,1,0:T(8,128)(2,1)S(1)} %copy-done.2, bf16[384,6144]{1,0:T(8,128)(2,1)S(1)} %bitcast.45, f32[8,6144]{1,0:T(8,128)S(1)} %add.128.hidden_ref, bf16[16,6144]{1,0:T(8,128)(2,1)S(1)} %copy-done.7), custom_call_target="tpu_custom_call" | custom-call | flops 78643200 | bytes 6291456 | tf_op jit(solution)/shard_map/feature_part/pallas_call | solution.py:433
  156.3 3.8 %all-to-all-start.3 = ((f32[16,8,384]{2,1,0:T(8,128)}), f32[16,8,384]{2,1,0:T(8,128)S(1)}, u32[]{:S(2)}, u32[]{:S(2)}) async-start(f32[16,8,384]{2,1,0:T(8,128)} %feature_part.1), calls=%async_computation.3 | async-start | bytes 393216 | tf_op jit(solution)/shard_map/all_to_all | solution.py:550
  160.1 0.8 dynamic_slice.3
  160.9 0.7 fusion.45
  161.6 7.5 %all-to-all-done.3 = f32[16,8,384]{2,1,0:T(8,128)S(1)} async-done(((f32[16,8,384]{2,1,0:T(8,128)}), f32[16,8,384]{2,1,0:T(8,128)S(1)}, u32[]{:S(2)}, u32[]{:S(2)}) %all-to-all-start.3) | async-done | bytes 196640 | tf_op jit(solution)/shard_map/all_to_all | solution.py:550
  169.1 0.2 fusion.40
  169.3 0.2 multiply_reduce_fusion.1
  169.5 0.8 fusion.19
  170.5 1.2 collective-permute-done.14
  171.7 0.2 subtract_reduce_fusion.7
  172.1 4.3 %collective-permute-done.15 = f32[9,1002]{1,0:T(8,128)S(1)} collective-permute-done((f32[9,1002]{1,0:T(8,128)S(1)}, f32[9,1002]{1,0:T(8,128)S(1)}, u32[]{:S(2)}, u32[]{:S(2)}) %collective-permute-start.15) | collective-permute-done | bytes 36104 | tf_op jit(solution)/shard_map/ppermute | solution.py:48
  176.4 0.2 subtract_reduce_fusion.5
  176.7 0.1 collective-permute-start.16
  176.8 4.1 %collective-permute-done.16 = f32[9,1002]{1,0:T(8,128)S(1)} collective-permute-done((f32[9,1002]{1,0:T(8,128)S(1)}, f32[9,1002]{1,0:T(8,128)S(1)}, u32[]{:S(2)}, u32[]{:S(2)}) %collective-permute-start.16) | collective-permute-done | bytes 36104 | tf_op jit(solution)/shard_map/ppermute | solution.py:48
  181.0 0.2 subtract_reduce_fusion.3
  181.3 0.7 collective-permute-start.17
  182.1 4.7 %collective-permute-done.17 = f32[9,1002]{1,0:T(8,128)S(1)} collective-permute-done((f32[9,1002]{1,0:T(8,128)S(1)}, f32[9,1002]{1,0:T(8,128)S(1)}, u32[]{:S(2)}, u32[]{:S(2)}) %collective-permute-start.17) | collective-permute-done | bytes 36104 | tf_op jit(solution)/shard_map/ppermute | solution.py:48
  186.8 0.2 subtract_reduce_fusion.1
  187.0 0.7 fusion.18
  187.7 0.2 exponential_reduce_fusion
  187.9 0.2 multiply_reduce_fusion
  188.1 0.6 fusion.25
  189.4 0.6 subtract_reduce_fusion.8
  (62 shorter events, 1.5 us)
Async XLA Ops:
  0.6 160.3 %copy-start = (bf16[384,1000]{0,1:T(8,128)(2,1)S(1)}, bf16[384,1000]{0,1:T(8,128)(2,1)}, u32[]{:S(2)}) copy-start(bf16[384,1000]{0,1:T(8,128)(2,1)} %param.21) | copy-start | bytes 2304004
  0.6 1.0 copy-start.6
  1.6 0.7 copy-start.8
  2.7 11.7 %collective-permute-start.2 = (bf16[16,4096]{1,0:T(8,128)(2,1)S(1)}, bf16[16,4096]{1,0:T(8,128)(2,1)S(1)}, u32[]{:S(2)}, u32[]{:S(2)}) collective-permute-start(bf16[16,4096]{1,0:T(8,128)(2,1)S(1)} %get-tuple-element.19), channel_id=1, source_target_pairs={{0,12},{1,13},{2,14},{3,15},{4,8},{5,9},{6,10},{7,11},{8,4},{9,5},... | collective-permute-start | bytes 393224 | tf_op jit(solution)/shard_map/ppermute | solution.py:48
  7.8 11.1 %collective-permute-start.1 = (bf16[16,4096]{1,0:T(8,128)(2,1)S(1)}, bf16[16,4096]{1,0:T(8,128)(2,1)S(1)}, u32[]{:S(2)}, u32[]{:S(2)}) collective-permute-start(bf16[16,4096]{1,0:T(8,128)(2,1)S(1)} %get-tuple-element.19), channel_id=1, source_target_pairs={{0,8},{1,9},{2,10},{3,11},{4,12},{5,13},{6,14},{7,15},{8,0},{9,1},... | collective-permute-start | bytes 393224 | tf_op jit(solution)/shard_map/ppermute | solution.py:48
  7.8 11.1 %collective-permute-start = (bf16[16,4096]{1,0:T(8,128)(2,1)S(1)}, bf16[16,4096]{1,0:T(8,128)(2,1)S(1)}, u32[]{:S(2)}, u32[]{:S(2)}) collective-permute-start(bf16[16,4096]{1,0:T(8,128)(2,1)S(1)} %get-tuple-element.19), channel_id=1, source_target_pairs={{0,4},{1,5},{2,6},{3,7},{4,0},{5,1},{6,2},{7,3},{8,12},{9,13},{10,... | collective-permute-start | bytes 393224 | tf_op jit(solution)/shard_map/ppermute | solution.py:48
  8.5 5.9 %collective-permute-start.3 = (bf16[16,2048]{1,0:T(8,128)(2,1)S(1)}, bf16[16,2048]{1,0:T(8,128)(2,1)S(1)}, u32[]{:S(2)}, u32[]{:S(2)}) collective-permute-start(bf16[16,2048]{1,0:T(8,128)(2,1)S(1)} %get-tuple-element.20), channel_id=1, source_target_pairs={{0,2},{1,3},{2,0},{3,1},{4,6},{5,7},{6,4},{7,5},{8,10},{9,11},{10,... | collective-permute-start | bytes 196616 | tf_op jit(solution)/shard_map/ppermute | solution.py:48
  19.0 13.8 %collective-permute-start.4 = (bf16[4,16,4096]{2,1,0:T(8,128)(2,1)S(1)}, bf16[4,16,4096]{2,1,0:T(8,128)(2,1)S(1)}, u32[]{:S(2)}, u32[]{:S(2)}) collective-permute-start(bf16[4,16,4096]{2,1,0:T(8,128)(2,1)S(1)} %pad_maximum_fusion.refs_0_), channel_id=1, source_target_pairs={{0,2},{1,3},{2,0},{3,1},{4,6},{5,7},{6,4},{7,5},{8,10},{9,11},{10,... | collective-permute-start | bytes 1572872 | tf_op jit(solution)/shard_map/ppermute | solution.py:48
  20.5 6.1 %collective-permute-start.5 = (bf16[2,16,2048]{2,1,0:T(8,128)(2,1)S(1)}, bf16[2,16,2048]{2,1,0:T(8,128)(2,1)S(1)}, u32[]{:S(2)}, u32[]{:S(2)}) collective-permute-start(bf16[2,16,2048]{2,1,0:T(8,128)(2,1)S(1)} %pad_maximum_fusion.1.refs_2_), channel_id=1, source_target_pairs={{0,4},{1,5},{2,6},{3,7},{4,0},{5,1},{6,2},{7,3},{8,12},{9,13},{10,... | collective-permute-start | bytes 393224 | tf_op jit(solution)/shard_map/ppermute | solution.py:48
  20.6 12.2 %collective-permute-start.6 = (bf16[2,16,2048]{2,1,0:T(8,128)(2,1)S(1)}, bf16[2,16,2048]{2,1,0:T(8,128)(2,1)S(1)}, u32[]{:S(2)}, u32[]{:S(2)}) collective-permute-start(bf16[2,16,2048]{2,1,0:T(8,128)(2,1)S(1)} %pad_maximum_fusion.1.refs_2_), channel_id=1, source_target_pairs={{0,8},{1,9},{2,10},{3,11},{4,12},{5,13},{6,14},{7,15},{8,0},{9,1},... | collective-permute-start | bytes 393224 | tf_op jit(solution)/shard_map/ppermute | solution.py:48
  23.6 9.2 %collective-permute-start.7 = (bf16[2,16,2048]{2,1,0:T(8,128)(2,1)S(1)}, bf16[2,16,2048]{2,1,0:T(8,128)(2,1)S(1)}, u32[]{:S(2)}, u32[]{:S(2)}) collective-permute-start(bf16[2,16,2048]{2,1,0:T(8,128)(2,1)S(1)} %pad_maximum_fusion.1.refs_2_), channel_id=1, source_target_pairs={{0,12},{1,13},{2,14},{3,15},{4,8},{5,9},{6,10},{7,11},{8,4},{9,5},... | collective-permute-start | bytes 393224 | tf_op jit(solution)/shard_map/ppermute | solution.py:48
  24.9 10.3 %collective-permute-start.8 = (bf16[4,16,4096]{2,1,0:T(8,128)(2,1)S(1)}, bf16[4,16,4096]{2,1,0:T(8,128)(2,1)S(1)}, u32[]{:S(2)}, u32[]{:S(2)}) collective-permute-start(bf16[4,16,4096]{2,1,0:T(8,128)(2,1)S(1)} %pad_maximum_fusion.refs_0_), channel_id=1, source_target_pairs={{0,1},{1,0},{2,3},{3,2},{4,5},{5,4},{6,7},{7,6},{8,9},{9,8},{10,11... | collective-permute-start | bytes 1572872 | tf_op jit(solution)/shard_map/ppermute | solution.py:48
  32.8 3.8 %collective-permute-start.9 = (bf16[4,16,4096]{2,1,0:T(8,128)(2,1)S(1)}, bf16[4,16,4096]{2,1,0:T(8,128)(2,1)S(1)}, u32[]{:S(2)}, u32[]{:S(2)}) collective-permute-start(bf16[4,16,4096]{2,1,0:T(8,128)(2,1)S(1)} %collective-permute-done.4.refs_1_), channel_id=1, source_target_pairs={{0,1},{1,0},{2,3},{3,2},{4,5},{5,4},{6,7},{7,6},{8,9},{9,8},{10,11... | collective-permute-start | bytes 1572872 | tf_op jit(solution)/shard_map/ppermute | solution.py:48
  32.8 2.3 %collective-permute-start.10 = (bf16[2,16,2048]{2,1,0:T(8,128)(2,1)S(1)}, bf16[2,16,2048]{2,1,0:T(8,128)(2,1)S(1)}, u32[]{:S(2)}, u32[]{:S(2)}) collective-permute-start(bf16[2,16,2048]{2,1,0:T(8,128)(2,1)S(1)} %pad_maximum_fusion.1.refs_2_), channel_id=1, source_target_pairs={{0,1},{1,0},{2,3},{3,2},{4,5},{5,4},{6,7},{7,6},{8,9},{9,8},{10,11... | collective-permute-start | bytes 393224 | tf_op jit(solution)/shard_map/ppermute | solution.py:48
  33.3 1.9 %collective-permute-start.11 = (bf16[2,16,2048]{2,1,0:T(8,128)(2,1)S(1)}, bf16[2,16,2048]{2,1,0:T(8,128)(2,1)}, u32[]{:S(2)}, u32[]{:S(2)}) collective-permute-start(bf16[2,16,2048]{2,1,0:T(8,128)(2,1)S(1)} %collective-permute-done.5.refs_3_), channel_id=1, source_target_pairs={{0,1},{1,0},{2,3},{3,2},{4,5},{5,4},{6,7},{7,6},{8,9},{9,8},{10,11... | collective-permute-start | bytes 393224 | tf_op jit(solution)/shard_map/ppermute | solution.py:48
  33.4 2.0 %collective-permute-start.12 = (bf16[2,16,2048]{2,1,0:T(8,128)(2,1)S(1)}, bf16[2,16,2048]{2,1,0:T(8,128)(2,1)}, u32[]{:S(2)}, u32[]{:S(2)}) collective-permute-start(bf16[2,16,2048]{2,1,0:T(8,128)(2,1)S(1)} %collective-permute-done.6.refs_4_), channel_id=1, source_target_pairs={{0,1},{1,0},{2,3},{3,2},{4,5},{5,4},{6,7},{7,6},{8,9},{9,8},{10,11... | collective-permute-start | bytes 393224 | tf_op jit(solution)/shard_map/ppermute | solution.py:48
  35.1 1.5 collective-permute-start.13
  37.8 1.7 copy-start.1
  47.6 27.1 %all-to-all-start = ((bf16[16,8,16,256]{3,2,1,0:T(8,128)(2,1)}), bf16[16,8,16,256]{3,2,1,0:T(8,128)(2,1)S(1)}, u32[]{:S(2)}, u32[]{:S(2)}) async-start(bf16[16,8,16,256]{3,2,1,0:T(8,128)(2,1)} %query_key.2), calls=%async_computation | async-start | bytes 2097152 | tf_op jit(solution)/shard_map/all_to_all | solution.py:518
  60.8 21.9 %copy-start.10 = (f32[128]{0:T(128)S(1)}, f32[128]{0:T(128)}, u32[]{:S(2)}) copy-start(f32[128]{0:T(128)} %param.16) | copy-start | bytes 1540
  60.8 22.0 %copy-start.11 = (f32[128]{0:T(128)S(1)}, f32[128]{0:T(128)}, u32[]{:S(2)}) copy-start(f32[128]{0:T(128)} %param.17) | copy-start | bytes 1540
  74.8 1.0 copy-start.4
  75.8 54.5 %all-to-all-start.1 = ((bf16[16,16,16,256]{3,2,1,0:T(8,128)(2,1)}), bf16[16,16,16,256]{3,2,1,0:T(8,128)(2,1)S(1)}, u32[]{:S(2)}, u32[]{:S(2)}) async-start(bf16[16,16,16,256]{3,2,1,0:T(8,128)(2,1)} %bitcast.50), calls=%async_computation.1 | async-start | bytes 4194304 | tf_op jit(solution)/shard_map/all_to_all | solution.py:518
  82.9 1.2 copy-start.5
  136.1 15.0 %all-to-all-start.2 = ((bf16[16,24,256]{2,1,0:T(8,128)(2,1)}), bf16[16,24,256]{2,1,0:T(8,128)(2,1)S(1)}, u32[]{:S(2)}, u32[]{:S(2)}) async-start(bf16[16,24,256]{2,1,0:T(8,128)(2,1)} %broadcast_in_dim.18), calls=%async_computation.2 | async-start | bytes 393216 | tf_op jit(solution)/shard_map/all_to_all | solution.py:538
  142.1 5.8 %copy-start.9 = (f32[8,6144]{1,0:T(8,128)S(1)}, f32[8,6144]{1,0:T(8,128)}, u32[]{:S(2)}) copy-start(f32[8,6144]{1,0:T(8,128)} %down_part.2) | copy-start | bytes 589828
  142.1 9.0 %copy-start.2 = (bf16[8,256,384]{2,1,0:T(8,128)(2,1)S(1)}, bf16[8,256,384]{2,1,0:T(8,128)(2,1)}, u32[]{:S(2)}) copy-start(bf16[8,256,384]{2,1,0:T(8,128)(2,1)} %value_rows.1.value_ref) | copy-start | bytes 4718596
  142.1 9.0 %copy-start.7 = (bf16[16,6144]{1,0:T(8,128)(2,1)S(1)}, bf16[16,6144]{1,0:T(8,128)(2,1)}, u32[]{:S(2)}) copy-start(bf16[16,6144]{1,0:T(8,128)(2,1)} %token_ref.1) | copy-start | bytes 589828
  151.1 2.3 %copy-start.3 = (bf16[8,48,6144]{2,1,0:T(8,128)(2,1)S(1)}, bf16[8,48,6144]{2,1,0:T(8,128)(2,1)}, u32[]{:S(2)}) copy-start(bf16[8,48,6144]{2,1,0:T(8,128)(2,1)} %param.18) | copy-start | bytes 14155780
  156.3 12.8 %all-to-all-start.3 = ((f32[16,8,384]{2,1,0:T(8,128)}), f32[16,8,384]{2,1,0:T(8,128)S(1)}, u32[]{:S(2)}, u32[]{:S(2)}) async-start(f32[16,8,384]{2,1,0:T(8,128)} %feature_part.1), calls=%async_computation.3 | async-start | bytes 393216 | tf_op jit(solution)/shard_map/all_to_all | solution.py:550
  170.5 1.3 collective-permute-start.14
  172.1 4.3 %collective-permute-start.15 = (f32[9,1002]{1,0:T(8,128)S(1)}, f32[9,1002]{1,0:T(8,128)S(1)}, u32[]{:S(2)}, u32[]{:S(2)}) collective-permute-start(f32[9,1002]{1,0:T(8,128)S(1)} %select_maximum_fusion.2), channel_id=1, source_target_pairs={{0,2},{1,3},{2,0},{3,1},{4,6},{5,7},{6,4},{7,5},{8,10},{9,11},{10,... | collective-permute-start | bytes 108224 | tf_op jit(solution)/shard_map/ppermute | solution.py:48
  176.7 4.3 %collective-permute-start.16 = (f32[9,1002]{1,0:T(8,128)S(1)}, f32[9,1002]{1,0:T(8,128)S(1)}, u32[]{:S(2)}, u32[]{:S(2)}) collective-permute-start(f32[9,1002]{1,0:T(8,128)S(1)} %select_maximum_fusion.1), channel_id=1, source_target_pairs={{0,4},{1,5},{2,6},{3,7},{4,0},{5,1},{6,2},{7,3},{8,12},{9,13},{10,... | collective-permute-start | bytes 108224 | tf_op jit(solution)/shard_map/ppermute | solution.py:48
  181.3 5.4 %collective-permute-start.17 = (f32[9,1002]{1,0:T(8,128)S(1)}, f32[9,1002]{1,0:T(8,128)S(1)}, u32[]{:S(2)}, u32[]{:S(2)}) collective-permute-start(f32[9,1002]{1,0:T(8,128)S(1)} %select_maximum_fusion), channel_id=1, source_target_pairs={{0,8},{1,9},{2,10},{3,11},{4,12},{5,13},{6,14},{7,15},{8,0},{9,1},... | collective-permute-start | bytes 108224 | tf_op jit(solution)/shard_map/ppermute | solution.py:48

commit v2 on v1

--- a/solution.py
+++ b/solution.py
@@ -64,7 +64,7 @@
             jax.ShapeDtypeStruct((rows, cut), BF16),
             jax.ShapeDtypeStruct((rows, width - cut), BF16),
         ),
-        compiler_params=pltpu.CompilerParams(vmem_limit_bytes=8 * MIB),
+        compiler_params=pltpu.CompilerParams(vmem_limit_bytes=60 * MIB),
         name="own_norm",
     )(tokens, gain.reshape(1, width))
 
@@ -109,7 +109,7 @@
         in_specs=[pl.BlockSpec(memory_space=pltpu.SMEM)]
         + [pl.BlockSpec(memory_space=pltpu.VMEM)] * len(pieces),
         out_specs=pl.BlockSpec(memory_space=pltpu.VMEM),
-        compiler_params=pltpu.CompilerParams(vmem_limit_bytes=16 * MIB),
+        compiler_params=pltpu.CompilerParams(vmem_limit_bytes=50 * MIB),
         name="place_rows",
     )(me.reshape(1), *[array for _, _, array in pieces])
 
@@ -198,7 +198,7 @@
             pltpu.VMEM((samples, rows, columns), F32),
             pltpu.VMEM((samples * rows // 128, columns, 128), F32),
         ],
-        compiler_params=pltpu.CompilerParams(vmem_limit_bytes=54 * MIB),
+        compiler_params=pltpu.CompilerParams(vmem_limit_bytes=50 * MIB),
         cost_estimate=pl.CostEstimate(
             flops=8 * rows * width * columns,
             bytes_accessed=2 * (norm.size + choose.size + columns * width),
@@ -244,7 +244,7 @@
         ],
         out_specs=pl.BlockSpec((samples, rows, columns), lambda k: (0, 0, 0)),
         scratch_shapes=[pltpu.VMEM((width // BLOCK, rows, columns), BF16)],
-        compiler_params=pltpu.CompilerParams(vmem_limit_bytes=54 * MIB),
+        compiler_params=pltpu.CompilerParams(vmem_limit_bytes=50 * MIB),
         cost_estimate=pl.CostEstimate(
             flops=8 * rows * width * columns,
             bytes_accessed=2 * (norm.size + choose.size + columns * width),
@@ -303,7 +303,7 @@
         ],
         out_specs=pl.BlockSpec((samples, UNITS), lambda i, k: (0, i)),
         scratch_shapes=[pltpu.VMEM((width // BLOCK, rows, UNITS), BF16)],
-        compiler_params=pltpu.CompilerParams(vmem_limit_bytes=54 * MIB),
+        compiler_params=pltpu.CompilerParams(vmem_limit_bytes=50 * MIB),
         cost_estimate=pl.CostEstimate(
             flops=8 * rows * width * UNITS * tiles,
             bytes_accessed=2 * (norm.size + choose.size + UNITS * tiles * width),
@@ -340,7 +340,7 @@
             pl.BlockSpec((UNITS, width), lambda i: (first + i, 0)),
         ],
         out_specs=pl.BlockSpec((samples, width), lambda i: (0, 0)),
-        compiler_params=pltpu.CompilerParams(vmem_limit_bytes=54 * MIB),
+        compiler_params=pltpu.CompilerParams(vmem_limit_bytes=50 * MIB),
         cost_estimate=pl.CostEstimate(
             flops=32 * units * width, bytes_accessed=2 * units * width, transcendentals=0
         ),
@@ -378,7 +378,7 @@
     return pl.pallas_call(
         functools.partial(attention_kernel, items),
         out_shape=jax.ShapeDtypeStruct((items, rows), F32),
-        compiler_params=pltpu.CompilerParams(vmem_limit_bytes=16 * MIB),
+        compiler_params=pltpu.CompilerParams(vmem_limit_bytes=50 * MIB),
         cost_estimate=pl.CostEstimate(
             flops=2 * items * rows * rows * head_dim,
             bytes_accessed=2 * exchanged.size,
@@ -443,7 +443,7 @@
         ],
         out_specs=pl.BlockSpec((parts // steps, samples, width // parts), lambda i: (i, 0, 0)),
         scratch_shapes=[pltpu.VMEM((16, columns), BF16)],
-        compiler_params=pltpu.CompilerParams(vmem_limit_bytes=16 * MIB),
+        compiler_params=pltpu.CompilerParams(vmem_limit_bytes=40 * MIB),
         cost_estimate=pl.CostEstimate(
             flops=2 * samples * rows * columns * 2 + 32 * columns * width,
             bytes_accessed=2 * columns * width + 2 * value.size,
@@ -453,7 +453,44 @@
     )(key_mean, value, w_proj, hidden, tokens)
 
 
-def pooled_logits(feature, final_gain, w_head):
+def joined(mine, other, columns):
+    classes = mine.shape[1] - 2
+    samples = mine.shape[0] - 1
+    mean, other_mean = (x[:samples, classes : classes + 1] for x in (mine, other))
+    joint = 0.5 * (mean + other_mean)
+    logits = (
+        mine[:samples, :classes]
+        + other[:samples, :classes]
+        + (mean - joint) * mine[samples:, :classes]
+        + (other_mean - joint) * other[samples:, :classes]
+    )
+    gap = mean - other_mean
+    spread = mine[:samples, classes + 1 :] + other[:samples, classes + 1 :]
+    spread = spread + gap * gap * (0.5 * columns)
+    return logits, joint, spread, mine[samples:, :classes] + other[samples:, :classes]
+
+
+def packed(logits, mean, spread, gain_head):
+    rows = jnp.concatenate([logits, mean, spread], axis=1)
+    return jnp.concatenate([rows, jnp.pad(gain_head, ((0, 0), (0, 2)))], axis=0)
+
+
+def finish_kernel(columns, mine_ref, other_ref, feature_ref, gain_ref, out_ref, bald_ref):
+    logits, mean, spread, _ = joined(mine_ref[...], other_ref[...], columns)
+    scale = lax.rsqrt(spread / (2 * columns) + 1e-06)
+    out_ref[...] = (feature_ref[...] - mean) * scale * gain_ref[...]
+    logits = soft_cap * jnp.tanh(logits * scale / soft_cap)
+    samples = logits.shape[0]
+    exp_logits = jnp.exp(logits)
+    totals = jnp.sum(exp_logits, axis=1, keepdims=True)
+    probs = exp_logits / totals
+    entropy = jnp.log(totals) - jnp.sum(probs * logits, axis=1, keepdims=True)
+    mean_probs = jnp.sum(probs, axis=0, keepdims=True) * (1.0 / samples)
+    whole = -jnp.sum(mean_probs * jnp.log(mean_probs), axis=1, keepdims=True)
+    bald_ref[...] = whole - jnp.sum(entropy, axis=0, keepdims=True) * (1.0 / samples)
+
+
+def finished(feature, final_gain, w_head):
     highest = lax.Precision.HIGHEST
     gain_head = jnp.dot(final_gain[None], w_head.astype(F32), precision=highest)
     mean = jnp.mean(feature, axis=-1, keepdims=True)
@@ -461,33 +498,22 @@
     spread = jnp.sum(centered * centered, axis=-1, keepdims=True)
     logits = jnp.dot(centered * final_gain, w_head.astype(F32), precision=highest)
     columns = feature.shape[1]
-    samples, classes = logits.shape
+    mine = packed(logits, mean, spread, gain_head)
     bits = 1
-    while bits < lax.axis_size("inp"):
-        sent = jnp.concatenate(
-            [
-                jnp.concatenate([logits, mean, spread], axis=1),
-                jnp.pad(gain_head, ((0, 0), (0, 2))),
-            ],
-            axis=0,
-        )
-        other = permuted(sent, bits)
-        other_mean = other[:samples, classes : classes + 1]
-        joint = 0.5 * (mean + other_mean)
-        logits = (
-            logits
-            + other[:samples, :classes]
-            + (mean - joint) * gain_head
-            + (other_mean - joint) * other[samples:, :classes]
-        )
-        gap = mean - other_mean
-        spread = spread + other[:samples, classes + 1 :] + gap * gap * (0.5 * columns)
-        gain_head = gain_head + other[samples:, :classes]
-        mean = joint
+    while 2 * bits < lax.axis_size("inp"):
+        mine = packed(*joined(mine, permuted(mine, bits), columns))
         columns = 2 * columns
         bits = 2 * bits
-    scale = lax.rsqrt(spread / columns + 1e-06)
-    return mean, scale, logits * scale
+    embedding, score = pl.pallas_call(
+        functools.partial(finish_kernel, columns),
+        out_shape=(
+            jax.ShapeDtypeStruct(feature.shape, F32),
+            jax.ShapeDtypeStruct((1, 1), F32),
+        ),
+        compiler_params=pltpu.CompilerParams(vmem_limit_bytes=16 * MIB),
+        name="finish",
+    )(mine, permuted(mine, bits), feature, final_gain[None])
+    return embedding[None], score.reshape(1)
 
 
 def pipelined(
@@ -550,10 +576,7 @@
         lax.all_to_all(partial_feature, "inp", split_axis=0, concat_axis=0, tiled=True), axis=0
     )
     gain = lax.dynamic_slice_in_dim(final_gain, me * slice_width, slice_width, 0)
-    mean, scale, raw_logits = pooled_logits(feature, gain, w_head)
-    embedding = (feature - mean) * scale * gain
-    logits = soft_cap * jnp.tanh(raw_logits / soft_cap)
-    return (embedding[None], bald_score(logits[None]))
+    return finished(feature, gain, w_head)
 
 
 def local(

time: 193 us -> 187 us (0.969)
  other arithmetic: 5.27 us -> 1.8 us
  Pallas kernels: 91.4 us -> 88.9 us
  between operations: 3.36 us -> 0.98 us
    pallas_call x2, Pallas kernels: 38.4 us -> 35.4 us  [hidden_part(): pl.pallas_call(hidden_kernel, grid=(tiles, width // depth), out_shape=jax...]
    unnamed x25 -> x29, local copies, waits for them, and re-layouts: 9.35 us -> 10.3 us
  transfers between devices with their start and end apart: 22 -> 22, of which waited for: 13 -> 13; matrix products, arithmetic and copies ran while one was open for 4% -> 3% of each run, Pallas kernels for 38% -> 36%
where the time goes in v2:
time: 187 us; the launch traced here: 186 us
  Pallas kernels  88.9 us (48%)
  waiting for transfers between devices  41.8 us (22%)
  starting transfers between devices  35.9 us (19%)
  local copies, waits for them, and re-layouts  12.2 us (7%)
  matrix products  4.14 us (2%)
    pallas_call x2, Pallas kernels, hidden_part(): pl.pallas_call(hidden_kernel, grid=(tiles, width // depth), out_shape=jax...  35.4 us
    ppermute x18, waiting for transfers between devices, permuted(): return lax.ppermute(array, 'inp', [(i, i ^ bits) for i in range(count)])  29.5 us
    pallas_call x2, Pallas kernels, query_key(): pl.pallas_call(query_key_kernel, grid=(width // depth,), out_shape=jax.Sh...  19.7 us
    ppermute x18, starting transfers between devices, permuted(): return lax.ppermute(array, 'inp', [(i, i ^ bits) for i in range(count)])  15.2 us
    all_to_all x2, starting transfers between devices, exchange(): return lax.all_to_all(array, 'inp', split_axis=0, concat_axis=0, tiled=True)  11.1 us
    pallas_call x2, Pallas kernels, down_part(): pl.pallas_call(down_kernel, grid=(units // UNITS,), out_shape=jax.ShapeDt...  10.4 us
    unnamed x29, local copies, waits for them, and re-layouts  10.3 us
    pallas_call x1, Pallas kernels, values_of(): pl.pallas_call(value_kernel, grid=(width // depth,), out_shape=jax.ShapeD...  7.74 us
  transfers between devices with their start and end apart: 22, of which 13 were waited for; matrix products, arithmetic and copies ran while one was open for 3% of the time, Pallas kernels for 36%

profile of v2, /device:TPU:0, one launch (start us, length us, event | category | flops | bytes accessed | tf_op | source)
XLA Modules:
  0.0 185.8 jit_solution(5490168405108434990)
XLA Ops:
  0.6 2.0 %own_norm.1 = (bf16[16,4096]{1,0:T(8,128)(2,1)}, bf16[16,2048]{1,0:T(8,128)(2,1)}) custom-call(bf16[16,6144]{1,0:T(8,128)(2,1)} %token_ref.1, f32[1,6144]{1,0:T(1,128)} %bitcast.51), custom_call_target="tpu_custom_call" | custom-call | tf_op jit(solution)/shard_map/own_norm/pallas_call | solution.py:61
  2.6 5.0 %collective-permute-start.2 = (bf16[16,4096]{1,0:T(8,128)(2,1)}, bf16[16,4096]{1,0:T(8,128)(2,1)S(1)}, u32[]{:S(2)}, u32[]{:S(2)}) collective-permute-start(bf16[16,4096]{1,0:T(8,128)(2,1)} %get-tuple-element.21), channel_id=1, source_target_pairs={{0,12},{1,13},{2,14},{3,15},{4,8},{5,9},{6,10},{7,11},{8,4},{9,5},... | collective-permute-start | bytes 393224 | tf_op jit(solution)/shard_map/ppermute | solution.py:48
  7.7 0.6 collective-permute-start
  8.3 1.7 collective-permute-start.3
  10.0 1.3 copy.25
  11.5 0.1 broadcast_compare_fusion
  11.6 2.6 %fusion.choose_ref = bf16[16,128,768]{2,1,0:T(8,128)(2,1)} fusion(pred[128,768]{1,0:T(8,128)(4,1)S(1)} %broadcast_compare_fusion, bf16[16,128,48]{2,1,0:T(8,128)(2,1)S(1)} %bitcast.41, s32[768]{0:T(1024)S(1)} %add_select_fusion), kind=kOutput, calls=%fused_computation.1 | convolution fusion | flops 155750400 | bytes 3443712 | tf_op jit(solution)/shard_map/trb,bc->trc/dot_general | solution.py:130
  14.3 4.7 %collective-permute-done.1 = bf16[16,4096]{1,0:T(8,128)(2,1)S(1)} collective-permute-done((bf16[16,4096]{1,0:T(8,128)(2,1)}, bf16[16,4096]{1,0:T(8,128)(2,1)S(1)}, u32[]{:S(2)}, u32[]{:S(2)}) %collective-permute-start.1) | collective-permute-done | bytes 131104 | tf_op jit(solution)/shard_map/ppermute | solution.py:48
  19.0 1.6 collective-permute-start.4
  20.6 3.0 %collective-permute-start.6 = (bf16[2,16,2048]{2,1,0:T(8,128)(2,1)S(1)}, bf16[2,16,2048]{2,1,0:T(8,128)(2,1)S(1)}, u32[]{:S(2)}, u32[]{:S(2)}) collective-permute-start(bf16[2,16,2048]{2,1,0:T(8,128)(2,1)S(1)} %pad_maximum_fusion.1.refs_2_), channel_id=1, source_target_pairs={{0,8},{1,9},{2,10},{3,11},{4,12},{5,13},{6,14},{7,15},{8,0},{9,1},... | collective-permute-start | bytes 393224 | tf_op jit(solution)/shard_map/ppermute | solution.py:48
  23.7 1.3 collective-permute-start.7
  25.0 1.6 collective-permute-done.5.refs_3_
  26.6 6.3 %collective-permute-done.6.refs_4_ = bf16[2,16,2048]{2,1,0:T(8,128)(2,1)S(1)} collective-permute-done((bf16[2,16,2048]{2,1,0:T(8,128)(2,1)S(1)}, bf16[2,16,2048]{2,1,0:T(8,128)(2,1)S(1)}, u32[]{:S(2)}, u32[]{:S(2)}) %collective-permute-start.6) | collective-permute-done | bytes 131104 | tf_op jit(solution)/shard_map/ppermute | solution.py:48
  32.8 0.5 collective-permute-start.10
  33.4 0.4 collective-permute-start.12
  33.9 1.3 collective-permute-done.10.refs_8_
  35.1 0.1 collective-permute-start.13
  35.3 0.2 collective-permute-done.12.refs_10_
  35.4 1.2 collective-permute-done.13.refs_11_
  36.6 2.9 %place_rows.1.norm_ref = bf16[256,6144]{1,0:T(8,128)(2,1)} custom-call(s32[1]{0:T(128)} %bitcast.me_ref, bf16[4,16,4096]{2,1,0:T(8,128)(2,1)S(1)} %pad_maximum_fusion.refs_0_, bf16[4,16,4096]{2,1,0:T(8,128)(2,1)S(1)} %collective-permute-done.4.refs_1_, bf16[2,16,2048]{2,1,0:T(8,128)(2,1)S(1)} %pad_maximum_fusion.1.refs_2_, ...), custom_call_target="tpu_custom_call" | custom-call | tf_op jit(solution)/shard_map/place_rows/pallas_call | solution.py:106
  39.5 8.1 %query_key.2 = bf16[16,8,16,256]{3,2,1,0:T(8,128)(2,1)} custom-call(bf16[256,6144]{1,0:T(8,128)(2,1)} %place_rows.1.norm_ref, bf16[16,128,768]{2,1,0:T(8,128)(2,1)} %fusion.choose_ref, bf16[8,3,48,6144]{3,2,1,0:T(8,128)(2,1)} %w_ref.5), custom_call_target="tpu_custom_call" | custom-call | flops 3221225472 | bytes 9437184 | tf_op jit(solution)/shard_map/query_key/pallas_call | solution.py:186
  47.6 4.2 %all-to-all-start = ((bf16[16,8,16,256]{3,2,1,0:T(8,128)(2,1)}), bf16[16,8,16,256]{3,2,1,0:T(8,128)(2,1)S(1)}, u32[]{:S(2)}, u32[]{:S(2)}) async-start(bf16[16,8,16,256]{3,2,1,0:T(8,128)(2,1)} %query_key.2), calls=%async_computation | async-start | bytes 2097152 | tf_op jit(solution)/shard_map/all_to_all | solution.py:544
  51.8 7.7 %value_rows.1.value_ref = bf16[8,256,384]{2,1,0:T(8,128)(2,1)S(1)} custom-call(bf16[256,6144]{1,0:T(8,128)(2,1)} %place_rows.1.norm_ref, bf16[16,128,768]{2,1,0:T(8,128)(2,1)} %fusion.choose_ref, bf16[8,3,48,6144]{3,2,1,0:T(8,128)(2,1)} %w_ref.5), custom_call_target="tpu_custom_call" | custom-call | flops 4831838208 | bytes 11010048 | tf_op jit(solution)/shard_map/value_rows/pallas_call | solution.py:236
  59.6 1.2 copy-done.3
  60.7 11.6 %query_key.3 = bf16[32,8,16,256]{3,2,1,0:T(8,128)(2,1)S(1)} custom-call(bf16[256,6144]{1,0:T(8,128)(2,1)} %place_rows.1.norm_ref, bf16[16,128,768]{2,1,0:T(8,128)(2,1)} %fusion.choose_ref, bf16[8,3,48,6144]{3,2,1,0:T(8,128)(2,1)} %w_ref.5), custom_call_target="tpu_custom_call" | custom-call | flops 6442450944 | bytes 12582912 | tf_op jit(solution)/shard_map/query_key/pallas_call | solution.py:186
  72.3 1.4 copy-done.8
  73.7 1.0 all-to-all-done.x_ref
  74.7 1.0 copy-done.6
  75.7 6.9 %all-to-all-start.1 = ((bf16[16,16,16,256]{3,2,1,0:T(8,128)(2,1)}), bf16[16,16,16,256]{3,2,1,0:T(8,128)(2,1)S(1)}, u32[]{:S(2)}, u32[]{:S(2)}) async-start(bf16[16,16,16,256]{3,2,1,0:T(8,128)(2,1)} %bitcast.39), calls=%async_computation.1 | async-start | bytes 4194304 | tf_op jit(solution)/shard_map/all_to_all | solution.py:544
  82.6 0.1 copy.29.query_gain_ref
  82.7 0.1 copy.30.key_gain_ref
  82.8 1.2 copy-done.7
  84.0 2.1 %key_weights.2 = f32[8,256]{1,0:T(8,128)S(1)} custom-call(bf16[16,8,16,256]{3,2,1,0:T(8,128)(2,1)S(1)} %copy-done.7, f32[128,1]{1,0:T(8,128)S(1)} %copy.29.query_gain_ref, f32[128,1]{1,0:T(8,128)S(1)} %copy.30.key_gain_ref), custom_call_target="tpu_custom_call" | custom-call | flops 134217728 | bytes 1048576 | tf_op jit(solution)/shard_map/key_weights/pallas_call | solution.py:378
  86.1 1.9 %copy-done.1 = bf16[256,6144]{1,0:T(8,128)(2,1)S(1)} copy-done((bf16[256,6144]{1,0:T(8,128)(2,1)S(1)}, bf16[256,6144]{1,0:T(8,128)(2,1)}, u32[]{:S(2)}) %copy-start.1) | copy-done | bytes 3145752
  88.0 17.6 %hidden_part.2.pooled_ref = f32[8,768]{1,0:T(8,128)S(1)} custom-call(bf16[256,6144]{1,0:T(8,128)(2,1)S(1)} %copy-done.1, bf16[16,128,768]{2,1,0:T(8,128)(2,1)} %fusion.choose_ref, bf16[1536,6144]{1,0:T(8,128)(2,1)} %up_ref.3), custom_call_target="tpu_custom_call" | custom-call | flops 9663676416 | bytes 15728640 | tf_op jit(solution)/shard_map/hidden_part/pallas_call | solution.py:295
  105.6 5.3 %down_part.2 = f32[8,6144]{1,0:T(8,128)S(1)} custom-call(f32[8,768]{1,0:T(8,128)S(1)} %hidden_part.2.pooled_ref, bf16[1536,6144]{1,0:T(8,128)(2,1)} %down_ref.3), custom_call_target="tpu_custom_call" | custom-call | flops 150994944 | bytes 9437184 | tf_op jit(solution)/shard_map/down_part/pallas_call | solution.py:334
  110.9 17.8 %hidden_part.3.pooled_ref = f32[8,768]{1,0:T(8,128)S(1)} custom-call(bf16[256,6144]{1,0:T(8,128)(2,1)S(1)} %copy-done.2, bf16[16,128,768]{2,1,0:T(8,128)(2,1)} %fusion.choose_ref, bf16[1536,6144]{1,0:T(8,128)(2,1)} %up_ref.3), custom_call_target="tpu_custom_call" | custom-call | flops 9663676416 | bytes 15728640 | tf_op jit(solution)/shard_map/hidden_part/pallas_call | solution.py:295
  128.7 5.1 %key_weights.3 = f32[16,256]{1,0:T(8,128)S(1)} custom-call(bf16[16,16,16,256]{3,2,1,0:T(8,128)(2,1)S(1)} %all-to-all-done.1.x_ref, f32[128,1]{1,0:T(8,128)S(1)} %copy.29.query_gain_ref, f32[128,1]{1,0:T(8,128)S(1)} %copy.30.key_gain_ref), custom_call_target="tpu_custom_call" | custom-call | flops 268435456 | bytes 2097152 | tf_op jit(solution)/shard_map/key_weights/pallas_call | solution.py:378
  133.9 0.7 broadcast_in_dim.22
  134.6 6.1 %all-to-all-start.2 = ((bf16[16,24,256]{2,1,0:T(8,128)(2,1)}), bf16[16,24,256]{2,1,0:T(8,128)(2,1)S(1)}, u32[]{:S(2)}, u32[]{:S(2)}) async-start(bf16[16,24,256]{2,1,0:T(8,128)(2,1)} %broadcast_in_dim.22), calls=%async_computation.2 | async-start | bytes 393216 | tf_op jit(solution)/shard_map/all_to_all | solution.py:564
  140.7 5.1 %down_part.3 = f32[8,6144]{1,0:T(8,128)S(1)} custom-call(f32[8,768]{1,0:T(8,128)S(1)} %hidden_part.3.pooled_ref, bf16[1536,6144]{1,0:T(8,128)(2,1)} %down_ref.3), custom_call_target="tpu_custom_call" | custom-call | flops 150994944 | bytes 9437184 | tf_op jit(solution)/shard_map/down_part/pallas_call | solution.py:334
  145.9 3.8 %all-to-all-done.2.key_ref = bf16[16,24,256]{2,1,0:T(8,128)(2,1)S(1)} async-done(((bf16[16,24,256]{2,1,0:T(8,128)(2,1)}), bf16[16,24,256]{2,1,0:T(8,128)(2,1)S(1)}, u32[]{:S(2)}, u32[]{:S(2)}) %all-to-all-start.2) | async-done | bytes 196640 | tf_op jit(solution)/shard_map/all_to_all | solution.py:564
  149.7 2.3 %copy-done.5 = bf16[8,48,6144]{2,1,0:T(8,128)(2,1)S(1)} copy-done((bf16[8,48,6144]{2,1,0:T(8,128)(2,1)S(1)}, bf16[8,48,6144]{2,1,0:T(8,128)(2,1)}, u32[]{:S(2)}) %copy-start.5) | copy-done | bytes 4718616
  152.0 2.8 %feature_part.1 = f32[16,8,384]{2,1,0:T(8,128)} custom-call(bf16[16,24,256]{2,1,0:T(8,128)(2,1)S(1)} %all-to-all-done.2.key_ref, bf16[8,256,384]{2,1,0:T(8,128)(2,1)S(1)} %copy-done.4, bf16[384,6144]{1,0:T(8,128)(2,1)S(1)} %bitcast.38, f32[8,6144]{1,0:T(8,128)S(1)} %add.107.hidden_ref, bf16[16,6144]{1,0:T(8,128)(2,1)S(1)} %copy-done.9), custom_call_target="tpu_custom_call" | custom-call | flops 78643200 | bytes 6291456 | tf_op jit(solution)/shard_map/feature_part/pallas_call | solution.py:433
  154.9 3.5 %all-to-all-start.3 = ((f32[16,8,384]{2,1,0:T(8,128)}), f32[16,8,384]{2,1,0:T(8,128)S(1)}, u32[]{:S(2)}, u32[]{:S(2)}) async-start(f32[16,8,384]{2,1,0:T(8,128)} %feature_part.1), calls=%async_computation.3 | async-start | bytes 393216 | tf_op jit(solution)/shard_map/all_to_all | solution.py:576
  158.4 0.8 dynamic_slice.3
  159.2 0.7 fusion.28
  159.9 7.4 %all-to-all-done.3 = f32[16,8,384]{2,1,0:T(8,128)S(1)} async-done(((f32[16,8,384]{2,1,0:T(8,128)}), f32[16,8,384]{2,1,0:T(8,128)S(1)}, u32[]{:S(2)}, u32[]{:S(2)}) %all-to-all-start.3) | async-done | bytes 196640 | tf_op jit(solution)/shard_map/all_to_all | solution.py:576
  167.4 0.2 fusion.24
  167.5 0.2 multiply_reduce_fusion
  167.7 0.8 fusion.10
  168.5 0.1 copy.34
  168.6 0.1 copy.33
  168.6 0.1 select_maximum_fusion.3
  168.7 1.2 collective-permute-done.14
  170.0 0.2 subtract_reduce_fusion.5
  170.3 0.1 select_maximum_fusion.2
  170.4 4.3 %collective-permute-done.15 = f32[9,1002]{1,0:T(8,128)S(1)} collective-permute-done((f32[9,1002]{1,0:T(8,128)S(1)}, f32[9,1002]{1,0:T(8,128)S(1)}, u32[]{:S(2)}, u32[]{:S(2)}) %collective-permute-start.15) | collective-permute-done | bytes 36104 | tf_op jit(solution)/shard_map/ppermute | solution.py:48
  174.6 0.2 subtract_reduce_fusion.3
  175.0 4.3 %collective-permute-done.16 = f32[9,1002]{1,0:T(8,128)S(1)} collective-permute-done((f32[9,1002]{1,0:T(8,128)S(1)}, f32[9,1002]{1,0:T(8,128)S(1)}, u32[]{:S(2)}, u32[]{:S(2)}) %collective-permute-start.16) | collective-permute-done | bytes 36104 | tf_op jit(solution)/shard_map/ppermute | solution.py:48
  179.2 0.2 subtract_reduce_fusion.1
  179.6 0.7 collective-permute-start.17
  180.3 4.7 %collective-permute-done.17.other_ref = f32[9,1002]{1,0:T(8,128)S(1)} collective-permute-done((f32[9,1002]{1,0:T(8,128)S(1)}, f32[9,1002]{1,0:T(8,128)S(1)}, u32[]{:S(2)}, u32[]{:S(2)}) %collective-permute-start.17) | collective-permute-done | bytes 36104 | tf_op jit(solution)/shard_map/ppermute | solution.py:48
  184.9 0.9 finish.1
  (61 shorter events, 0.9 us)
Async XLA Ops:
  0.6 158.6 %copy-start = (bf16[384,1000]{0,1:T(8,128)(2,1)S(1)}, bf16[384,1000]{0,1:T(8,128)(2,1)}, u32[]{:S(2)}) copy-start(bf16[384,1000]{0,1:T(8,128)(2,1)} %param.21) | copy-start | bytes 2304004
  2.6 11.6 %copy-start.11 = (bf16[16,2048]{1,0:T(8,128)(2,1)S(1)}, bf16[16,2048]{1,0:T(8,128)(2,1)}, u32[]{:S(2)}) copy-start(bf16[16,2048]{1,0:T(8,128)(2,1)} %get-tuple-element.22) | copy-start | bytes 196612
  2.6 16.3 %copy-start.10 = (bf16[16,4096]{1,0:T(8,128)(2,1)S(1)}, bf16[16,4096]{1,0:T(8,128)(2,1)}, u32[]{:S(2)}) copy-start(bf16[16,4096]{1,0:T(8,128)(2,1)} %get-tuple-element.21) | copy-start | bytes 393220
  2.6 11.6 %collective-permute-start.2 = (bf16[16,4096]{1,0:T(8,128)(2,1)}, bf16[16,4096]{1,0:T(8,128)(2,1)S(1)}, u32[]{:S(2)}, u32[]{:S(2)}) collective-permute-start(bf16[16,4096]{1,0:T(8,128)(2,1)} %get-tuple-element.21), channel_id=1, source_target_pairs={{0,12},{1,13},{2,14},{3,15},{4,8},{5,9},{6,10},{7,11},{8,4},{9,5},... | collective-permute-start | bytes 393224 | tf_op jit(solution)/shard_map/ppermute | solution.py:48
  7.7 11.3 %collective-permute-start.1 = (bf16[16,4096]{1,0:T(8,128)(2,1)}, bf16[16,4096]{1,0:T(8,128)(2,1)S(1)}, u32[]{:S(2)}, u32[]{:S(2)}) collective-permute-start(bf16[16,4096]{1,0:T(8,128)(2,1)} %get-tuple-element.21), channel_id=1, source_target_pairs={{0,8},{1,9},{2,10},{3,11},{4,12},{5,13},{6,14},{7,15},{8,0},{9,1},... | collective-permute-start | bytes 393224 | tf_op jit(solution)/shard_map/ppermute | solution.py:48
  7.7 11.3 %collective-permute-start = (bf16[16,4096]{1,0:T(8,128)(2,1)}, bf16[16,4096]{1,0:T(8,128)(2,1)S(1)}, u32[]{:S(2)}, u32[]{:S(2)}) collective-permute-start(bf16[16,4096]{1,0:T(8,128)(2,1)} %get-tuple-element.21), channel_id=1, source_target_pairs={{0,4},{1,5},{2,6},{3,7},{4,0},{5,1},{6,2},{7,3},{8,12},{9,13},{10,... | collective-permute-start | bytes 393224 | tf_op jit(solution)/shard_map/ppermute | solution.py:48
  8.3 5.9 %collective-permute-start.3 = (bf16[16,2048]{1,0:T(8,128)(2,1)}, bf16[16,2048]{1,0:T(8,128)(2,1)S(1)}, u32[]{:S(2)}, u32[]{:S(2)}) collective-permute-start(bf16[16,2048]{1,0:T(8,128)(2,1)} %get-tuple-element.22), channel_id=1, source_target_pairs={{0,2},{1,3},{2,0},{3,1},{4,6},{5,7},{6,4},{7,5},{8,10},{9,11},{10,... | collective-permute-start | bytes 196616 | tf_op jit(solution)/shard_map/ppermute | solution.py:48
  19.0 13.8 %collective-permute-start.4 = (bf16[4,16,4096]{2,1,0:T(8,128)(2,1)S(1)}, bf16[4,16,4096]{2,1,0:T(8,128)(2,1)S(1)}, u32[]{:S(2)}, u32[]{:S(2)}) collective-permute-start(bf16[4,16,4096]{2,1,0:T(8,128)(2,1)S(1)} %pad_maximum_fusion.refs_0_), channel_id=1, source_target_pairs={{0,2},{1,3},{2,0},{3,1},{4,6},{5,7},{6,4},{7,5},{8,10},{9,11},{10,... | collective-permute-start | bytes 1572872 | tf_op jit(solution)/shard_map/ppermute | solution.py:48
  20.6 6.0 %collective-permute-start.5 = (bf16[2,16,2048]{2,1,0:T(8,128)(2,1)S(1)}, bf16[2,16,2048]{2,1,0:T(8,128)(2,1)S(1)}, u32[]{:S(2)}, u32[]{:S(2)}) collective-permute-start(bf16[2,16,2048]{2,1,0:T(8,128)(2,1)S(1)} %pad_maximum_fusion.1.refs_2_), channel_id=1, source_target_pairs={{0,4},{1,5},{2,6},{3,7},{4,0},{5,1},{6,2},{7,3},{8,12},{9,13},{10,... | collective-permute-start | bytes 393224 | tf_op jit(solution)/shard_map/ppermute | solution.py:48
  20.6 12.2 %collective-permute-start.6 = (bf16[2,16,2048]{2,1,0:T(8,128)(2,1)S(1)}, bf16[2,16,2048]{2,1,0:T(8,128)(2,1)S(1)}, u32[]{:S(2)}, u32[]{:S(2)}) collective-permute-start(bf16[2,16,2048]{2,1,0:T(8,128)(2,1)S(1)} %pad_maximum_fusion.1.refs_2_), channel_id=1, source_target_pairs={{0,8},{1,9},{2,10},{3,11},{4,12},{5,13},{6,14},{7,15},{8,0},{9,1},... | collective-permute-start | bytes 393224 | tf_op jit(solution)/shard_map/ppermute | solution.py:48
  23.7 9.2 %collective-permute-start.7 = (bf16[2,16,2048]{2,1,0:T(8,128)(2,1)S(1)}, bf16[2,16,2048]{2,1,0:T(8,128)(2,1)S(1)}, u32[]{:S(2)}, u32[]{:S(2)}) collective-permute-start(bf16[2,16,2048]{2,1,0:T(8,128)(2,1)S(1)} %pad_maximum_fusion.1.refs_2_), channel_id=1, source_target_pairs={{0,12},{1,13},{2,14},{3,15},{4,8},{5,9},{6,10},{7,11},{8,4},{9,5},... | collective-permute-start | bytes 393224 | tf_op jit(solution)/shard_map/ppermute | solution.py:48
  25.0 10.3 %collective-permute-start.8 = (bf16[4,16,4096]{2,1,0:T(8,128)(2,1)S(1)}, bf16[4,16,4096]{2,1,0:T(8,128)(2,1)S(1)}, u32[]{:S(2)}, u32[]{:S(2)}) collective-permute-start(bf16[4,16,4096]{2,1,0:T(8,128)(2,1)S(1)} %pad_maximum_fusion.refs_0_), channel_id=1, source_target_pairs={{0,1},{1,0},{2,3},{3,2},{4,5},{5,4},{6,7},{7,6},{8,9},{9,8},{10,11... | collective-permute-start | bytes 1572872 | tf_op jit(solution)/shard_map/ppermute | solution.py:48
  32.8 3.8 %collective-permute-start.9 = (bf16[4,16,4096]{2,1,0:T(8,128)(2,1)S(1)}, bf16[4,16,4096]{2,1,0:T(8,128)(2,1)S(1)}, u32[]{:S(2)}, u32[]{:S(2)}) collective-permute-start(bf16[4,16,4096]{2,1,0:T(8,128)(2,1)S(1)} %collective-permute-done.4.refs_1_), channel_id=1, source_target_pairs={{0,1},{1,0},{2,3},{3,2},{4,5},{5,4},{6,7},{7,6},{8,9},{9,8},{10,11... | collective-permute-start | bytes 1572872 | tf_op jit(solution)/shard_map/ppermute | solution.py:48
  32.8 2.3 %collective-permute-start.10 = (bf16[2,16,2048]{2,1,0:T(8,128)(2,1)S(1)}, bf16[2,16,2048]{2,1,0:T(8,128)(2,1)S(1)}, u32[]{:S(2)}, u32[]{:S(2)}) collective-permute-start(bf16[2,16,2048]{2,1,0:T(8,128)(2,1)S(1)} %pad_maximum_fusion.1.refs_2_), channel_id=1, source_target_pairs={{0,1},{1,0},{2,3},{3,2},{4,5},{5,4},{6,7},{7,6},{8,9},{9,8},{10,11... | collective-permute-start | bytes 393224 | tf_op jit(solution)/shard_map/ppermute | solution.py:48
  33.4 1.9 %collective-permute-start.11 = (bf16[2,16,2048]{2,1,0:T(8,128)(2,1)S(1)}, bf16[2,16,2048]{2,1,0:T(8,128)(2,1)}, u32[]{:S(2)}, u32[]{:S(2)}) collective-permute-start(bf16[2,16,2048]{2,1,0:T(8,128)(2,1)S(1)} %collective-permute-done.5.refs_3_), channel_id=1, source_target_pairs={{0,1},{1,0},{2,3},{3,2},{4,5},{5,4},{6,7},{7,6},{8,9},{9,8},{10,11... | collective-permute-start | bytes 393224 | tf_op jit(solution)/shard_map/ppermute | solution.py:48
  33.4 2.0 %collective-permute-start.12 = (bf16[2,16,2048]{2,1,0:T(8,128)(2,1)S(1)}, bf16[2,16,2048]{2,1,0:T(8,128)(2,1)}, u32[]{:S(2)}, u32[]{:S(2)}) collective-permute-start(bf16[2,16,2048]{2,1,0:T(8,128)(2,1)S(1)} %collective-permute-done.6.refs_4_), channel_id=1, source_target_pairs={{0,1},{1,0},{2,3},{3,2},{4,5},{5,4},{6,7},{7,6},{8,9},{9,8},{10,11... | collective-permute-start | bytes 393224 | tf_op jit(solution)/shard_map/ppermute | solution.py:48
  35.1 1.5 collective-permute-start.13
  47.6 27.1 %all-to-all-start = ((bf16[16,8,16,256]{3,2,1,0:T(8,128)(2,1)}), bf16[16,8,16,256]{3,2,1,0:T(8,128)(2,1)S(1)}, u32[]{:S(2)}, u32[]{:S(2)}) async-start(bf16[16,8,16,256]{3,2,1,0:T(8,128)(2,1)} %query_key.2), calls=%async_computation | async-start | bytes 2097152 | tf_op jit(solution)/shard_map/all_to_all | solution.py:544
  59.5 1.2 copy-start.3
  60.7 21.8 %copy-start.12 = (f32[128]{0:T(128)S(1)}, f32[128]{0:T(128)}, u32[]{:S(2)}) copy-start(f32[128]{0:T(128)} %param.16) | copy-start | bytes 1540
  60.7 22.0 %copy-start.13 = (f32[128]{0:T(128)S(1)}, f32[128]{0:T(128)}, u32[]{:S(2)}) copy-start(f32[128]{0:T(128)} %param.17) | copy-start | bytes 1540
  72.3 1.4 copy-start.8
  74.7 1.0 copy-start.6
  75.7 53.0 %all-to-all-start.1 = ((bf16[16,16,16,256]{3,2,1,0:T(8,128)(2,1)}), bf16[16,16,16,256]{3,2,1,0:T(8,128)(2,1)S(1)}, u32[]{:S(2)}, u32[]{:S(2)}) async-start(bf16[16,16,16,256]{3,2,1,0:T(8,128)(2,1)} %bitcast.39), calls=%async_computation.1 | async-start | bytes 4194304 | tf_op jit(solution)/shard_map/all_to_all | solution.py:544
  82.8 1.2 copy-start.7
  86.1 1.9 %copy-start.1 = (bf16[256,6144]{1,0:T(8,128)(2,1)S(1)}, bf16[256,6144]{1,0:T(8,128)(2,1)}, u32[]{:S(2)}) copy-start(bf16[256,6144]{1,0:T(8,128)(2,1)} %place_rows.1.norm_ref) | copy-start | bytes 9437188
  105.6 5.3 %copy-start.2 = (bf16[256,6144]{1,0:T(8,128)(2,1)S(1)}, bf16[256,6144]{1,0:T(8,128)(2,1)}, u32[]{:S(2)}) copy-start(bf16[256,6144]{1,0:T(8,128)(2,1)} %place_rows.1.norm_ref) | copy-start | bytes 9437188
  134.6 15.1 %all-to-all-start.2 = ((bf16[16,24,256]{2,1,0:T(8,128)(2,1)}), bf16[16,24,256]{2,1,0:T(8,128)(2,1)S(1)}, u32[]{:S(2)}, u32[]{:S(2)}) async-start(bf16[16,24,256]{2,1,0:T(8,128)(2,1)} %broadcast_in_dim.22), calls=%async_computation.2 | async-start | bytes 393216 | tf_op jit(solution)/shard_map/all_to_all | solution.py:564
  140.7 9.0 %copy-start.4 = (bf16[8,256,384]{2,1,0:T(8,128)(2,1)S(1)}, bf16[8,256,384]{2,1,0:T(8,128)(2,1)}, u32[]{:S(2)}) copy-start(bf16[8,256,384]{2,1,0:T(8,128)(2,1)} %copy-done.3) | copy-start | bytes 4718596
  140.7 9.0 %copy-start.9 = (bf16[16,6144]{1,0:T(8,128)(2,1)S(1)}, bf16[16,6144]{1,0:T(8,128)(2,1)}, u32[]{:S(2)}) copy-start(bf16[16,6144]{1,0:T(8,128)(2,1)} %token_ref.1) | copy-start | bytes 589828
  149.7 2.3 %copy-start.5 = (bf16[8,48,6144]{2,1,0:T(8,128)(2,1)S(1)}, bf16[8,48,6144]{2,1,0:T(8,128)(2,1)}, u32[]{:S(2)}) copy-start(bf16[8,48,6144]{2,1,0:T(8,128)(2,1)} %param.18) | copy-start | bytes 14155780
  154.9 12.5 %all-to-all-start.3 = ((f32[16,8,384]{2,1,0:T(8,128)}), f32[16,8,384]{2,1,0:T(8,128)S(1)}, u32[]{:S(2)}, u32[]{:S(2)}) async-start(f32[16,8,384]{2,1,0:T(8,128)} %feature_part.1), calls=%async_computation.3 | async-start | bytes 393216 | tf_op jit(solution)/shard_map/all_to_all | solution.py:576
  168.7 1.3 collective-permute-start.14
  170.3 4.3 %collective-permute-start.15 = (f32[9,1002]{1,0:T(8,128)S(1)}, f32[9,1002]{1,0:T(8,128)S(1)}, u32[]{:S(2)}, u32[]{:S(2)}) collective-permute-start(f32[9,1002]{1,0:T(8,128)S(1)} %select_maximum_fusion.2), channel_id=1, source_target_pairs={{0,2},{1,3},{2,0},{3,1},{4,6},{5,7},{6,4},{7,5},{8,10},{9,11},{10,... | collective-permute-start | bytes 108224 | tf_op jit(solution)/shard_map/ppermute | solution.py:48
  175.0 4.3 %collective-permute-start.16 = (f32[9,1002]{1,0:T(8,128)S(1)}, f32[9,1002]{1,0:T(8,128)S(1)}, u32[]{:S(2)}, u32[]{:S(2)}) collective-permute-start(f32[9,1002]{1,0:T(8,128)S(1)} %select_maximum_fusion.1), channel_id=1, source_target_pairs={{0,4},{1,5},{2,6},{3,7},{4,0},{5,1},{6,2},{7,3},{8,12},{9,13},{10,... | collective-permute-start | bytes 108224 | tf_op jit(solution)/shard_map/ppermute | solution.py:48
  179.6 5.3 %collective-permute-start.17 = (f32[9,1002]{1,0:T(8,128)S(1)}, f32[9,1002]{1,0:T(8,128)S(1)}, u32[]{:S(2)}, u32[]{:S(2)}) collective-permute-start(f32[9,1002]{1,0:T(8,128)S(1)} %select_maximum_fusion.mine_ref), channel_id=1, source_target_pairs={{0,8},{1,9},{2,10},{3,11},{4,12},{5,13},{6,14},{7,15},{8,0},{9,1},... | collective-permute-start | bytes 108224 | tf_op jit(solution)/shard_map/ppermute | solution.py:48

commit v3 on v2

--- a/solution.py
+++ b/solution.py
@@ -348,10 +348,13 @@
     )(pooled, w_down)
 
 
-def attention_kernel(items, x_ref, query_gain_ref, key_gain_ref, out_ref):
+def attention_kernel(items, x_ref, query_gain_ref, key_gain_ref, *refs):
+    *before, out_ref, held = refs
     parts, _, both, rows = x_ref.shape
     comps = both // 2
     head_dim = parts * comps
+    ones = jnp.ones((16, rows), BF16)
+    first = held.shape[0] - items
 
     def normed(values, gain_ref):
         values = values.reshape(head_dim, rows)
@@ -360,24 +363,37 @@
         spread_sq = jnp.mean(centered * centered, axis=0, keepdims=True)
         return (centered * lax.rsqrt(spread_sq + 1e-06) * gain_ref[...]).astype(BF16)
 
+    if before:
+        held[:first] = before[0][...]
     for j in range(items):
         x = x_ref[:, j].astype(F32)
         query = normed(x[:, :comps], query_gain_ref)
         key = normed(x[:, comps:], key_gain_ref)
         scores = lax.dot_general(
-            query, key, (((0,), (0,)), ((), ())), preferred_element_type=F32
+            key, query, (((0,), (0,)), ((), ())), preferred_element_type=F32
         )
         e = jnp.exp2(scores * (math.log2(math.e) / math.sqrt(head_dim)))
-        weights = (e * (1.0 / jnp.sum(e, axis=1, keepdims=True))).astype(BF16)
-        out_ref[j : j + 1, :] = jnp.sum(weights.astype(F32), axis=0, keepdims=True) * (1.0 / rows)
-
-
-def key_weights(exchanged, query_gain, key_gain):
+        weights = (e * (1.0 / jnp.sum(e, axis=0, keepdims=True))).astype(BF16)
+        mean = lax.dot_general(ones, weights, ACROSS, preferred_element_type=F32)[:1]
+        held[first + j : first + j + 1, :] = mean * (1.0 / rows)
+    if before:
+        for part in range(parts):
+            out_ref[part] = held[...].astype(BF16)
+    else:
+        out_ref[...] = held[...]
+
+
+def key_weights(exchanged, query_gain, key_gain, *before):
     parts, items, both, rows = exchanged.shape
     head_dim = parts * both // 2
+    count = items + sum(x.shape[0] for x in before)
+    shape = jax.ShapeDtypeStruct((items, rows), F32)
+    if before:
+        shape = jax.ShapeDtypeStruct((parts, count, rows), BF16)
     return pl.pallas_call(
         functools.partial(attention_kernel, items),
-        out_shape=jax.ShapeDtypeStruct((items, rows), F32),
+        out_shape=shape,
+        scratch_shapes=[pltpu.VMEM((count, rows), F32)],
         compiler_params=pltpu.CompilerParams(vmem_limit_bytes=50 * MIB),
         cost_estimate=pl.CostEstimate(
             flops=2 * items * rows * rows * head_dim,
@@ -385,7 +401,7 @@
             transcendentals=items * rows * rows,
         ),
         name="key_weights",
-    )(exchanged, query_gain.reshape(head_dim, 1), key_gain.reshape(head_dim, 1))
+    )(exchanged, query_gain.reshape(head_dim, 1), key_gain.reshape(head_dim, 1), *before)
 
 
 def feature_kernel(key_ref, value_ref, proj_ref, hidden_ref, token_ref, out_ref, attended):
@@ -557,17 +573,11 @@
     more_pooled = hidden_part(norm, choose, w_up, tiles, tiles)
     hidden = down_part(pooled, w_down, 0)
     key_mean = key_weights(first, query_gain, key_gain)
-    more = key_weights(second, query_gain, key_gain)
-    hidden, more_pooled, key_mean, more = together((hidden, more_pooled, key_mean, more))
-    key_mean = jnp.concatenate([key_mean, more], axis=0).astype(BF16)
+    hidden, more_pooled, key_mean, second = together((hidden, more_pooled, key_mean, second))
+    key_mean = key_weights(second, query_gain, key_gain, key_mean)
+    more_pooled, key_mean = together((more_pooled, key_mean))
     hidden = hidden + down_part(more_pooled, w_down, tiles)
-    key_mean = lax.all_to_all(
-        jnp.broadcast_to(key_mean[None], (n_parts,) + key_mean.shape),
-        "inp",
-        split_axis=0,
-        concat_axis=0,
-        tiled=True,
-    )
+    key_mean = lax.all_to_all(key_mean, "inp", split_axis=0, concat_axis=0, tiled=True)
     partial_feature = feature_part(
         key_mean, value, w_proj.reshape(n_comps * n_heads, model_width), hidden, tokens, 4
     )

time: 187 us -> 184 us (0.984)
  Pallas kernels: 88.9 us -> 85.9 us
    pallas_call x2, Pallas kernels: 7.18 us -> 4.47 us  [key_weights(): pl.pallas_call(functools.partial(attention_kernel, items), out_shape=shap...]
where the time goes in v3:
time: 184 us; the launch traced here: 183 us
  Pallas kernels  85.9 us (47%)
  waiting for transfers between devices  41.8 us (23%)
  starting transfers between devices  36.9 us (20%)
  local copies, waits for them, and re-layouts  11.6 us (6%)
  matrix products  4.14 us (2%)
    pallas_call x2, Pallas kernels, hidden_part(): pl.pallas_call(hidden_kernel, grid=(tiles, width // depth), out_shape=jax...  35.1 us
    ppermute x18, waiting for transfers between devices, permuted(): return lax.ppermute(array, 'inp', [(i, i ^ bits) for i in range(count)])  29.5 us
    pallas_call x2, Pallas kernels, query_key(): pl.pallas_call(query_key_kernel, grid=(width // depth,), out_shape=jax.Sh...  19.7 us
    ppermute x18, starting transfers between devices, permuted(): return lax.ppermute(array, 'inp', [(i, i ^ bits) for i in range(count)])  15.2 us
    all_to_all x2, starting transfers between devices, exchange(): return lax.all_to_all(array, 'inp', split_axis=0, concat_axis=0, tiled=True)  11.1 us
    pallas_call x2, Pallas kernels, down_part(): pl.pallas_call(down_kernel, grid=(units // UNITS,), out_shape=jax.ShapeDt...  10.4 us
    unnamed x29, local copies, waits for them, and re-layouts  10.4 us
    pallas_call x1, Pallas kernels, values_of(): pl.pallas_call(value_kernel, grid=(width // depth,), out_shape=jax.ShapeD...  7.74 us
  transfers between devices with their start and end apart: 22, of which 13 were waited for; matrix products, arithmetic and copies ran while one was open for 3% of the time, Pallas kernels for 36%

profile of v3, /device:TPU:0, one launch (start us, length us, event | category | flops | bytes accessed | tf_op | source)
XLA Modules:
  0.0 183.1 jit_solution(6956201425415418260)
XLA Ops:
  0.6 2.0 %own_norm.1 = (bf16[16,4096]{1,0:T(8,128)(2,1)}, bf16[16,2048]{1,0:T(8,128)(2,1)}) custom-call(bf16[16,6144]{1,0:T(8,128)(2,1)} %token_ref.1, f32[1,6144]{1,0:T(1,128)} %bitcast.51), custom_call_target="tpu_custom_call" | custom-call | tf_op jit(solution)/shard_map/own_norm/pallas_call | solution.py:61
  2.6 5.0 %collective-permute-start.2 = (bf16[16,4096]{1,0:T(8,128)(2,1)}, bf16[16,4096]{1,0:T(8,128)(2,1)S(1)}, u32[]{:S(2)}, u32[]{:S(2)}) collective-permute-start(bf16[16,4096]{1,0:T(8,128)(2,1)} %get-tuple-element.23), channel_id=1, source_target_pairs={{0,12},{1,13},{2,14},{3,15},{4,8},{5,9},{6,10},{7,11},{8,4},{9,5},... | collective-permute-start | bytes 393224 | tf_op jit(solution)/shard_map/ppermute | solution.py:48
  7.7 0.6 collective-permute-start
  8.3 1.7 collective-permute-start.3
  10.0 1.3 copy.25
  11.5 0.1 broadcast_compare_fusion
  11.6 2.6 %fusion.choose_ref = bf16[16,128,768]{2,1,0:T(8,128)(2,1)} fusion(pred[128,768]{1,0:T(8,128)(4,1)S(1)} %broadcast_compare_fusion, bf16[16,128,48]{2,1,0:T(8,128)(2,1)S(1)} %bitcast.41, s32[768]{0:T(1024)S(1)} %add_select_fusion), kind=kOutput, calls=%fused_computation.1 | convolution fusion | flops 155750400 | bytes 3443712 | tf_op jit(solution)/shard_map/trb,bc->trc/dot_general | solution.py:130
  14.3 4.7 %collective-permute-done.1 = bf16[16,4096]{1,0:T(8,128)(2,1)S(1)} collective-permute-done((bf16[16,4096]{1,0:T(8,128)(2,1)}, bf16[16,4096]{1,0:T(8,128)(2,1)S(1)}, u32[]{:S(2)}, u32[]{:S(2)}) %collective-permute-start.1) | collective-permute-done | bytes 131104 | tf_op jit(solution)/shard_map/ppermute | solution.py:48
  19.0 1.6 collective-permute-start.4
  20.6 3.0 %collective-permute-start.6 = (bf16[2,16,2048]{2,1,0:T(8,128)(2,1)S(1)}, bf16[2,16,2048]{2,1,0:T(8,128)(2,1)S(1)}, u32[]{:S(2)}, u32[]{:S(2)}) collective-permute-start(bf16[2,16,2048]{2,1,0:T(8,128)(2,1)S(1)} %pad_maximum_fusion.1.refs_2_), channel_id=1, source_target_pairs={{0,8},{1,9},{2,10},{3,11},{4,12},{5,13},{6,14},{7,15},{8,0},{9,1},... | collective-permute-start | bytes 393224 | tf_op jit(solution)/shard_map/ppermute | solution.py:48
  23.7 1.3 collective-permute-start.7
  25.0 1.6 collective-permute-done.5.refs_3_
  26.6 6.3 %collective-permute-done.6.refs_4_ = bf16[2,16,2048]{2,1,0:T(8,128)(2,1)S(1)} collective-permute-done((bf16[2,16,2048]{2,1,0:T(8,128)(2,1)S(1)}, bf16[2,16,2048]{2,1,0:T(8,128)(2,1)S(1)}, u32[]{:S(2)}, u32[]{:S(2)}) %collective-permute-start.6) | collective-permute-done | bytes 131104 | tf_op jit(solution)/shard_map/ppermute | solution.py:48
  32.8 0.5 collective-permute-start.10
  33.4 0.4 collective-permute-start.12
  33.9 1.3 collective-permute-done.10.refs_8_
  35.1 0.1 collective-permute-start.13
  35.3 0.2 collective-permute-done.12.refs_10_
  35.4 1.2 collective-permute-done.13.refs_11_
  36.6 2.9 %place_rows.1.norm_ref = bf16[256,6144]{1,0:T(8,128)(2,1)} custom-call(s32[1]{0:T(128)} %bitcast.me_ref, bf16[4,16,4096]{2,1,0:T(8,128)(2,1)S(1)} %pad_maximum_fusion.refs_0_, bf16[4,16,4096]{2,1,0:T(8,128)(2,1)S(1)} %collective-permute-done.4.refs_1_, bf16[2,16,2048]{2,1,0:T(8,128)(2,1)S(1)} %pad_maximum_fusion.1.refs_2_, ...), custom_call_target="tpu_custom_call" | custom-call | tf_op jit(solution)/shard_map/place_rows/pallas_call | solution.py:106
  39.5 8.1 %query_key.2 = bf16[16,8,16,256]{3,2,1,0:T(8,128)(2,1)} custom-call(bf16[256,6144]{1,0:T(8,128)(2,1)} %place_rows.1.norm_ref, bf16[16,128,768]{2,1,0:T(8,128)(2,1)} %fusion.choose_ref, bf16[8,3,48,6144]{3,2,1,0:T(8,128)(2,1)} %w_ref.5), custom_call_target="tpu_custom_call" | custom-call | flops 3221225472 | bytes 9437184 | tf_op jit(solution)/shard_map/query_key/pallas_call | solution.py:186
  47.6 4.2 %all-to-all-start = ((bf16[16,8,16,256]{3,2,1,0:T(8,128)(2,1)}), bf16[16,8,16,256]{3,2,1,0:T(8,128)(2,1)S(1)}, u32[]{:S(2)}, u32[]{:S(2)}) async-start(bf16[16,8,16,256]{3,2,1,0:T(8,128)(2,1)} %query_key.2), calls=%async_computation | async-start | bytes 2097152 | tf_op jit(solution)/shard_map/all_to_all | solution.py:560
  51.8 7.7 %value_rows.1.value_ref = bf16[8,256,384]{2,1,0:T(8,128)(2,1)S(1)} custom-call(bf16[256,6144]{1,0:T(8,128)(2,1)} %place_rows.1.norm_ref, bf16[16,128,768]{2,1,0:T(8,128)(2,1)} %fusion.choose_ref, bf16[8,3,48,6144]{3,2,1,0:T(8,128)(2,1)} %w_ref.5), custom_call_target="tpu_custom_call" | custom-call | flops 4831838208 | bytes 11010048 | tf_op jit(solution)/shard_map/value_rows/pallas_call | solution.py:236
  59.6 1.2 copy-done.3
  60.7 11.6 %query_key.3 = bf16[32,8,16,256]{3,2,1,0:T(8,128)(2,1)S(1)} custom-call(bf16[256,6144]{1,0:T(8,128)(2,1)} %place_rows.1.norm_ref, bf16[16,128,768]{2,1,0:T(8,128)(2,1)} %fusion.choose_ref, bf16[8,3,48,6144]{3,2,1,0:T(8,128)(2,1)} %w_ref.5), custom_call_target="tpu_custom_call" | custom-call | flops 6442450944 | bytes 12582912 | tf_op jit(solution)/shard_map/query_key/pallas_call | solution.py:186
  72.3 1.4 copy-done.8
  73.7 1.0 all-to-all-done.x_ref
  74.7 1.0 copy-done.6
  75.7 6.9 %all-to-all-start.1 = ((bf16[16,16,16,256]{3,2,1,0:T(8,128)(2,1)}), bf16[16,16,16,256]{3,2,1,0:T(8,128)(2,1)S(1)}, u32[]{:S(2)}, u32[]{:S(2)}) async-start(bf16[16,16,16,256]{3,2,1,0:T(8,128)(2,1)} %bitcast.39), calls=%async_computation.1 | async-start | bytes 4194304 | tf_op jit(solution)/shard_map/all_to_all | solution.py:560
  82.6 0.1 copy.29.query_gain_ref
  82.7 0.1 copy.30.key_gain_ref
  82.8 1.2 copy-done.7
  84.0 1.4 key_weights.2.refs_0_
  85.4 1.9 %copy-done.1 = bf16[256,6144]{1,0:T(8,128)(2,1)S(1)} copy-done((bf16[256,6144]{1,0:T(8,128)(2,1)S(1)}, bf16[256,6144]{1,0:T(8,128)(2,1)}, u32[]{:S(2)}) %copy-start.1) | copy-done | bytes 3145752
  87.3 17.6 %hidden_part.2.pooled_ref = f32[8,768]{1,0:T(8,128)S(1)} custom-call(bf16[256,6144]{1,0:T(8,128)(2,1)S(1)} %copy-done.1, bf16[16,128,768]{2,1,0:T(8,128)(2,1)} %fusion.choose_ref, bf16[1536,6144]{1,0:T(8,128)(2,1)} %up_ref.3), custom_call_target="tpu_custom_call" | custom-call | flops 9663676416 | bytes 15728640 | tf_op jit(solution)/shard_map/hidden_part/pallas_call | solution.py:295
  104.9 5.3 %down_part.2 = f32[8,6144]{1,0:T(8,128)S(1)} custom-call(f32[8,768]{1,0:T(8,128)S(1)} %hidden_part.2.pooled_ref, bf16[1536,6144]{1,0:T(8,128)(2,1)} %down_ref.3), custom_call_target="tpu_custom_call" | custom-call | flops 150994944 | bytes 9437184 | tf_op jit(solution)/shard_map/down_part/pallas_call | solution.py:334
  110.2 17.6 %hidden_part.3.pooled_ref = f32[8,768]{1,0:T(8,128)S(1)} custom-call(bf16[256,6144]{1,0:T(8,128)(2,1)S(1)} %copy-done.2, bf16[16,128,768]{2,1,0:T(8,128)(2,1)} %fusion.choose_ref, bf16[1536,6144]{1,0:T(8,128)(2,1)} %up_ref.3), custom_call_target="tpu_custom_call" | custom-call | flops 9663676416 | bytes 15728640 | tf_op jit(solution)/shard_map/hidden_part/pallas_call | solution.py:295
  127.8 3.1 %key_weights.3 = bf16[16,24,256]{2,1,0:T(8,128)(2,1)} custom-call(bf16[16,16,16,256]{3,2,1,0:T(8,128)(2,1)S(1)} %all-to-all-done.1.x_ref, f32[128,1]{1,0:T(8,128)S(1)} %copy.29.query_gain_ref, f32[128,1]{1,0:T(8,128)S(1)} %copy.30.key_gain_ref, f32[8,256]{1,0:T(8,128)S(1)} %key_weights.2.refs_0_), custom_call_target="tpu_custom_call" | custom-call | flops 268435456 | bytes 2097152 | tf_op jit(solution)/shard_map/key_weights/pallas_call | solution.py:393
  130.9 7.1 %all-to-all-start.2 = ((bf16[16,24,256]{2,1,0:T(8,128)(2,1)}), bf16[16,24,256]{2,1,0:T(8,128)(2,1)S(1)}, u32[]{:S(2)}, u32[]{:S(2)}) async-start(bf16[16,24,256]{2,1,0:T(8,128)(2,1)} %key_weights.3), calls=%async_computation.2 | async-start | bytes 393216 | tf_op jit(solution)/shard_map/all_to_all | solution.py:580
  138.0 5.1 %down_part.3 = f32[8,6144]{1,0:T(8,128)S(1)} custom-call(f32[8,768]{1,0:T(8,128)S(1)} %hidden_part.3.pooled_ref, bf16[1536,6144]{1,0:T(8,128)(2,1)} %down_ref.3), custom_call_target="tpu_custom_call" | custom-call | flops 150994944 | bytes 9437184 | tf_op jit(solution)/shard_map/down_part/pallas_call | solution.py:334
  143.2 3.8 %all-to-all-done.2.key_ref = bf16[16,24,256]{2,1,0:T(8,128)(2,1)S(1)} async-done(((bf16[16,24,256]{2,1,0:T(8,128)(2,1)}), bf16[16,24,256]{2,1,0:T(8,128)(2,1)S(1)}, u32[]{:S(2)}, u32[]{:S(2)}) %all-to-all-start.2) | async-done | bytes 196640 | tf_op jit(solution)/shard_map/all_to_all | solution.py:580
  147.0 2.3 %copy-done.5 = bf16[8,48,6144]{2,1,0:T(8,128)(2,1)S(1)} copy-done((bf16[8,48,6144]{2,1,0:T(8,128)(2,1)S(1)}, bf16[8,48,6144]{2,1,0:T(8,128)(2,1)}, u32[]{:S(2)}) %copy-start.5) | copy-done | bytes 4718616
  149.3 2.8 %feature_part.1 = f32[16,8,384]{2,1,0:T(8,128)} custom-call(bf16[16,24,256]{2,1,0:T(8,128)(2,1)S(1)} %all-to-all-done.2.key_ref, bf16[8,256,384]{2,1,0:T(8,128)(2,1)S(1)} %copy-done.4, bf16[384,6144]{1,0:T(8,128)(2,1)S(1)} %bitcast.38, f32[8,6144]{1,0:T(8,128)S(1)} %add.107.hidden_ref, bf16[16,6144]{1,0:T(8,128)(2,1)S(1)} %copy-done.9), custom_call_target="tpu_custom_call" | custom-call | flops 78643200 | bytes 6291456 | tf_op jit(solution)/shard_map/feature_part/pallas_call | solution.py:449
  152.2 3.5 %all-to-all-start.3 = ((f32[16,8,384]{2,1,0:T(8,128)}), f32[16,8,384]{2,1,0:T(8,128)S(1)}, u32[]{:S(2)}, u32[]{:S(2)}) async-start(f32[16,8,384]{2,1,0:T(8,128)} %feature_part.1), calls=%async_computation.3 | async-start | bytes 393216 | tf_op jit(solution)/shard_map/all_to_all | solution.py:586
  155.7 0.8 dynamic_slice.3
  156.5 0.7 fusion.28
  157.2 7.4 %all-to-all-done.3 = f32[16,8,384]{2,1,0:T(8,128)S(1)} async-done(((f32[16,8,384]{2,1,0:T(8,128)}), f32[16,8,384]{2,1,0:T(8,128)S(1)}, u32[]{:S(2)}, u32[]{:S(2)}) %all-to-all-start.3) | async-done | bytes 196640 | tf_op jit(solution)/shard_map/all_to_all | solution.py:586
  164.7 0.2 fusion.24
  164.8 0.2 multiply_reduce_fusion
  165.0 0.8 fusion.10
  165.8 0.1 copy.34
  165.9 0.1 copy.33
  165.9 0.1 select_maximum_fusion.3
  166.1 1.2 collective-permute-done.14
  167.3 0.2 subtract_reduce_fusion.5
  167.6 0.1 select_maximum_fusion.2
  167.7 4.3 %collective-permute-done.15 = f32[9,1002]{1,0:T(8,128)S(1)} collective-permute-done((f32[9,1002]{1,0:T(8,128)S(1)}, f32[9,1002]{1,0:T(8,128)S(1)}, u32[]{:S(2)}, u32[]{:S(2)}) %collective-permute-start.15) | collective-permute-done | bytes 36104 | tf_op jit(solution)/shard_map/ppermute | solution.py:48
  171.9 0.2 subtract_reduce_fusion.3
  172.2 0.1 select_maximum_fusion.1
  172.3 4.3 %collective-permute-done.16 = f32[9,1002]{1,0:T(8,128)S(1)} collective-permute-done((f32[9,1002]{1,0:T(8,128)S(1)}, f32[9,1002]{1,0:T(8,128)S(1)}, u32[]{:S(2)}, u32[]{:S(2)}) %collective-permute-start.16) | collective-permute-done | bytes 36104 | tf_op jit(solution)/shard_map/ppermute | solution.py:48
  176.6 0.2 subtract_reduce_fusion.1
  176.9 0.7 collective-permute-start.17
  177.6 4.7 %collective-permute-done.17.other_ref = f32[9,1002]{1,0:T(8,128)S(1)} collective-permute-done((f32[9,1002]{1,0:T(8,128)S(1)}, f32[9,1002]{1,0:T(8,128)S(1)}, u32[]{:S(2)}, u32[]{:S(2)}) %collective-permute-start.17) | collective-permute-done | bytes 36104 | tf_op jit(solution)/shard_map/ppermute | solution.py:48
  182.2 0.9 finish.1
  (57 shorter events, 0.8 us)
Async XLA Ops:
  0.6 155.9 %copy-start = (bf16[384,1000]{0,1:T(8,128)(2,1)S(1)}, bf16[384,1000]{0,1:T(8,128)(2,1)}, u32[]{:S(2)}) copy-start(bf16[384,1000]{0,1:T(8,128)(2,1)} %param.21) | copy-start | bytes 2304004
  2.6 11.6 %copy-start.11 = (bf16[16,2048]{1,0:T(8,128)(2,1)S(1)}, bf16[16,2048]{1,0:T(8,128)(2,1)}, u32[]{:S(2)}) copy-start(bf16[16,2048]{1,0:T(8,128)(2,1)} %get-tuple-element.24) | copy-start | bytes 196612
  2.6 16.3 %copy-start.10 = (bf16[16,4096]{1,0:T(8,128)(2,1)S(1)}, bf16[16,4096]{1,0:T(8,128)(2,1)}, u32[]{:S(2)}) copy-start(bf16[16,4096]{1,0:T(8,128)(2,1)} %get-tuple-element.23) | copy-start | bytes 393220
  2.6 11.6 %collective-permute-start.2 = (bf16[16,4096]{1,0:T(8,128)(2,1)}, bf16[16,4096]{1,0:T(8,128)(2,1)S(1)}, u32[]{:S(2)}, u32[]{:S(2)}) collective-permute-start(bf16[16,4096]{1,0:T(8,128)(2,1)} %get-tuple-element.23), channel_id=1, source_target_pairs={{0,12},{1,13},{2,14},{3,15},{4,8},{5,9},{6,10},{7,11},{8,4},{9,5},... | collective-permute-start | bytes 393224 | tf_op jit(solution)/shard_map/ppermute | solution.py:48
  7.7 11.3 %collective-permute-start.1 = (bf16[16,4096]{1,0:T(8,128)(2,1)}, bf16[16,4096]{1,0:T(8,128)(2,1)S(1)}, u32[]{:S(2)}, u32[]{:S(2)}) collective-permute-start(bf16[16,4096]{1,0:T(8,128)(2,1)} %get-tuple-element.23), channel_id=1, source_target_pairs={{0,8},{1,9},{2,10},{3,11},{4,12},{5,13},{6,14},{7,15},{8,0},{9,1},... | collective-permute-start | bytes 393224 | tf_op jit(solution)/shard_map/ppermute | solution.py:48
  7.7 11.3 %collective-permute-start = (bf16[16,4096]{1,0:T(8,128)(2,1)}, bf16[16,4096]{1,0:T(8,128)(2,1)S(1)}, u32[]{:S(2)}, u32[]{:S(2)}) collective-permute-start(bf16[16,4096]{1,0:T(8,128)(2,1)} %get-tuple-element.23), channel_id=1, source_target_pairs={{0,4},{1,5},{2,6},{3,7},{4,0},{5,1},{6,2},{7,3},{8,12},{9,13},{10,... | collective-permute-start | bytes 393224 | tf_op jit(solution)/shard_map/ppermute | solution.py:48
  8.3 5.9 %collective-permute-start.3 = (bf16[16,2048]{1,0:T(8,128)(2,1)}, bf16[16,2048]{1,0:T(8,128)(2,1)S(1)}, u32[]{:S(2)}, u32[]{:S(2)}) collective-permute-start(bf16[16,2048]{1,0:T(8,128)(2,1)} %get-tuple-element.24), channel_id=1, source_target_pairs={{0,2},{1,3},{2,0},{3,1},{4,6},{5,7},{6,4},{7,5},{8,10},{9,11},{10,... | collective-permute-start | bytes 196616 | tf_op jit(solution)/shard_map/ppermute | solution.py:48
  19.0 13.8 %collective-permute-start.4 = (bf16[4,16,4096]{2,1,0:T(8,128)(2,1)S(1)}, bf16[4,16,4096]{2,1,0:T(8,128)(2,1)S(1)}, u32[]{:S(2)}, u32[]{:S(2)}) collective-permute-start(bf16[4,16,4096]{2,1,0:T(8,128)(2,1)S(1)} %pad_maximum_fusion.refs_0_), channel_id=1, source_target_pairs={{0,2},{1,3},{2,0},{3,1},{4,6},{5,7},{6,4},{7,5},{8,10},{9,11},{10,... | collective-permute-start | bytes 1572872 | tf_op jit(solution)/shard_map/ppermute | solution.py:48
  20.6 6.0 %collective-permute-start.5 = (bf16[2,16,2048]{2,1,0:T(8,128)(2,1)S(1)}, bf16[2,16,2048]{2,1,0:T(8,128)(2,1)S(1)}, u32[]{:S(2)}, u32[]{:S(2)}) collective-permute-start(bf16[2,16,2048]{2,1,0:T(8,128)(2,1)S(1)} %pad_maximum_fusion.1.refs_2_), channel_id=1, source_target_pairs={{0,4},{1,5},{2,6},{3,7},{4,0},{5,1},{6,2},{7,3},{8,12},{9,13},{10,... | collective-permute-start | bytes 393224 | tf_op jit(solution)/shard_map/ppermute | solution.py:48
  20.6 12.2 %collective-permute-start.6 = (bf16[2,16,2048]{2,1,0:T(8,128)(2,1)S(1)}, bf16[2,16,2048]{2,1,0:T(8,128)(2,1)S(1)}, u32[]{:S(2)}, u32[]{:S(2)}) collective-permute-start(bf16[2,16,2048]{2,1,0:T(8,128)(2,1)S(1)} %pad_maximum_fusion.1.refs_2_), channel_id=1, source_target_pairs={{0,8},{1,9},{2,10},{3,11},{4,12},{5,13},{6,14},{7,15},{8,0},{9,1},... | collective-permute-start | bytes 393224 | tf_op jit(solution)/shard_map/ppermute | solution.py:48
  23.7 9.2 %collective-permute-start.7 = (bf16[2,16,2048]{2,1,0:T(8,128)(2,1)S(1)}, bf16[2,16,2048]{2,1,0:T(8,128)(2,1)S(1)}, u32[]{:S(2)}, u32[]{:S(2)}) collective-permute-start(bf16[2,16,2048]{2,1,0:T(8,128)(2,1)S(1)} %pad_maximum_fusion.1.refs_2_), channel_id=1, source_target_pairs={{0,12},{1,13},{2,14},{3,15},{4,8},{5,9},{6,10},{7,11},{8,4},{9,5},... | collective-permute-start | bytes 393224 | tf_op jit(solution)/shard_map/ppermute | solution.py:48
  25.0 10.3 %collective-permute-start.8 = (bf16[4,16,4096]{2,1,0:T(8,128)(2,1)S(1)}, bf16[4,16,4096]{2,1,0:T(8,128)(2,1)S(1)}, u32[]{:S(2)}, u32[]{:S(2)}) collective-permute-start(bf16[4,16,4096]{2,1,0:T(8,128)(2,1)S(1)} %pad_maximum_fusion.refs_0_), channel_id=1, source_target_pairs={{0,1},{1,0},{2,3},{3,2},{4,5},{5,4},{6,7},{7,6},{8,9},{9,8},{10,11... | collective-permute-start | bytes 1572872 | tf_op jit(solution)/shard_map/ppermute | solution.py:48
  32.8 3.8 %collective-permute-start.9 = (bf16[4,16,4096]{2,1,0:T(8,128)(2,1)S(1)}, bf16[4,16,4096]{2,1,0:T(8,128)(2,1)S(1)}, u32[]{:S(2)}, u32[]{:S(2)}) collective-permute-start(bf16[4,16,4096]{2,1,0:T(8,128)(2,1)S(1)} %collective-permute-done.4.refs_1_), channel_id=1, source_target_pairs={{0,1},{1,0},{2,3},{3,2},{4,5},{5,4},{6,7},{7,6},{8,9},{9,8},{10,11... | collective-permute-start | bytes 1572872 | tf_op jit(solution)/shard_map/ppermute | solution.py:48
  32.8 2.3 %collective-permute-start.10 = (bf16[2,16,2048]{2,1,0:T(8,128)(2,1)S(1)}, bf16[2,16,2048]{2,1,0:T(8,128)(2,1)S(1)}, u32[]{:S(2)}, u32[]{:S(2)}) collective-permute-start(bf16[2,16,2048]{2,1,0:T(8,128)(2,1)S(1)} %pad_maximum_fusion.1.refs_2_), channel_id=1, source_target_pairs={{0,1},{1,0},{2,3},{3,2},{4,5},{5,4},{6,7},{7,6},{8,9},{9,8},{10,11... | collective-permute-start | bytes 393224 | tf_op jit(solution)/shard_map/ppermute | solution.py:48
  33.4 1.9 %collective-permute-start.11 = (bf16[2,16,2048]{2,1,0:T(8,128)(2,1)S(1)}, bf16[2,16,2048]{2,1,0:T(8,128)(2,1)}, u32[]{:S(2)}, u32[]{:S(2)}) collective-permute-start(bf16[2,16,2048]{2,1,0:T(8,128)(2,1)S(1)} %collective-permute-done.5.refs_3_), channel_id=1, source_target_pairs={{0,1},{1,0},{2,3},{3,2},{4,5},{5,4},{6,7},{7,6},{8,9},{9,8},{10,11... | collective-permute-start | bytes 393224 | tf_op jit(solution)/shard_map/ppermute | solution.py:48
  33.4 2.0 %collective-permute-start.12 = (bf16[2,16,2048]{2,1,0:T(8,128)(2,1)S(1)}, bf16[2,16,2048]{2,1,0:T(8,128)(2,1)}, u32[]{:S(2)}, u32[]{:S(2)}) collective-permute-start(bf16[2,16,2048]{2,1,0:T(8,128)(2,1)S(1)} %collective-permute-done.6.refs_4_), channel_id=1, source_target_pairs={{0,1},{1,0},{2,3},{3,2},{4,5},{5,4},{6,7},{7,6},{8,9},{9,8},{10,11... | collective-permute-start | bytes 393224 | tf_op jit(solution)/shard_map/ppermute | solution.py:48
  35.1 1.5 collective-permute-start.13
  47.6 27.1 %all-to-all-start = ((bf16[16,8,16,256]{3,2,1,0:T(8,128)(2,1)}), bf16[16,8,16,256]{3,2,1,0:T(8,128)(2,1)S(1)}, u32[]{:S(2)}, u32[]{:S(2)}) async-start(bf16[16,8,16,256]{3,2,1,0:T(8,128)(2,1)} %query_key.2), calls=%async_computation | async-start | bytes 2097152 | tf_op jit(solution)/shard_map/all_to_all | solution.py:560
  59.5 1.2 copy-start.3
  60.7 21.8 %copy-start.12 = (f32[128]{0:T(128)S(1)}, f32[128]{0:T(128)}, u32[]{:S(2)}) copy-start(f32[128]{0:T(128)} %param.16) | copy-start | bytes 1540
  60.7 22.0 %copy-start.13 = (f32[128]{0:T(128)S(1)}, f32[128]{0:T(128)}, u32[]{:S(2)}) copy-start(f32[128]{0:T(128)} %param.17) | copy-start | bytes 1540
  72.3 1.4 copy-start.8
  74.7 1.0 copy-start.6
  75.7 52.1 %all-to-all-start.1 = ((bf16[16,16,16,256]{3,2,1,0:T(8,128)(2,1)}), bf16[16,16,16,256]{3,2,1,0:T(8,128)(2,1)S(1)}, u32[]{:S(2)}, u32[]{:S(2)}) async-start(bf16[16,16,16,256]{3,2,1,0:T(8,128)(2,1)} %bitcast.39), calls=%async_computation.1 | async-start | bytes 4194304 | tf_op jit(solution)/shard_map/all_to_all | solution.py:560
  82.8 1.2 copy-start.7
  85.4 1.9 %copy-start.1 = (bf16[256,6144]{1,0:T(8,128)(2,1)S(1)}, bf16[256,6144]{1,0:T(8,128)(2,1)}, u32[]{:S(2)}) copy-start(bf16[256,6144]{1,0:T(8,128)(2,1)} %place_rows.1.norm_ref) | copy-start | bytes 9437188
  104.9 5.3 %copy-start.2 = (bf16[256,6144]{1,0:T(8,128)(2,1)S(1)}, bf16[256,6144]{1,0:T(8,128)(2,1)}, u32[]{:S(2)}) copy-start(bf16[256,6144]{1,0:T(8,128)(2,1)} %place_rows.1.norm_ref) | copy-start | bytes 9437188
  130.9 16.1 %all-to-all-start.2 = ((bf16[16,24,256]{2,1,0:T(8,128)(2,1)}), bf16[16,24,256]{2,1,0:T(8,128)(2,1)S(1)}, u32[]{:S(2)}, u32[]{:S(2)}) async-start(bf16[16,24,256]{2,1,0:T(8,128)(2,1)} %key_weights.3), calls=%async_computation.2 | async-start | bytes 393216 | tf_op jit(solution)/shard_map/all_to_all | solution.py:580
  138.0 9.0 %copy-start.4 = (bf16[8,256,384]{2,1,0:T(8,128)(2,1)S(1)}, bf16[8,256,384]{2,1,0:T(8,128)(2,1)}, u32[]{:S(2)}) copy-start(bf16[8,256,384]{2,1,0:T(8,128)(2,1)} %copy-done.3) | copy-start | bytes 4718596
  138.0 9.0 %copy-start.9 = (bf16[16,6144]{1,0:T(8,128)(2,1)S(1)}, bf16[16,6144]{1,0:T(8,128)(2,1)}, u32[]{:S(2)}) copy-start(bf16[16,6144]{1,0:T(8,128)(2,1)} %token_ref.1) | copy-start | bytes 589828
  147.0 2.3 %copy-start.5 = (bf16[8,48,6144]{2,1,0:T(8,128)(2,1)S(1)}, bf16[8,48,6144]{2,1,0:T(8,128)(2,1)}, u32[]{:S(2)}) copy-start(bf16[8,48,6144]{2,1,0:T(8,128)(2,1)} %param.18) | copy-start | bytes 14155780
  152.2 12.5 %all-to-all-start.3 = ((f32[16,8,384]{2,1,0:T(8,128)}), f32[16,8,384]{2,1,0:T(8,128)S(1)}, u32[]{:S(2)}, u32[]{:S(2)}) async-start(f32[16,8,384]{2,1,0:T(8,128)} %feature_part.1), calls=%async_computation.3 | async-start | bytes 393216 | tf_op jit(solution)/shard_map/all_to_all | solution.py:586
  166.0 1.3 collective-permute-start.14
  167.6 4.3 %collective-permute-start.15 = (f32[9,1002]{1,0:T(8,128)S(1)}, f32[9,1002]{1,0:T(8,128)S(1)}, u32[]{:S(2)}, u32[]{:S(2)}) collective-permute-start(f32[9,1002]{1,0:T(8,128)S(1)} %select_maximum_fusion.2), channel_id=1, source_target_pairs={{0,2},{1,3},{2,0},{3,1},{4,6},{5,7},{6,4},{7,5},{8,10},{9,11},{10,... | collective-permute-start | bytes 108224 | tf_op jit(solution)/shard_map/ppermute | solution.py:48
  172.3 4.3 %collective-permute-start.16 = (f32[9,1002]{1,0:T(8,128)S(1)}, f32[9,1002]{1,0:T(8,128)S(1)}, u32[]{:S(2)}, u32[]{:S(2)}) collective-permute-start(f32[9,1002]{1,0:T(8,128)S(1)} %select_maximum_fusion.1), channel_id=1, source_target_pairs={{0,4},{1,5},{2,6},{3,7},{4,0},{5,1},{6,2},{7,3},{8,12},{9,13},{10,... | collective-permute-start | bytes 108224 | tf_op jit(solution)/shard_map/ppermute | solution.py:48
  176.9 5.3 %collective-permute-start.17 = (f32[9,1002]{1,0:T(8,128)S(1)}, f32[9,1002]{1,0:T(8,128)S(1)}, u32[]{:S(2)}, u32[]{:S(2)}) collective-permute-start(f32[9,1002]{1,0:T(8,128)S(1)} %select_maximum_fusion.mine_ref), channel_id=1, source_target_pairs={{0,8},{1,9},{2,10},{3,11},{4,12},{5,13},{6,14},{7,15},{8,0},{9,1},... | collective-permute-start | bytes 108224 | tf_op jit(solution)/shard_map/ppermute | solution.py:48

commit v4 on v3

--- a/solution.py
+++ b/solution.py
@@ -459,7 +459,7 @@
         ],
         out_specs=pl.BlockSpec((parts // steps, samples, width // parts), lambda i: (i, 0, 0)),
         scratch_shapes=[pltpu.VMEM((16, columns), BF16)],
-        compiler_params=pltpu.CompilerParams(vmem_limit_bytes=40 * MIB),
+        compiler_params=pltpu.CompilerParams(vmem_limit_bytes=60 * MIB),
         cost_estimate=pl.CostEstimate(
             flops=2 * samples * rows * columns * 2 + 32 * columns * width,
             bytes_accessed=2 * columns * width + 2 * value.size,
@@ -579,7 +579,7 @@
     hidden = hidden + down_part(more_pooled, w_down, tiles)
     key_mean = lax.all_to_all(key_mean, "inp", split_axis=0, concat_axis=0, tiled=True)
     partial_feature = feature_part(
-        key_mean, value, w_proj.reshape(n_comps * n_heads, model_width), hidden, tokens, 4
+        key_mean, value, w_proj.reshape(n_comps * n_heads, model_width), hidden, tokens, 8
     )
     slice_width = model_width // n_parts
     feature = jnp.sum(

time: 184 us -> 187 us (1.016)
  Pallas kernels: 85.9 us -> 90.6 us
    pallas_call x1, Pallas kernels: 2.83 us -> 7.63 us  [feature_part(): pl.pallas_call(feature_kernel, grid=(steps,), out_shape=jax.ShapeDtypeStr...]
    unnamed x29 -> x25, local copies, waits for them, and re-layouts: 10.4 us -> 8.69 us
  transfers between devices with their start and end apart: 22 -> 22, of which waited for: 13 -> 13; matrix products, arithmetic and copies ran while one was open for 3% -> 4% of each run, Pallas kernels for 36% -> 35%
where the time goes in v4:
time: 187 us; the launch traced here: 186 us
  Pallas kernels  90.6 us (48%)
  waiting for transfers between devices  41.3 us (22%)
  starting transfers between devices  36.9 us (20%)
  local copies, waits for them, and re-layouts  9.91 us (5%)
  matrix products  4.15 us (2%)
  other arithmetic  2.45 us (1%)
    pallas_call x2, Pallas kernels, hidden_part(): pl.pallas_call(hidden_kernel, grid=(tiles, width // depth), out_shape=jax...  35.1 us
    ppermute x18, waiting for transfers between devices, permuted(): return lax.ppermute(array, 'inp', [(i, i ^ bits) for i in range(count)])  29.5 us
    pallas_call x2, Pallas kernels, query_key(): pl.pallas_call(query_key_kernel, grid=(width // depth,), out_shape=jax.Sh...  19.7 us
    ppermute x18, starting transfers between devices, permuted(): return lax.ppermute(array, 'inp', [(i, i ^ bits) for i in range(count)])  15.2 us
    all_to_all x2, starting transfers between devices, exchange(): return lax.all_to_all(array, 'inp', split_axis=0, concat_axis=0, tiled=True)  11.1 us
    pallas_call x2, Pallas kernels, down_part(): pl.pallas_call(down_kernel, grid=(units // UNITS,), out_shape=jax.ShapeDt...  10.2 us
    unnamed x25, local copies, waits for them, and re-layouts  8.69 us
    pallas_call x1, Pallas kernels, values_of(): pl.pallas_call(value_kernel, grid=(width // depth,), out_shape=jax.ShapeD...  7.74 us
  transfers between devices with their start and end apart: 22, of which 13 were waited for; matrix products, arithmetic and copies ran while one was open for 4% of the time, Pallas kernels for 35%

profile of v4, /device:TPU:0, one launch (start us, length us, event | category | flops | bytes accessed | tf_op | source)
XLA Modules:
  0.0 186.2 jit_solution(8722809082063848193)
XLA Ops:
  0.6 2.0 %own_norm.1 = (bf16[16,4096]{1,0:T(8,128)(2,1)}, bf16[16,2048]{1,0:T(8,128)(2,1)}) custom-call(bf16[16,6144]{1,0:T(8,128)(2,1)} %token_ref.1, f32[1,6144]{1,0:T(1,128)} %bitcast.51), custom_call_target="tpu_custom_call" | custom-call | tf_op jit(solution)/shard_map/own_norm/pallas_call | solution.py:61
  2.6 5.0 %collective-permute-start.2 = (bf16[16,4096]{1,0:T(8,128)(2,1)}, bf16[16,4096]{1,0:T(8,128)(2,1)S(1)}, u32[]{:S(2)}, u32[]{:S(2)}) collective-permute-start(bf16[16,4096]{1,0:T(8,128)(2,1)} %get-tuple-element.23), channel_id=1, source_target_pairs={{0,12},{1,13},{2,14},{3,15},{4,8},{5,9},{6,10},{7,11},{8,4},{9,5},... | collective-permute-start | bytes 393224 | tf_op jit(solution)/shard_map/ppermute | solution.py:48
  7.7 0.6 collective-permute-start
  8.3 1.7 collective-permute-start.3
  10.0 1.3 copy.25
  11.5 0.1 broadcast_compare_fusion
  11.6 2.7 %fusion.choose_ref = bf16[16,128,768]{2,1,0:T(8,128)(2,1)} fusion(pred[128,768]{1,0:T(8,128)(4,1)S(1)} %broadcast_compare_fusion, bf16[16,128,48]{2,1,0:T(8,128)(2,1)S(1)} %bitcast.41, s32[768]{0:T(1024)S(1)} %add_select_fusion), kind=kOutput, calls=%fused_computation.1 | convolution fusion | flops 155750400 | bytes 3443712 | tf_op jit(solution)/shard_map/trb,bc->trc/dot_general | solution.py:130
  14.3 4.7 %collective-permute-done.1 = bf16[16,4096]{1,0:T(8,128)(2,1)S(1)} collective-permute-done((bf16[16,4096]{1,0:T(8,128)(2,1)}, bf16[16,4096]{1,0:T(8,128)(2,1)S(1)}, u32[]{:S(2)}, u32[]{:S(2)}) %collective-permute-start.1) | collective-permute-done | bytes 131104 | tf_op jit(solution)/shard_map/ppermute | solution.py:48
  19.0 1.6 collective-permute-start.4
  20.6 3.0 %collective-permute-start.6 = (bf16[2,16,2048]{2,1,0:T(8,128)(2,1)S(1)}, bf16[2,16,2048]{2,1,0:T(8,128)(2,1)S(1)}, u32[]{:S(2)}, u32[]{:S(2)}) collective-permute-start(bf16[2,16,2048]{2,1,0:T(8,128)(2,1)S(1)} %pad_maximum_fusion.1.refs_2_), channel_id=1, source_target_pairs={{0,8},{1,9},{2,10},{3,11},{4,12},{5,13},{6,14},{7,15},{8,0},{9,1},... | collective-permute-start | bytes 393224 | tf_op jit(solution)/shard_map/ppermute | solution.py:48
  23.7 1.3 collective-permute-start.7
  25.0 1.6 collective-permute-done.5.refs_3_
  26.6 6.3 %collective-permute-done.6.refs_4_ = bf16[2,16,2048]{2,1,0:T(8,128)(2,1)S(1)} collective-permute-done((bf16[2,16,2048]{2,1,0:T(8,128)(2,1)S(1)}, bf16[2,16,2048]{2,1,0:T(8,128)(2,1)S(1)}, u32[]{:S(2)}, u32[]{:S(2)}) %collective-permute-start.6) | collective-permute-done | bytes 131104 | tf_op jit(solution)/shard_map/ppermute | solution.py:48
  32.8 0.5 collective-permute-start.10
  33.4 0.4 collective-permute-start.12
  33.9 1.3 collective-permute-done.10.refs_8_
  35.1 0.1 collective-permute-start.13
  35.3 0.2 collective-permute-done.12.refs_10_
  35.4 1.2 collective-permute-done.13.refs_11_
  36.6 2.9 %place_rows.1.norm_ref = bf16[256,6144]{1,0:T(8,128)(2,1)} custom-call(s32[1]{0:T(128)} %bitcast.me_ref, bf16[4,16,4096]{2,1,0:T(8,128)(2,1)S(1)} %pad_maximum_fusion.refs_0_, bf16[4,16,4096]{2,1,0:T(8,128)(2,1)S(1)} %collective-permute-done.4.refs_1_, bf16[2,16,2048]{2,1,0:T(8,128)(2,1)S(1)} %pad_maximum_fusion.1.refs_2_, ...), custom_call_target="tpu_custom_call" | custom-call | tf_op jit(solution)/shard_map/place_rows/pallas_call | solution.py:106
  39.5 8.1 %query_key.2 = bf16[16,8,16,256]{3,2,1,0:T(8,128)(2,1)} custom-call(bf16[256,6144]{1,0:T(8,128)(2,1)} %place_rows.1.norm_ref, bf16[16,128,768]{2,1,0:T(8,128)(2,1)} %fusion.choose_ref, bf16[8,3,48,6144]{3,2,1,0:T(8,128)(2,1)} %w_ref.5), custom_call_target="tpu_custom_call" | custom-call | flops 3221225472 | bytes 9437184 | tf_op jit(solution)/shard_map/query_key/pallas_call | solution.py:186
  47.6 4.2 %all-to-all-start = ((bf16[16,8,16,256]{3,2,1,0:T(8,128)(2,1)}), bf16[16,8,16,256]{3,2,1,0:T(8,128)(2,1)S(1)}, u32[]{:S(2)}, u32[]{:S(2)}) async-start(bf16[16,8,16,256]{3,2,1,0:T(8,128)(2,1)} %query_key.2), calls=%async_computation | async-start | bytes 2097152 | tf_op jit(solution)/shard_map/all_to_all | solution.py:560
  51.8 7.7 %value_rows.1.value_ref = bf16[8,256,384]{2,1,0:T(8,128)(2,1)S(1)} custom-call(bf16[256,6144]{1,0:T(8,128)(2,1)} %place_rows.1.norm_ref, bf16[16,128,768]{2,1,0:T(8,128)(2,1)} %fusion.choose_ref, bf16[8,3,48,6144]{3,2,1,0:T(8,128)(2,1)} %w_ref.5), custom_call_target="tpu_custom_call" | custom-call | flops 4831838208 | bytes 11010048 | tf_op jit(solution)/shard_map/value_rows/pallas_call | solution.py:236
  59.6 1.2 copy-done.3
  60.8 11.6 %query_key.3 = bf16[32,8,16,256]{3,2,1,0:T(8,128)(2,1)S(1)} custom-call(bf16[256,6144]{1,0:T(8,128)(2,1)} %place_rows.1.norm_ref, bf16[16,128,768]{2,1,0:T(8,128)(2,1)} %fusion.choose_ref, bf16[8,3,48,6144]{3,2,1,0:T(8,128)(2,1)} %w_ref.5), custom_call_target="tpu_custom_call" | custom-call | flops 6442450944 | bytes 12582912 | tf_op jit(solution)/shard_map/query_key/pallas_call | solution.py:186
  72.4 1.4 copy-done.6
  73.7 1.0 all-to-all-done.x_ref
  74.8 1.0 copy-done.4
  75.7 6.9 %all-to-all-start.1 = ((bf16[16,16,16,256]{3,2,1,0:T(8,128)(2,1)}), bf16[16,16,16,256]{3,2,1,0:T(8,128)(2,1)S(1)}, u32[]{:S(2)}, u32[]{:S(2)}) async-start(bf16[16,16,16,256]{3,2,1,0:T(8,128)(2,1)} %bitcast.38), calls=%async_computation.1 | async-start | bytes 4194304 | tf_op jit(solution)/shard_map/all_to_all | solution.py:560
  82.6 0.1 copy.29.query_gain_ref
  82.7 0.1 copy.30.key_gain_ref
  82.8 1.2 copy-done.5
  84.1 1.4 key_weights.2.refs_0_
  85.4 1.9 %copy-done.1 = bf16[256,6144]{1,0:T(8,128)(2,1)S(1)} copy-done((bf16[256,6144]{1,0:T(8,128)(2,1)S(1)}, bf16[256,6144]{1,0:T(8,128)(2,1)}, u32[]{:S(2)}) %copy-start.1) | copy-done | bytes 3145752
  87.3 17.5 %hidden_part.2.pooled_ref = f32[8,768]{1,0:T(8,128)S(1)} custom-call(bf16[256,6144]{1,0:T(8,128)(2,1)S(1)} %copy-done.1, bf16[16,128,768]{2,1,0:T(8,128)(2,1)} %fusion.choose_ref, bf16[1536,6144]{1,0:T(8,128)(2,1)} %up_ref.3), custom_call_target="tpu_custom_call" | custom-call | flops 9663676416 | bytes 15728640 | tf_op jit(solution)/shard_map/hidden_part/pallas_call | solution.py:295
  104.9 5.3 %down_part.2 = f32[8,6144]{1,0:T(8,128)S(1)} custom-call(f32[8,768]{1,0:T(8,128)S(1)} %hidden_part.2.pooled_ref, bf16[1536,6144]{1,0:T(8,128)(2,1)} %down_ref.3), custom_call_target="tpu_custom_call" | custom-call | flops 150994944 | bytes 9437184 | tf_op jit(solution)/shard_map/down_part/pallas_call | solution.py:334
  110.2 17.6 %hidden_part.3.pooled_ref = f32[8,768]{1,0:T(8,128)S(1)} custom-call(bf16[256,6144]{1,0:T(8,128)(2,1)S(1)} %copy-done.2, bf16[16,128,768]{2,1,0:T(8,128)(2,1)} %fusion.choose_ref, bf16[1536,6144]{1,0:T(8,128)(2,1)} %up_ref.3), custom_call_target="tpu_custom_call" | custom-call | flops 9663676416 | bytes 15728640 | tf_op jit(solution)/shard_map/hidden_part/pallas_call | solution.py:295
  127.8 3.1 %key_weights.3 = bf16[16,24,256]{2,1,0:T(8,128)(2,1)} custom-call(bf16[16,16,16,256]{3,2,1,0:T(8,128)(2,1)S(1)} %all-to-all-done.1.x_ref, f32[128,1]{1,0:T(8,128)S(1)} %copy.29.query_gain_ref, f32[128,1]{1,0:T(8,128)S(1)} %copy.30.key_gain_ref, f32[8,256]{1,0:T(8,128)S(1)} %key_weights.2.refs_0_), custom_call_target="tpu_custom_call" | custom-call | flops 268435456 | bytes 2097152 | tf_op jit(solution)/shard_map/key_weights/pallas_call | solution.py:393
  130.9 7.1 %all-to-all-start.2 = ((bf16[16,24,256]{2,1,0:T(8,128)(2,1)}), bf16[16,24,256]{2,1,0:T(8,128)(2,1)S(1)}, u32[]{:S(2)}, u32[]{:S(2)}) async-start(bf16[16,24,256]{2,1,0:T(8,128)(2,1)} %key_weights.3), calls=%async_computation.2 | async-start | bytes 393216 | tf_op jit(solution)/shard_map/all_to_all | solution.py:580
  138.1 5.0 %down_part.3 = f32[8,6144]{1,0:T(8,128)S(1)} custom-call(f32[8,768]{1,0:T(8,128)S(1)} %hidden_part.3.pooled_ref, bf16[1536,6144]{1,0:T(8,128)(2,1)} %down_ref.3), custom_call_target="tpu_custom_call" | custom-call | flops 150994944 | bytes 9437184 | tf_op jit(solution)/shard_map/down_part/pallas_call | solution.py:334
  143.0 0.7 add.107.hidden_ref
  143.7 3.3 %all-to-all-done.2.key_ref = bf16[16,24,256]{2,1,0:T(8,128)(2,1)S(1)} async-done(((bf16[16,24,256]{2,1,0:T(8,128)(2,1)}), bf16[16,24,256]{2,1,0:T(8,128)(2,1)S(1)}, u32[]{:S(2)}, u32[]{:S(2)}) %all-to-all-start.2) | async-done | bytes 196640 | tf_op jit(solution)/shard_map/all_to_all | solution.py:580
  147.0 0.7 copy-done.7
  147.7 7.6 %feature_part.1 = f32[16,8,384]{2,1,0:T(8,128)} custom-call(bf16[16,24,256]{2,1,0:T(8,128)(2,1)} %copy-done.7, bf16[8,256,384]{2,1,0:T(8,128)(2,1)} %copy-done.3, bf16[384,6144]{1,0:T(8,128)(2,1)} %bitcast.39, f32[8,6144]{1,0:T(8,128)} %add.107.hidden_ref, bf16[16,6144]{1,0:T(8,128)(2,1)} %token_ref.1), custom_call_target="tpu_custom_call" | custom-call | flops 78643200 | bytes 6291456 | tf_op jit(solution)/shard_map/feature_part/pallas_call | solution.py:449
  155.3 3.5 %all-to-all-start.3 = ((f32[16,8,384]{2,1,0:T(8,128)}), f32[16,8,384]{2,1,0:T(8,128)S(1)}, u32[]{:S(2)}, u32[]{:S(2)}) async-start(f32[16,8,384]{2,1,0:T(8,128)} %feature_part.1), calls=%async_computation.3 | async-start | bytes 393216 | tf_op jit(solution)/shard_map/all_to_all | solution.py:586
  158.9 0.8 dynamic_slice.3
  159.7 0.7 fusion.28
  160.4 7.4 %all-to-all-done.3 = f32[16,8,384]{2,1,0:T(8,128)S(1)} async-done(((f32[16,8,384]{2,1,0:T(8,128)}), f32[16,8,384]{2,1,0:T(8,128)S(1)}, u32[]{:S(2)}, u32[]{:S(2)}) %all-to-all-start.3) | async-done | bytes 196640 | tf_op jit(solution)/shard_map/all_to_all | solution.py:586
  167.8 0.2 fusion.24
  168.0 0.2 multiply_reduce_fusion
  168.2 0.8 fusion.10
  168.9 0.1 copy.34
  169.0 0.1 copy.33
  169.1 0.1 select_maximum_fusion.3
  169.2 1.2 collective-permute-done.14
  170.5 0.2 subtract_reduce_fusion.5
  170.7 0.1 select_maximum_fusion.2
  170.8 4.3 %collective-permute-done.15 = f32[9,1002]{1,0:T(8,128)S(1)} collective-permute-done((f32[9,1002]{1,0:T(8,128)S(1)}, f32[9,1002]{1,0:T(8,128)S(1)}, u32[]{:S(2)}, u32[]{:S(2)}) %collective-permute-start.15) | collective-permute-done | bytes 36104 | tf_op jit(solution)/shard_map/ppermute | solution.py:48
  175.1 0.2 subtract_reduce_fusion.3
  175.5 4.3 %collective-permute-done.16 = f32[9,1002]{1,0:T(8,128)S(1)} collective-permute-done((f32[9,1002]{1,0:T(8,128)S(1)}, f32[9,1002]{1,0:T(8,128)S(1)}, u32[]{:S(2)}, u32[]{:S(2)}) %collective-permute-start.16) | collective-permute-done | bytes 36104 | tf_op jit(solution)/shard_map/ppermute | solution.py:48
  179.7 0.2 subtract_reduce_fusion.1
  180.1 0.7 collective-permute-start.17
  180.7 4.7 %collective-permute-done.17.other_ref = f32[9,1002]{1,0:T(8,128)S(1)} collective-permute-done((f32[9,1002]{1,0:T(8,128)S(1)}, f32[9,1002]{1,0:T(8,128)S(1)}, u32[]{:S(2)}, u32[]{:S(2)}) %collective-permute-start.17) | collective-permute-done | bytes 36104 | tf_op jit(solution)/shard_map/ppermute | solution.py:48
  185.4 0.9 finish.1
  (53 shorter events, 0.8 us)
Async XLA Ops:
  0.6 159.0 %copy-start = (bf16[384,1000]{0,1:T(8,128)(2,1)S(1)}, bf16[384,1000]{0,1:T(8,128)(2,1)}, u32[]{:S(2)}) copy-start(bf16[384,1000]{0,1:T(8,128)(2,1)} %param.21) | copy-start | bytes 2304004
  2.6 11.6 %copy-start.9 = (bf16[16,2048]{1,0:T(8,128)(2,1)S(1)}, bf16[16,2048]{1,0:T(8,128)(2,1)}, u32[]{:S(2)}) copy-start(bf16[16,2048]{1,0:T(8,128)(2,1)} %get-tuple-element.24) | copy-start | bytes 196612
  2.6 16.3 %copy-start.8 = (bf16[16,4096]{1,0:T(8,128)(2,1)S(1)}, bf16[16,4096]{1,0:T(8,128)(2,1)}, u32[]{:S(2)}) copy-start(bf16[16,4096]{1,0:T(8,128)(2,1)} %get-tuple-element.23) | copy-start | bytes 393220
  2.6 11.6 %collective-permute-start.2 = (bf16[16,4096]{1,0:T(8,128)(2,1)}, bf16[16,4096]{1,0:T(8,128)(2,1)S(1)}, u32[]{:S(2)}, u32[]{:S(2)}) collective-permute-start(bf16[16,4096]{1,0:T(8,128)(2,1)} %get-tuple-element.23), channel_id=1, source_target_pairs={{0,12},{1,13},{2,14},{3,15},{4,8},{5,9},{6,10},{7,11},{8,4},{9,5},... | collective-permute-start | bytes 393224 | tf_op jit(solution)/shard_map/ppermute | solution.py:48
  7.7 11.3 %collective-permute-start.1 = (bf16[16,4096]{1,0:T(8,128)(2,1)}, bf16[16,4096]{1,0:T(8,128)(2,1)S(1)}, u32[]{:S(2)}, u32[]{:S(2)}) collective-permute-start(bf16[16,4096]{1,0:T(8,128)(2,1)} %get-tuple-element.23), channel_id=1, source_target_pairs={{0,8},{1,9},{2,10},{3,11},{4,12},{5,13},{6,14},{7,15},{8,0},{9,1},... | collective-permute-start | bytes 393224 | tf_op jit(solution)/shard_map/ppermute | solution.py:48
  7.7 11.3 %collective-permute-start = (bf16[16,4096]{1,0:T(8,128)(2,1)}, bf16[16,4096]{1,0:T(8,128)(2,1)S(1)}, u32[]{:S(2)}, u32[]{:S(2)}) collective-permute-start(bf16[16,4096]{1,0:T(8,128)(2,1)} %get-tuple-element.23), channel_id=1, source_target_pairs={{0,4},{1,5},{2,6},{3,7},{4,0},{5,1},{6,2},{7,3},{8,12},{9,13},{10,... | collective-permute-start | bytes 393224 | tf_op jit(solution)/shard_map/ppermute | solution.py:48
  8.3 5.9 %collective-permute-start.3 = (bf16[16,2048]{1,0:T(8,128)(2,1)}, bf16[16,2048]{1,0:T(8,128)(2,1)S(1)}, u32[]{:S(2)}, u32[]{:S(2)}) collective-permute-start(bf16[16,2048]{1,0:T(8,128)(2,1)} %get-tuple-element.24), channel_id=1, source_target_pairs={{0,2},{1,3},{2,0},{3,1},{4,6},{5,7},{6,4},{7,5},{8,10},{9,11},{10,... | collective-permute-start | bytes 196616 | tf_op jit(solution)/shard_map/ppermute | solution.py:48
  19.0 13.8 %collective-permute-start.4 = (bf16[4,16,4096]{2,1,0:T(8,128)(2,1)S(1)}, bf16[4,16,4096]{2,1,0:T(8,128)(2,1)S(1)}, u32[]{:S(2)}, u32[]{:S(2)}) collective-permute-start(bf16[4,16,4096]{2,1,0:T(8,128)(2,1)S(1)} %pad_maximum_fusion.refs_0_), channel_id=1, source_target_pairs={{0,2},{1,3},{2,0},{3,1},{4,6},{5,7},{6,4},{7,5},{8,10},{9,11},{10,... | collective-permute-start | bytes 1572872 | tf_op jit(solution)/shard_map/ppermute | solution.py:48
  20.6 6.0 %collective-permute-start.5 = (bf16[2,16,2048]{2,1,0:T(8,128)(2,1)S(1)}, bf16[2,16,2048]{2,1,0:T(8,128)(2,1)S(1)}, u32[]{:S(2)}, u32[]{:S(2)}) collective-permute-start(bf16[2,16,2048]{2,1,0:T(8,128)(2,1)S(1)} %pad_maximum_fusion.1.refs_2_), channel_id=1, source_target_pairs={{0,4},{1,5},{2,6},{3,7},{4,0},{5,1},{6,2},{7,3},{8,12},{9,13},{10,... | collective-permute-start | bytes 393224 | tf_op jit(solution)/shard_map/ppermute | solution.py:48
  20.6 12.2 %collective-permute-start.6 = (bf16[2,16,2048]{2,1,0:T(8,128)(2,1)S(1)}, bf16[2,16,2048]{2,1,0:T(8,128)(2,1)S(1)}, u32[]{:S(2)}, u32[]{:S(2)}) collective-permute-start(bf16[2,16,2048]{2,1,0:T(8,128)(2,1)S(1)} %pad_maximum_fusion.1.refs_2_), channel_id=1, source_target_pairs={{0,8},{1,9},{2,10},{3,11},{4,12},{5,13},{6,14},{7,15},{8,0},{9,1},... | collective-permute-start | bytes 393224 | tf_op jit(solution)/shard_map/ppermute | solution.py:48
  23.7 9.2 %collective-permute-start.7 = (bf16[2,16,2048]{2,1,0:T(8,128)(2,1)S(1)}, bf16[2,16,2048]{2,1,0:T(8,128)(2,1)S(1)}, u32[]{:S(2)}, u32[]{:S(2)}) collective-permute-start(bf16[2,16,2048]{2,1,0:T(8,128)(2,1)S(1)} %pad_maximum_fusion.1.refs_2_), channel_id=1, source_target_pairs={{0,12},{1,13},{2,14},{3,15},{4,8},{5,9},{6,10},{7,11},{8,4},{9,5},... | collective-permute-start | bytes 393224 | tf_op jit(solution)/shard_map/ppermute | solution.py:48
  25.0 10.3 %collective-permute-start.8 = (bf16[4,16,4096]{2,1,0:T(8,128)(2,1)S(1)}, bf16[4,16,4096]{2,1,0:T(8,128)(2,1)S(1)}, u32[]{:S(2)}, u32[]{:S(2)}) collective-permute-start(bf16[4,16,4096]{2,1,0:T(8,128)(2,1)S(1)} %pad_maximum_fusion.refs_0_), channel_id=1, source_target_pairs={{0,1},{1,0},{2,3},{3,2},{4,5},{5,4},{6,7},{7,6},{8,9},{9,8},{10,11... | collective-permute-start | bytes 1572872 | tf_op jit(solution)/shard_map/ppermute | solution.py:48
  32.8 3.8 %collective-permute-start.9 = (bf16[4,16,4096]{2,1,0:T(8,128)(2,1)S(1)}, bf16[4,16,4096]{2,1,0:T(8,128)(2,1)S(1)}, u32[]{:S(2)}, u32[]{:S(2)}) collective-permute-start(bf16[4,16,4096]{2,1,0:T(8,128)(2,1)S(1)} %collective-permute-done.4.refs_1_), channel_id=1, source_target_pairs={{0,1},{1,0},{2,3},{3,2},{4,5},{5,4},{6,7},{7,6},{8,9},{9,8},{10,11... | collective-permute-start | bytes 1572872 | tf_op jit(solution)/shard_map/ppermute | solution.py:48
  32.8 2.3 %collective-permute-start.10 = (bf16[2,16,2048]{2,1,0:T(8,128)(2,1)S(1)}, bf16[2,16,2048]{2,1,0:T(8,128)(2,1)S(1)}, u32[]{:S(2)}, u32[]{:S(2)}) collective-permute-start(bf16[2,16,2048]{2,1,0:T(8,128)(2,1)S(1)} %pad_maximum_fusion.1.refs_2_), channel_id=1, source_target_pairs={{0,1},{1,0},{2,3},{3,2},{4,5},{5,4},{6,7},{7,6},{8,9},{9,8},{10,11... | collective-permute-start | bytes 393224 | tf_op jit(solution)/shard_map/ppermute | solution.py:48
  33.4 1.9 %collective-permute-start.11 = (bf16[2,16,2048]{2,1,0:T(8,128)(2,1)S(1)}, bf16[2,16,2048]{2,1,0:T(8,128)(2,1)}, u32[]{:S(2)}, u32[]{:S(2)}) collective-permute-start(bf16[2,16,2048]{2,1,0:T(8,128)(2,1)S(1)} %collective-permute-done.5.refs_3_), channel_id=1, source_target_pairs={{0,1},{1,0},{2,3},{3,2},{4,5},{5,4},{6,7},{7,6},{8,9},{9,8},{10,11... | collective-permute-start | bytes 393224 | tf_op jit(solution)/shard_map/ppermute | solution.py:48
  33.4 2.0 %collective-permute-start.12 = (bf16[2,16,2048]{2,1,0:T(8,128)(2,1)S(1)}, bf16[2,16,2048]{2,1,0:T(8,128)(2,1)}, u32[]{:S(2)}, u32[]{:S(2)}) collective-permute-start(bf16[2,16,2048]{2,1,0:T(8,128)(2,1)S(1)} %collective-permute-done.6.refs_4_), channel_id=1, source_target_pairs={{0,1},{1,0},{2,3},{3,2},{4,5},{5,4},{6,7},{7,6},{8,9},{9,8},{10,11... | collective-permute-start | bytes 393224 | tf_op jit(solution)/shard_map/ppermute | solution.py:48
  35.1 1.5 collective-permute-start.13
  47.6 27.2 %all-to-all-start = ((bf16[16,8,16,256]{3,2,1,0:T(8,128)(2,1)}), bf16[16,8,16,256]{3,2,1,0:T(8,128)(2,1)S(1)}, u32[]{:S(2)}, u32[]{:S(2)}) async-start(bf16[16,8,16,256]{3,2,1,0:T(8,128)(2,1)} %query_key.2), calls=%async_computation | async-start | bytes 2097152 | tf_op jit(solution)/shard_map/all_to_all | solution.py:560
  59.6 1.2 copy-start.3
  60.8 21.8 %copy-start.10 = (f32[128]{0:T(128)S(1)}, f32[128]{0:T(128)}, u32[]{:S(2)}) copy-start(f32[128]{0:T(128)} %param.16) | copy-start | bytes 1540
  60.8 21.9 %copy-start.11 = (f32[128]{0:T(128)S(1)}, f32[128]{0:T(128)}, u32[]{:S(2)}) copy-start(f32[128]{0:T(128)} %param.17) | copy-start | bytes 1540
  72.4 1.4 copy-start.6
  74.8 1.0 copy-start.4
  75.7 52.1 %all-to-all-start.1 = ((bf16[16,16,16,256]{3,2,1,0:T(8,128)(2,1)}), bf16[16,16,16,256]{3,2,1,0:T(8,128)(2,1)S(1)}, u32[]{:S(2)}, u32[]{:S(2)}) async-start(bf16[16,16,16,256]{3,2,1,0:T(8,128)(2,1)} %bitcast.38), calls=%async_computation.1 | async-start | bytes 4194304 | tf_op jit(solution)/shard_map/all_to_all | solution.py:560
  82.8 1.2 copy-start.5
  85.4 1.9 %copy-start.1 = (bf16[256,6144]{1,0:T(8,128)(2,1)S(1)}, bf16[256,6144]{1,0:T(8,128)(2,1)}, u32[]{:S(2)}) copy-start(bf16[256,6144]{1,0:T(8,128)(2,1)} %place_rows.1.norm_ref) | copy-start | bytes 9437188
  104.9 5.3 %copy-start.2 = (bf16[256,6144]{1,0:T(8,128)(2,1)S(1)}, bf16[256,6144]{1,0:T(8,128)(2,1)}, u32[]{:S(2)}) copy-start(bf16[256,6144]{1,0:T(8,128)(2,1)} %place_rows.1.norm_ref) | copy-start | bytes 9437188
  130.9 16.1 %all-to-all-start.2 = ((bf16[16,24,256]{2,1,0:T(8,128)(2,1)}), bf16[16,24,256]{2,1,0:T(8,128)(2,1)S(1)}, u32[]{:S(2)}, u32[]{:S(2)}) async-start(bf16[16,24,256]{2,1,0:T(8,128)(2,1)} %key_weights.3), calls=%async_computation.2 | async-start | bytes 393216 | tf_op jit(solution)/shard_map/all_to_all | solution.py:580
  147.0 0.7 copy-start.7
  155.3 12.5 %all-to-all-start.3 = ((f32[16,8,384]{2,1,0:T(8,128)}), f32[16,8,384]{2,1,0:T(8,128)S(1)}, u32[]{:S(2)}, u32[]{:S(2)}) async-start(f32[16,8,384]{2,1,0:T(8,128)} %feature_part.1), calls=%async_computation.3 | async-start | bytes 393216 | tf_op jit(solution)/shard_map/all_to_all | solution.py:586
  169.2 1.3 collective-permute-start.14
  170.8 4.3 %collective-permute-start.15 = (f32[9,1002]{1,0:T(8,128)S(1)}, f32[9,1002]{1,0:T(8,128)S(1)}, u32[]{:S(2)}, u32[]{:S(2)}) collective-permute-start(f32[9,1002]{1,0:T(8,128)S(1)} %select_maximum_fusion.2), channel_id=1, source_target_pairs={{0,2},{1,3},{2,0},{3,1},{4,6},{5,7},{6,4},{7,5},{8,10},{9,11},{10,... | collective-permute-start | bytes 108224 | tf_op jit(solution)/shard_map/ppermute | solution.py:48
  175.4 4.3 %collective-permute-start.16 = (f32[9,1002]{1,0:T(8,128)S(1)}, f32[9,1002]{1,0:T(8,128)S(1)}, u32[]{:S(2)}, u32[]{:S(2)}) collective-permute-start(f32[9,1002]{1,0:T(8,128)S(1)} %select_maximum_fusion.1), channel_id=1, source_target_pairs={{0,4},{1,5},{2,6},{3,7},{4,0},{5,1},{6,2},{7,3},{8,12},{9,13},{10,... | collective-permute-start | bytes 108224 | tf_op jit(solution)/shard_map/ppermute | solution.py:48
  180.1 5.3 %collective-permute-start.17 = (f32[9,1002]{1,0:T(8,128)S(1)}, f32[9,1002]{1,0:T(8,128)S(1)}, u32[]{:S(2)}, u32[]{:S(2)}) collective-permute-start(f32[9,1002]{1,0:T(8,128)S(1)} %select_maximum_fusion.mine_ref), channel_id=1, source_target_pairs={{0,8},{1,9},{2,10},{3,11},{4,12},{5,13},{6,14},{7,15},{8,0},{9,1},... | collective-permute-start | bytes 108224 | tf_op jit(solution)/shard_map/ppermute | solution.py:48

commit v5 on v3

--- a/solution.py
+++ b/solution.py
@@ -579,7 +579,7 @@
     hidden = hidden + down_part(more_pooled, w_down, tiles)
     key_mean = lax.all_to_all(key_mean, "inp", split_axis=0, concat_axis=0, tiled=True)
     partial_feature = feature_part(
-        key_mean, value, w_proj.reshape(n_comps * n_heads, model_width), hidden, tokens, 4
+        key_mean, value, w_proj.reshape(n_comps * n_heads, model_width), hidden, tokens, 2
     )
     slice_width = model_width // n_parts
     feature = jnp.sum(

time: 184 us -> 183 us (level)
  no operation moved by 1% of the time
where the time goes in v5:
time: 183 us
  Pallas kernels  85.4 us (47%)
  waiting for transfers between devices  41.8 us (23%)
  starting transfers between devices  36.9 us (20%)
  local copies, waits for them, and re-layouts  11.6 us (6%)
  matrix products  4.14 us (2%)
    pallas_call x2, Pallas kernels, hidden_part(): pl.pallas_call(hidden_kernel, grid=(tiles, width // depth), out_shape=jax...  35.1 us
    ppermute x18, waiting for transfers between devices, permuted(): return lax.ppermute(array, 'inp', [(i, i ^ bits) for i in range(count)])  29.5 us
    pallas_call x2, Pallas kernels, query_key(): pl.pallas_call(query_key_kernel, grid=(width // depth,), out_shape=jax.Sh...  19.7 us
    ppermute x18, starting transfers between devices, permuted(): return lax.ppermute(array, 'inp', [(i, i ^ bits) for i in range(count)])  15.2 us
    all_to_all x2, starting transfers between devices, exchange(): return lax.all_to_all(array, 'inp', split_axis=0, concat_axis=0, tiled=True)  11.1 us
    pallas_call x2, Pallas kernels, down_part(): pl.pallas_call(down_kernel, grid=(units // UNITS,), out_shape=jax.ShapeDt...  10.4 us
    unnamed x29, local copies, waits for them, and re-layouts  10.4 us
    pallas_call x1, Pallas kernels, values_of(): pl.pallas_call(value_kernel, grid=(width // depth,), out_shape=jax.ShapeD...  7.74 us
  transfers between devices with their start and end apart: 22, of which 13 were waited for; matrix products, arithmetic and copies ran while one was open for 3% of the time, Pallas kernels for 36%

profile of v5, /device:TPU:0, one launch (start us, length us, event | category | flops | bytes accessed | tf_op | source)
XLA Modules:
  0.0 182.6 jit_solution(7714318782567268954)
XLA Ops:
  0.6 2.0 %own_norm.1 = (bf16[16,4096]{1,0:T(8,128)(2,1)}, bf16[16,2048]{1,0:T(8,128)(2,1)}) custom-call(bf16[16,6144]{1,0:T(8,128)(2,1)} %token_ref.1, f32[1,6144]{1,0:T(1,128)} %bitcast.51), custom_call_target="tpu_custom_call" | custom-call | tf_op jit(solution)/shard_map/own_norm/pallas_call | solution.py:61
  2.6 5.0 %collective-permute-start.2 = (bf16[16,4096]{1,0:T(8,128)(2,1)}, bf16[16,4096]{1,0:T(8,128)(2,1)S(1)}, u32[]{:S(2)}, u32[]{:S(2)}) collective-permute-start(bf16[16,4096]{1,0:T(8,128)(2,1)} %get-tuple-element.23), channel_id=1, source_target_pairs={{0,12},{1,13},{2,14},{3,15},{4,8},{5,9},{6,10},{7,11},{8,4},{9,5},... | collective-permute-start | bytes 393224 | tf_op jit(solution)/shard_map/ppermute | solution.py:48
  7.7 0.6 collective-permute-start
  8.3 1.7 collective-permute-start.3
  10.0 1.3 copy.25
  11.5 0.1 broadcast_compare_fusion
  11.6 2.6 %fusion.choose_ref = bf16[16,128,768]{2,1,0:T(8,128)(2,1)} fusion(pred[128,768]{1,0:T(8,128)(4,1)S(1)} %broadcast_compare_fusion, bf16[16,128,48]{2,1,0:T(8,128)(2,1)S(1)} %bitcast.41, s32[768]{0:T(1024)S(1)} %add_select_fusion), kind=kOutput, calls=%fused_computation.1 | convolution fusion | flops 155750400 | bytes 3443712 | tf_op jit(solution)/shard_map/trb,bc->trc/dot_general | solution.py:130
  14.3 4.7 %collective-permute-done.1 = bf16[16,4096]{1,0:T(8,128)(2,1)S(1)} collective-permute-done((bf16[16,4096]{1,0:T(8,128)(2,1)}, bf16[16,4096]{1,0:T(8,128)(2,1)S(1)}, u32[]{:S(2)}, u32[]{:S(2)}) %collective-permute-start.1) | collective-permute-done | bytes 131104 | tf_op jit(solution)/shard_map/ppermute | solution.py:48
  19.0 1.6 collective-permute-start.4
  20.6 3.0 %collective-permute-start.6 = (bf16[2,16,2048]{2,1,0:T(8,128)(2,1)S(1)}, bf16[2,16,2048]{2,1,0:T(8,128)(2,1)S(1)}, u32[]{:S(2)}, u32[]{:S(2)}) collective-permute-start(bf16[2,16,2048]{2,1,0:T(8,128)(2,1)S(1)} %pad_maximum_fusion.1.refs_2_), channel_id=1, source_target_pairs={{0,8},{1,9},{2,10},{3,11},{4,12},{5,13},{6,14},{7,15},{8,0},{9,1},... | collective-permute-start | bytes 393224 | tf_op jit(solution)/shard_map/ppermute | solution.py:48
  23.7 1.3 collective-permute-start.7
  25.0 1.6 collective-permute-done.5.refs_3_
  26.6 6.3 %collective-permute-done.6.refs_4_ = bf16[2,16,2048]{2,1,0:T(8,128)(2,1)S(1)} collective-permute-done((bf16[2,16,2048]{2,1,0:T(8,128)(2,1)S(1)}, bf16[2,16,2048]{2,1,0:T(8,128)(2,1)S(1)}, u32[]{:S(2)}, u32[]{:S(2)}) %collective-permute-start.6) | collective-permute-done | bytes 131104 | tf_op jit(solution)/shard_map/ppermute | solution.py:48
  32.8 0.5 collective-permute-start.10
  33.4 0.4 collective-permute-start.12
  33.9 1.3 collective-permute-done.10.refs_8_
  35.1 0.1 collective-permute-start.13
  35.3 0.2 collective-permute-done.12.refs_10_
  35.4 1.2 collective-permute-done.13.refs_11_
  36.6 2.9 %place_rows.1.norm_ref = bf16[256,6144]{1,0:T(8,128)(2,1)} custom-call(s32[1]{0:T(128)} %bitcast.me_ref, bf16[4,16,4096]{2,1,0:T(8,128)(2,1)S(1)} %pad_maximum_fusion.refs_0_, bf16[4,16,4096]{2,1,0:T(8,128)(2,1)S(1)} %collective-permute-done.4.refs_1_, bf16[2,16,2048]{2,1,0:T(8,128)(2,1)S(1)} %pad_maximum_fusion.1.refs_2_, ...), custom_call_target="tpu_custom_call" | custom-call | tf_op jit(solution)/shard_map/place_rows/pallas_call | solution.py:106
  39.5 8.1 %query_key.2 = bf16[16,8,16,256]{3,2,1,0:T(8,128)(2,1)} custom-call(bf16[256,6144]{1,0:T(8,128)(2,1)} %place_rows.1.norm_ref, bf16[16,128,768]{2,1,0:T(8,128)(2,1)} %fusion.choose_ref, bf16[8,3,48,6144]{3,2,1,0:T(8,128)(2,1)} %w_ref.5), custom_call_target="tpu_custom_call" | custom-call | flops 3221225472 | bytes 9437184 | tf_op jit(solution)/shard_map/query_key/pallas_call | solution.py:186
  47.6 4.2 %all-to-all-start = ((bf16[16,8,16,256]{3,2,1,0:T(8,128)(2,1)}), bf16[16,8,16,256]{3,2,1,0:T(8,128)(2,1)S(1)}, u32[]{:S(2)}, u32[]{:S(2)}) async-start(bf16[16,8,16,256]{3,2,1,0:T(8,128)(2,1)} %query_key.2), calls=%async_computation | async-start | bytes 2097152 | tf_op jit(solution)/shard_map/all_to_all | solution.py:560
  51.8 7.7 %value_rows.1.value_ref = bf16[8,256,384]{2,1,0:T(8,128)(2,1)S(1)} custom-call(bf16[256,6144]{1,0:T(8,128)(2,1)} %place_rows.1.norm_ref, bf16[16,128,768]{2,1,0:T(8,128)(2,1)} %fusion.choose_ref, bf16[8,3,48,6144]{3,2,1,0:T(8,128)(2,1)} %w_ref.5), custom_call_target="tpu_custom_call" | custom-call | flops 4831838208 | bytes 11010048 | tf_op jit(solution)/shard_map/value_rows/pallas_call | solution.py:236
  59.6 1.2 copy-done.3
  60.7 11.6 %query_key.3 = bf16[32,8,16,256]{3,2,1,0:T(8,128)(2,1)S(1)} custom-call(bf16[256,6144]{1,0:T(8,128)(2,1)} %place_rows.1.norm_ref, bf16[16,128,768]{2,1,0:T(8,128)(2,1)} %fusion.choose_ref, bf16[8,3,48,6144]{3,2,1,0:T(8,128)(2,1)} %w_ref.5), custom_call_target="tpu_custom_call" | custom-call | flops 6442450944 | bytes 12582912 | tf_op jit(solution)/shard_map/query_key/pallas_call | solution.py:186
  72.3 1.4 copy-done.8
  73.7 1.0 all-to-all-done.x_ref
  74.7 1.0 copy-done.6
  75.7 6.9 %all-to-all-start.1 = ((bf16[16,16,16,256]{3,2,1,0:T(8,128)(2,1)}), bf16[16,16,16,256]{3,2,1,0:T(8,128)(2,1)S(1)}, u32[]{:S(2)}, u32[]{:S(2)}) async-start(bf16[16,16,16,256]{3,2,1,0:T(8,128)(2,1)} %bitcast.39), calls=%async_computation.1 | async-start | bytes 4194304 | tf_op jit(solution)/shard_map/all_to_all | solution.py:560
  82.6 0.1 copy.29.query_gain_ref
  82.7 0.1 copy.30.key_gain_ref
  82.8 1.2 copy-done.7
  84.0 1.4 key_weights.2.refs_0_
  85.4 1.9 %copy-done.1 = bf16[256,6144]{1,0:T(8,128)(2,1)S(1)} copy-done((bf16[256,6144]{1,0:T(8,128)(2,1)S(1)}, bf16[256,6144]{1,0:T(8,128)(2,1)}, u32[]{:S(2)}) %copy-start.1) | copy-done | bytes 3145752
  87.3 17.6 %hidden_part.2.pooled_ref = f32[8,768]{1,0:T(8,128)S(1)} custom-call(bf16[256,6144]{1,0:T(8,128)(2,1)S(1)} %copy-done.1, bf16[16,128,768]{2,1,0:T(8,128)(2,1)} %fusion.choose_ref, bf16[1536,6144]{1,0:T(8,128)(2,1)} %up_ref.3), custom_call_target="tpu_custom_call" | custom-call | flops 9663676416 | bytes 15728640 | tf_op jit(solution)/shard_map/hidden_part/pallas_call | solution.py:295
  104.9 5.3 %down_part.2 = f32[8,6144]{1,0:T(8,128)S(1)} custom-call(f32[8,768]{1,0:T(8,128)S(1)} %hidden_part.2.pooled_ref, bf16[1536,6144]{1,0:T(8,128)(2,1)} %down_ref.3), custom_call_target="tpu_custom_call" | custom-call | flops 150994944 | bytes 9437184 | tf_op jit(solution)/shard_map/down_part/pallas_call | solution.py:334
  110.2 17.6 %hidden_part.3.pooled_ref = f32[8,768]{1,0:T(8,128)S(1)} custom-call(bf16[256,6144]{1,0:T(8,128)(2,1)S(1)} %copy-done.2, bf16[16,128,768]{2,1,0:T(8,128)(2,1)} %fusion.choose_ref, bf16[1536,6144]{1,0:T(8,128)(2,1)} %up_ref.3), custom_call_target="tpu_custom_call" | custom-call | flops 9663676416 | bytes 15728640 | tf_op jit(solution)/shard_map/hidden_part/pallas_call | solution.py:295
  127.8 3.1 %key_weights.3 = bf16[16,24,256]{2,1,0:T(8,128)(2,1)} custom-call(bf16[16,16,16,256]{3,2,1,0:T(8,128)(2,1)S(1)} %all-to-all-done.1.x_ref, f32[128,1]{1,0:T(8,128)S(1)} %copy.29.query_gain_ref, f32[128,1]{1,0:T(8,128)S(1)} %copy.30.key_gain_ref, f32[8,256]{1,0:T(8,128)S(1)} %key_weights.2.refs_0_), custom_call_target="tpu_custom_call" | custom-call | flops 268435456 | bytes 2097152 | tf_op jit(solution)/shard_map/key_weights/pallas_call | solution.py:393
  130.9 7.1 %all-to-all-start.2 = ((bf16[16,24,256]{2,1,0:T(8,128)(2,1)}), bf16[16,24,256]{2,1,0:T(8,128)(2,1)S(1)}, u32[]{:S(2)}, u32[]{:S(2)}) async-start(bf16[16,24,256]{2,1,0:T(8,128)(2,1)} %key_weights.3), calls=%async_computation.2 | async-start | bytes 393216 | tf_op jit(solution)/shard_map/all_to_all | solution.py:580
  138.0 5.1 %down_part.3 = f32[8,6144]{1,0:T(8,128)S(1)} custom-call(f32[8,768]{1,0:T(8,128)S(1)} %hidden_part.3.pooled_ref, bf16[1536,6144]{1,0:T(8,128)(2,1)} %down_ref.3), custom_call_target="tpu_custom_call" | custom-call | flops 150994944 | bytes 9437184 | tf_op jit(solution)/shard_map/down_part/pallas_call | solution.py:334
  143.2 3.8 %all-to-all-done.2.key_ref = bf16[16,24,256]{2,1,0:T(8,128)(2,1)S(1)} async-done(((bf16[16,24,256]{2,1,0:T(8,128)(2,1)}), bf16[16,24,256]{2,1,0:T(8,128)(2,1)S(1)}, u32[]{:S(2)}, u32[]{:S(2)}) %all-to-all-start.2) | async-done | bytes 196640 | tf_op jit(solution)/shard_map/all_to_all | solution.py:580
  147.0 2.3 %copy-done.5 = bf16[8,48,6144]{2,1,0:T(8,128)(2,1)S(1)} copy-done((bf16[8,48,6144]{2,1,0:T(8,128)(2,1)S(1)}, bf16[8,48,6144]{2,1,0:T(8,128)(2,1)}, u32[]{:S(2)}) %copy-start.5) | copy-done | bytes 4718616
  149.3 2.3 %feature_part.1 = f32[16,8,384]{2,1,0:T(8,128)} custom-call(bf16[16,24,256]{2,1,0:T(8,128)(2,1)S(1)} %all-to-all-done.2.key_ref, bf16[8,256,384]{2,1,0:T(8,128)(2,1)S(1)} %copy-done.4, bf16[384,6144]{1,0:T(8,128)(2,1)S(1)} %bitcast.38, f32[8,6144]{1,0:T(8,128)S(1)} %add.107.hidden_ref, bf16[16,6144]{1,0:T(8,128)(2,1)S(1)} %copy-done.9), custom_call_target="tpu_custom_call" | custom-call | flops 78643200 | bytes 6291456 | tf_op jit(solution)/shard_map/feature_part/pallas_call | solution.py:449
  151.7 3.5 %all-to-all-start.3 = ((f32[16,8,384]{2,1,0:T(8,128)}), f32[16,8,384]{2,1,0:T(8,128)S(1)}, u32[]{:S(2)}, u32[]{:S(2)}) async-start(f32[16,8,384]{2,1,0:T(8,128)} %feature_part.1), calls=%async_computation.3 | async-start | bytes 393216 | tf_op jit(solution)/shard_map/all_to_all | solution.py:586
  155.2 0.8 dynamic_slice.3
  156.0 0.7 fusion.28
  156.7 7.4 %all-to-all-done.3 = f32[16,8,384]{2,1,0:T(8,128)S(1)} async-done(((f32[16,8,384]{2,1,0:T(8,128)}), f32[16,8,384]{2,1,0:T(8,128)S(1)}, u32[]{:S(2)}, u32[]{:S(2)}) %all-to-all-start.3) | async-done | bytes 196640 | tf_op jit(solution)/shard_map/all_to_all | solution.py:586
  164.2 0.2 fusion.24
  164.3 0.2 multiply_reduce_fusion
  164.5 0.8 fusion.10
  165.3 0.1 copy.34
  165.4 0.1 copy.33
  165.5 0.1 select_maximum_fusion.3
  165.6 1.2 collective-permute-done.14
  166.8 0.2 subtract_reduce_fusion.5
  167.1 0.1 select_maximum_fusion.2
  167.2 4.3 %collective-permute-done.15 = f32[9,1002]{1,0:T(8,128)S(1)} collective-permute-done((f32[9,1002]{1,0:T(8,128)S(1)}, f32[9,1002]{1,0:T(8,128)S(1)}, u32[]{:S(2)}, u32[]{:S(2)}) %collective-permute-start.15) | collective-permute-done | bytes 36104 | tf_op jit(solution)/shard_map/ppermute | solution.py:48
  171.4 0.2 subtract_reduce_fusion.3
  171.7 0.1 select_maximum_fusion.1
  171.8 4.3 %collective-permute-done.16 = f32[9,1002]{1,0:T(8,128)S(1)} collective-permute-done((f32[9,1002]{1,0:T(8,128)S(1)}, f32[9,1002]{1,0:T(8,128)S(1)}, u32[]{:S(2)}, u32[]{:S(2)}) %collective-permute-start.16) | collective-permute-done | bytes 36104 | tf_op jit(solution)/shard_map/ppermute | solution.py:48
  176.1 0.2 subtract_reduce_fusion.1
  176.4 0.7 collective-permute-start.17
  177.1 4.7 %collective-permute-done.17.other_ref = f32[9,1002]{1,0:T(8,128)S(1)} collective-permute-done((f32[9,1002]{1,0:T(8,128)S(1)}, f32[9,1002]{1,0:T(8,128)S(1)}, u32[]{:S(2)}, u32[]{:S(2)}) %collective-permute-start.17) | collective-permute-done | bytes 36104 | tf_op jit(solution)/shard_map/ppermute | solution.py:48
  181.7 0.9 finish.1
  (57 shorter events, 0.8 us)
Async XLA Ops:
  0.6 155.4 %copy-start = (bf16[384,1000]{0,1:T(8,128)(2,1)S(1)}, bf16[384,1000]{0,1:T(8,128)(2,1)}, u32[]{:S(2)}) copy-start(bf16[384,1000]{0,1:T(8,128)(2,1)} %param.21) | copy-start | bytes 2304004
  2.6 11.6 %copy-start.11 = (bf16[16,2048]{1,0:T(8,128)(2,1)S(1)}, bf16[16,2048]{1,0:T(8,128)(2,1)}, u32[]{:S(2)}) copy-start(bf16[16,2048]{1,0:T(8,128)(2,1)} %get-tuple-element.24) | copy-start | bytes 196612
  2.6 16.3 %copy-start.10 = (bf16[16,4096]{1,0:T(8,128)(2,1)S(1)}, bf16[16,4096]{1,0:T(8,128)(2,1)}, u32[]{:S(2)}) copy-start(bf16[16,4096]{1,0:T(8,128)(2,1)} %get-tuple-element.23) | copy-start | bytes 393220
  2.6 11.6 %collective-permute-start.2 = (bf16[16,4096]{1,0:T(8,128)(2,1)}, bf16[16,4096]{1,0:T(8,128)(2,1)S(1)}, u32[]{:S(2)}, u32[]{:S(2)}) collective-permute-start(bf16[16,4096]{1,0:T(8,128)(2,1)} %get-tuple-element.23), channel_id=1, source_target_pairs={{0,12},{1,13},{2,14},{3,15},{4,8},{5,9},{6,10},{7,11},{8,4},{9,5},... | collective-permute-start | bytes 393224 | tf_op jit(solution)/shard_map/ppermute | solution.py:48
  7.7 11.3 %collective-permute-start.1 = (bf16[16,4096]{1,0:T(8,128)(2,1)}, bf16[16,4096]{1,0:T(8,128)(2,1)S(1)}, u32[]{:S(2)}, u32[]{:S(2)}) collective-permute-start(bf16[16,4096]{1,0:T(8,128)(2,1)} %get-tuple-element.23), channel_id=1, source_target_pairs={{0,8},{1,9},{2,10},{3,11},{4,12},{5,13},{6,14},{7,15},{8,0},{9,1},... | collective-permute-start | bytes 393224 | tf_op jit(solution)/shard_map/ppermute | solution.py:48
  7.7 11.3 %collective-permute-start = (bf16[16,4096]{1,0:T(8,128)(2,1)}, bf16[16,4096]{1,0:T(8,128)(2,1)S(1)}, u32[]{:S(2)}, u32[]{:S(2)}) collective-permute-start(bf16[16,4096]{1,0:T(8,128)(2,1)} %get-tuple-element.23), channel_id=1, source_target_pairs={{0,4},{1,5},{2,6},{3,7},{4,0},{5,1},{6,2},{7,3},{8,12},{9,13},{10,... | collective-permute-start | bytes 393224 | tf_op jit(solution)/shard_map/ppermute | solution.py:48
  8.3 5.9 %collective-permute-start.3 = (bf16[16,2048]{1,0:T(8,128)(2,1)}, bf16[16,2048]{1,0:T(8,128)(2,1)S(1)}, u32[]{:S(2)}, u32[]{:S(2)}) collective-permute-start(bf16[16,2048]{1,0:T(8,128)(2,1)} %get-tuple-element.24), channel_id=1, source_target_pairs={{0,2},{1,3},{2,0},{3,1},{4,6},{5,7},{6,4},{7,5},{8,10},{9,11},{10,... | collective-permute-start | bytes 196616 | tf_op jit(solution)/shard_map/ppermute | solution.py:48
  19.0 13.8 %collective-permute-start.4 = (bf16[4,16,4096]{2,1,0:T(8,128)(2,1)S(1)}, bf16[4,16,4096]{2,1,0:T(8,128)(2,1)S(1)}, u32[]{:S(2)}, u32[]{:S(2)}) collective-permute-start(bf16[4,16,4096]{2,1,0:T(8,128)(2,1)S(1)} %pad_maximum_fusion.refs_0_), channel_id=1, source_target_pairs={{0,2},{1,3},{2,0},{3,1},{4,6},{5,7},{6,4},{7,5},{8,10},{9,11},{10,... | collective-permute-start | bytes 1572872 | tf_op jit(solution)/shard_map/ppermute | solution.py:48
  20.6 6.0 %collective-permute-start.5 = (bf16[2,16,2048]{2,1,0:T(8,128)(2,1)S(1)}, bf16[2,16,2048]{2,1,0:T(8,128)(2,1)S(1)}, u32[]{:S(2)}, u32[]{:S(2)}) collective-permute-start(bf16[2,16,2048]{2,1,0:T(8,128)(2,1)S(1)} %pad_maximum_fusion.1.refs_2_), channel_id=1, source_target_pairs={{0,4},{1,5},{2,6},{3,7},{4,0},{5,1},{6,2},{7,3},{8,12},{9,13},{10,... | collective-permute-start | bytes 393224 | tf_op jit(solution)/shard_map/ppermute | solution.py:48
  20.6 12.2 %collective-permute-start.6 = (bf16[2,16,2048]{2,1,0:T(8,128)(2,1)S(1)}, bf16[2,16,2048]{2,1,0:T(8,128)(2,1)S(1)}, u32[]{:S(2)}, u32[]{:S(2)}) collective-permute-start(bf16[2,16,2048]{2,1,0:T(8,128)(2,1)S(1)} %pad_maximum_fusion.1.refs_2_), channel_id=1, source_target_pairs={{0,8},{1,9},{2,10},{3,11},{4,12},{5,13},{6,14},{7,15},{8,0},{9,1},... | collective-permute-start | bytes 393224 | tf_op jit(solution)/shard_map/ppermute | solution.py:48
  23.7 9.2 %collective-permute-start.7 = (bf16[2,16,2048]{2,1,0:T(8,128)(2,1)S(1)}, bf16[2,16,2048]{2,1,0:T(8,128)(2,1)S(1)}, u32[]{:S(2)}, u32[]{:S(2)}) collective-permute-start(bf16[2,16,2048]{2,1,0:T(8,128)(2,1)S(1)} %pad_maximum_fusion.1.refs_2_), channel_id=1, source_target_pairs={{0,12},{1,13},{2,14},{3,15},{4,8},{5,9},{6,10},{7,11},{8,4},{9,5},... | collective-permute-start | bytes 393224 | tf_op jit(solution)/shard_map/ppermute | solution.py:48
  25.0 10.3 %collective-permute-start.8 = (bf16[4,16,4096]{2,1,0:T(8,128)(2,1)S(1)}, bf16[4,16,4096]{2,1,0:T(8,128)(2,1)S(1)}, u32[]{:S(2)}, u32[]{:S(2)}) collective-permute-start(bf16[4,16,4096]{2,1,0:T(8,128)(2,1)S(1)} %pad_maximum_fusion.refs_0_), channel_id=1, source_target_pairs={{0,1},{1,0},{2,3},{3,2},{4,5},{5,4},{6,7},{7,6},{8,9},{9,8},{10,11... | collective-permute-start | bytes 1572872 | tf_op jit(solution)/shard_map/ppermute | solution.py:48
  32.8 3.8 %collective-permute-start.9 = (bf16[4,16,4096]{2,1,0:T(8,128)(2,1)S(1)}, bf16[4,16,4096]{2,1,0:T(8,128)(2,1)S(1)}, u32[]{:S(2)}, u32[]{:S(2)}) collective-permute-start(bf16[4,16,4096]{2,1,0:T(8,128)(2,1)S(1)} %collective-permute-done.4.refs_1_), channel_id=1, source_target_pairs={{0,1},{1,0},{2,3},{3,2},{4,5},{5,4},{6,7},{7,6},{8,9},{9,8},{10,11... | collective-permute-start | bytes 1572872 | tf_op jit(solution)/shard_map/ppermute | solution.py:48
  32.8 2.3 %collective-permute-start.10 = (bf16[2,16,2048]{2,1,0:T(8,128)(2,1)S(1)}, bf16[2,16,2048]{2,1,0:T(8,128)(2,1)S(1)}, u32[]{:S(2)}, u32[]{:S(2)}) collective-permute-start(bf16[2,16,2048]{2,1,0:T(8,128)(2,1)S(1)} %pad_maximum_fusion.1.refs_2_), channel_id=1, source_target_pairs={{0,1},{1,0},{2,3},{3,2},{4,5},{5,4},{6,7},{7,6},{8,9},{9,8},{10,11... | collective-permute-start | bytes 393224 | tf_op jit(solution)/shard_map/ppermute | solution.py:48
  33.4 1.9 %collective-permute-start.11 = (bf16[2,16,2048]{2,1,0:T(8,128)(2,1)S(1)}, bf16[2,16,2048]{2,1,0:T(8,128)(2,1)}, u32[]{:S(2)}, u32[]{:S(2)}) collective-permute-start(bf16[2,16,2048]{2,1,0:T(8,128)(2,1)S(1)} %collective-permute-done.5.refs_3_), channel_id=1, source_target_pairs={{0,1},{1,0},{2,3},{3,2},{4,5},{5,4},{6,7},{7,6},{8,9},{9,8},{10,11... | collective-permute-start | bytes 393224 | tf_op jit(solution)/shard_map/ppermute | solution.py:48
  33.4 2.0 %collective-permute-start.12 = (bf16[2,16,2048]{2,1,0:T(8,128)(2,1)S(1)}, bf16[2,16,2048]{2,1,0:T(8,128)(2,1)}, u32[]{:S(2)}, u32[]{:S(2)}) collective-permute-start(bf16[2,16,2048]{2,1,0:T(8,128)(2,1)S(1)} %collective-permute-done.6.refs_4_), channel_id=1, source_target_pairs={{0,1},{1,0},{2,3},{3,2},{4,5},{5,4},{6,7},{7,6},{8,9},{9,8},{10,11... | collective-permute-start | bytes 393224 | tf_op jit(solution)/shard_map/ppermute | solution.py:48
  35.1 1.5 collective-permute-start.13
  47.6 27.1 %all-to-all-start = ((bf16[16,8,16,256]{3,2,1,0:T(8,128)(2,1)}), bf16[16,8,16,256]{3,2,1,0:T(8,128)(2,1)S(1)}, u32[]{:S(2)}, u32[]{:S(2)}) async-start(bf16[16,8,16,256]{3,2,1,0:T(8,128)(2,1)} %query_key.2), calls=%async_computation | async-start | bytes 2097152 | tf_op jit(solution)/shard_map/all_to_all | solution.py:560
  59.5 1.2 copy-start.3
  60.7 21.8 %copy-start.12 = (f32[128]{0:T(128)S(1)}, f32[128]{0:T(128)}, u32[]{:S(2)}) copy-start(f32[128]{0:T(128)} %param.16) | copy-start | bytes 1540
  60.7 22.0 %copy-start.13 = (f32[128]{0:T(128)S(1)}, f32[128]{0:T(128)}, u32[]{:S(2)}) copy-start(f32[128]{0:T(128)} %param.17) | copy-start | bytes 1540
  72.3 1.4 copy-start.8
  74.7 1.0 copy-start.6
  75.7 52.1 %all-to-all-start.1 = ((bf16[16,16,16,256]{3,2,1,0:T(8,128)(2,1)}), bf16[16,16,16,256]{3,2,1,0:T(8,128)(2,1)S(1)}, u32[]{:S(2)}, u32[]{:S(2)}) async-start(bf16[16,16,16,256]{3,2,1,0:T(8,128)(2,1)} %bitcast.39), calls=%async_computation.1 | async-start | bytes 4194304 | tf_op jit(solution)/shard_map/all_to_all | solution.py:560
  82.8 1.2 copy-start.7
  85.4 1.9 %copy-start.1 = (bf16[256,6144]{1,0:T(8,128)(2,1)S(1)}, bf16[256,6144]{1,0:T(8,128)(2,1)}, u32[]{:S(2)}) copy-start(bf16[256,6144]{1,0:T(8,128)(2,1)} %place_rows.1.norm_ref) | copy-start | bytes 9437188
  104.9 5.3 %copy-start.2 = (bf16[256,6144]{1,0:T(8,128)(2,1)S(1)}, bf16[256,6144]{1,0:T(8,128)(2,1)}, u32[]{:S(2)}) copy-start(bf16[256,6144]{1,0:T(8,128)(2,1)} %place_rows.1.norm_ref) | copy-start | bytes 9437188
  130.9 16.1 %all-to-all-start.2 = ((bf16[16,24,256]{2,1,0:T(8,128)(2,1)}), bf16[16,24,256]{2,1,0:T(8,128)(2,1)S(1)}, u32[]{:S(2)}, u32[]{:S(2)}) async-start(bf16[16,24,256]{2,1,0:T(8,128)(2,1)} %key_weights.3), calls=%async_computation.2 | async-start | bytes 393216 | tf_op jit(solution)/shard_map/all_to_all | solution.py:580
  138.0 9.0 %copy-start.4 = (bf16[8,256,384]{2,1,0:T(8,128)(2,1)S(1)}, bf16[8,256,384]{2,1,0:T(8,128)(2,1)}, u32[]{:S(2)}) copy-start(bf16[8,256,384]{2,1,0:T(8,128)(2,1)} %copy-done.3) | copy-start | bytes 4718596
  138.0 9.0 %copy-start.9 = (bf16[16,6144]{1,0:T(8,128)(2,1)S(1)}, bf16[16,6144]{1,0:T(8,128)(2,1)}, u32[]{:S(2)}) copy-start(bf16[16,6144]{1,0:T(8,128)(2,1)} %token_ref.1) | copy-start | bytes 589828
  147.0 2.3 %copy-start.5 = (bf16[8,48,6144]{2,1,0:T(8,128)(2,1)S(1)}, bf16[8,48,6144]{2,1,0:T(8,128)(2,1)}, u32[]{:S(2)}) copy-start(bf16[8,48,6144]{2,1,0:T(8,128)(2,1)} %param.18) | copy-start | bytes 14155780
  151.7 12.5 %all-to-all-start.3 = ((f32[16,8,384]{2,1,0:T(8,128)}), f32[16,8,384]{2,1,0:T(8,128)S(1)}, u32[]{:S(2)}, u32[]{:S(2)}) async-start(f32[16,8,384]{2,1,0:T(8,128)} %feature_part.1), calls=%async_computation.3 | async-start | bytes 393216 | tf_op jit(solution)/shard_map/all_to_all | solution.py:586
  165.5 1.3 collective-permute-start.14
  167.2 4.3 %collective-permute-start.15 = (f32[9,1002]{1,0:T(8,128)S(1)}, f32[9,1002]{1,0:T(8,128)S(1)}, u32[]{:S(2)}, u32[]{:S(2)}) collective-permute-start(f32[9,1002]{1,0:T(8,128)S(1)} %select_maximum_fusion.2), channel_id=1, source_target_pairs={{0,2},{1,3},{2,0},{3,1},{4,6},{5,7},{6,4},{7,5},{8,10},{9,11},{10,... | collective-permute-start | bytes 108224 | tf_op jit(solution)/shard_map/ppermute | solution.py:48
  171.8 4.3 %collective-permute-start.16 = (f32[9,1002]{1,0:T(8,128)S(1)}, f32[9,1002]{1,0:T(8,128)S(1)}, u32[]{:S(2)}, u32[]{:S(2)}) collective-permute-start(f32[9,1002]{1,0:T(8,128)S(1)} %select_maximum_fusion.1), channel_id=1, source_target_pairs={{0,4},{1,5},{2,6},{3,7},{4,0},{5,1},{6,2},{7,3},{8,12},{9,13},{10,... | collective-permute-start | bytes 108224 | tf_op jit(solution)/shard_map/ppermute | solution.py:48
  176.4 5.3 %collective-permute-start.17 = (f32[9,1002]{1,0:T(8,128)S(1)}, f32[9,1002]{1,0:T(8,128)S(1)}, u32[]{:S(2)}, u32[]{:S(2)}) collective-permute-start(f32[9,1002]{1,0:T(8,128)S(1)} %select_maximum_fusion.mine_ref), channel_id=1, source_target_pairs={{0,8},{1,9},{2,10},{3,11},{4,12},{5,13},{6,14},{7,15},{8,0},{9,1},... | collective-permute-start | bytes 108224 | tf_op jit(solution)/shard_map/ppermute | solution.py:48
